TPU v7x, 128 devices: a whole 4x4x4 slice. The times are simulated.
128 devices in a mesh: gx: 16 (over z, y_lo, core), gy: 8 (over x, y_hi).
Axes of the slice: x: 4, y: 4 (y_hi: 2, y_lo: 2; y = y_hi * 2 + y_lo), z: 4, core: 2. Of those that a mesh axis runs over, the one named last changes fastest.
Arguments:
- raw_stack: float32 [2, 128, 256, 2048], P(None, ('gx', 'gy')), may hold values from 0 to 8
- psf_taps: float32 [3, 2, 31], replicated, may hold values from 0.05 to 1
Outputs:
- estimate: float32 [2, 128, 256, 2048], P(None, None, 'gy', 'gx')
All inputs are finite; a program needn't handle non-finite values.
Results may differ from a plain program's by a relative error of at most 0.0001.
Values sent between devices are 32-bit elements; how exact they have to be, the bound alone decides.
No kernel may reach another device: no remote copies, remote signals or barrier semaphores. Data moves between devices by JAX's collectives and lax.ppermute only.
A program may use at most 192 MiB of HBM per device.

v0:
```python
import jax
import jax.numpy as jnp
from jax import lax
from jax.sharding import PartitionSpec as P

ITERS = 2


BACKGROUND = 0.5
SIGMA_ACROSS = 48.0
SIGMA_ALONG = 96.0


def padded(block, sides, width):
    for axis, dim in sides:
        count = lax.axis_size(axis)
        forward = [(i, i + 1) for i in range(count - 1)]
        backward = [(target, source) for source, target in forward]
        low = lax.ppermute(
            lax.slice_in_dim(block, block.shape[dim] - width, None, axis=dim), axis, forward
        )
        high = lax.ppermute(lax.slice_in_dim(block, 0, width, axis=dim), axis, backward)
        block = jnp.concatenate([low, block, high], axis=dim)
    return block


def smoothing_table(length_cells, spread_cells, circular):
    places = lax.iota(jnp.int32, length_cells)
    offset = jnp.abs(places[:, None] - places[None, :])
    if circular:
        offset = jnp.minimum(offset, length_cells - offset)
    scaled = offset.astype(jnp.float32) / spread_cells
    kernel_table = jnp.exp(-0.5 * scaled * scaled)
    return kernel_table / jnp.sum(kernel_table, axis=1, keepdims=True)


def band_matrix(kernel_taps, size_in, size_out, start_lag):
    rows_in = lax.iota(jnp.int32, size_in)
    rows_out = lax.iota(jnp.int32, size_out)
    tap_index = lax.iota(jnp.int32, kernel_taps.shape[1])
    lag_grid = rows_in[:, None] - rows_out[None, :] - start_lag
    onehot = (lag_grid[:, :, None] == tap_index[None, None, :]).astype(jnp.float32)
    return jnp.einsum("jik,ck->cji", onehot, kernel_taps, precision=lax.Precision.HIGHEST)


def along_depth(volume, matrix):
    return jnp.einsum("cjxy,cji->cixy", volume, matrix, precision=lax.Precision.HIGHEST)


def along_rows(volume, matrix):
    return jnp.einsum("czjy,cji->cziy", volume, matrix, precision=lax.Precision.HIGHEST)


def along_lines(volume, matrix):
    return jnp.einsum("czxj,cji->czxi", volume, matrix, precision=lax.Precision.HIGHEST)


def blur_local(volume, kernel_set, half_taps):
    planes_count = volume.shape[1]
    filtered = along_depth(
        volume, band_matrix(kernel_set[0], planes_count, planes_count, -half_taps)
    )
    widened = padded(filtered, (("gy", 2),), half_taps)
    filtered = along_rows(
        widened, band_matrix(kernel_set[1], widened.shape[2], filtered.shape[2], 0)
    )
    widened = padded(filtered, (("gx", 3),), half_taps)
    return along_lines(widened, band_matrix(kernel_set[2], widened.shape[3], filtered.shape[3], 0))


def local(raw_stack, psf_taps):
    half_taps = psf_taps.shape[2] // 2
    channels = raw_stack.shape[0]
    lines_x = raw_stack.shape[2]
    lines_y = raw_stack.shape[3]
    count_gx = lax.axis_size("gx")
    count_gy = lax.axis_size("gy")
    width_x = lines_x // count_gy
    width_y = lines_y // count_gx
    across_table = smoothing_table(lines_x, SIGMA_ACROSS, False)
    along_table = smoothing_table(lines_y, SIGMA_ALONG, True)
    smoothed = jnp.einsum("ij,czjy->cziy", across_table, raw_stack, precision=lax.Precision.HIGHEST)
    stripes = smoothed - jnp.einsum(
        "czxj,jy->czxy", smoothed, along_table, precision=lax.Precision.HIGHEST
    )
    cleaned_plane = jnp.maximum(raw_stack - stripes, 0.0)
    blocks = cleaned_plane.reshape(channels, count_gy, width_x, count_gx, width_y)
    blocks = jnp.transpose(blocks, (3, 1, 0, 2, 4)).reshape(
        count_gx * count_gy, channels, 1, width_x, width_y
    )
    regrouped = lax.all_to_all(blocks, ("gx", "gy"), split_axis=0, concat_axis=2, tiled=True)
    cleaned = regrouped.reshape(channels, count_gx * count_gy, width_x, width_y)
    forward = psf_taps / jnp.sum(psf_taps, axis=2, keepdims=True)
    backward = forward[:, :, ::-1]
    estimate = cleaned
    for iteration in range(ITERS):
        blurred = blur_local(estimate, forward, half_taps)
        ratio_field = cleaned / (blurred + BACKGROUND)
        estimate = estimate * blur_local(ratio_field, backward, half_taps)
    return estimate


def solution(mesh):
    in_specs = (P(None, ("gx", "gy"), None, None), P())
    out_specs = P(None, None, "gy", "gx")
    return jax.shard_map(local, mesh=mesh, in_specs=in_specs, out_specs=out_specs, check_vma=False)
```

profile of v0, /device:TPU:15, one launch (start us, length us, event | category | flops | bytes accessed | tf_op | source)
XLA Modules:
  0.0 770.4 jit_solution(13306839842865993774)
XLA Ops:
  0.2 8.0 %fusion.4 = f32[2048]{0:T(1024)S(1)} fusion(), kind=kLoop, calls=%fused_computation.6 | loop fusion | flops 37746688 | bytes 8192 | tf_op jit(solution)/shard_map/reduce_sum | solution.py:34
  12.4 36.0 %fusion.31 = f32[2,1,256,2048]{3,2,0,1:T(8,128)S(1)} fusion(f32[256,2,2048]{2,0,1:T(8,128)S(1)} %fusion.32, f32[2,1,256,2048]{3,2,1,0:T(8,128)S(1)} %copy-done.7, f32[2048]{0:T(1024)S(1)} %fusion.4), kind=kOutput, calls=%fused_computation.45 | convolution fusion | flops 25810698240 | bytes 12591104 | tf_op jit(solution)/shard_map/czxj,jy->czxy/dot_general | solution.py:83
  52.6 11.7 %all-to-all-start = ((f32[128,2,1,32,128]{4,3,1,2,0:T(8,128)}), f32[128,2,1,32,128]{4,3,1,2,0:T(8,128)}, u32[]{:S(2)}, u32[]{:S(2)}) async-start(f32[128,2,1,32,128]{4,3,1,2,0:T(8,128)} %bitcast.106), calls=%async_computation | async-start | bytes 8388608 | tf_op jit(solution)/shard_map/all_to_all | solution.py:91
  65.4 48.7 %all-to-all-done = f32[128,2,1,32,128]{4,3,1,2,0:T(8,128)} async-done(((f32[128,2,1,32,128]{4,3,1,2,0:T(8,128)}), f32[128,2,1,32,128]{4,3,1,2,0:T(8,128)}, u32[]{:S(2)}, u32[]{:S(2)}) %all-to-all-start) | async-done | bytes 4194336 | tf_op jit(solution)/shard_map/all_to_all | solution.py:91
  114.1 8.4 %fusion.26 = f32[2,128,32,128]{3,1,2,0:T(8,128)S(1)} fusion(f32[2,128,128,1]{1,2,3,0:T(8,128)S(1)} %copy.58, f32[128,2,1,32,128]{4,3,1,2,0:T(8,128)} %all-to-all-done), kind=kOutput, calls=%fused_computation.39 | convolution fusion | flops 1610612736 | bytes 8519680 | tf_op jit(solution)/shard_map/cjxy,cji->cixy/dot_general | solution.py:47
  125.3 5.2 collective-permute-start.1
  130.8 40.0 %collective-permute-done = f32[2,128,15,128]{3,1,2,0:T(8,128)S(1)} collective-permute-done((f32[2,128,15,128]{3,1,2,0:T(8,128)S(1)}, f32[2,128,15,128]{3,1,2,0:T(8,128)S(1)}, u32[]{:S(2)}, u32[]{:S(2)}) %collective-permute-start) | collective-permute-done | bytes 1966112 | tf_op jit(solution)/shard_map/ppermute | solution.py:19
  170.8 43.2 %collective-permute-done.1 = f32[2,128,15,128]{3,1,2,0:T(8,128)S(1)} collective-permute-done((f32[2,128,15,128]{3,1,2,0:T(8,128)S(1)}, f32[2,128,15,128]{3,1,2,0:T(8,128)S(1)}, u32[]{:S(2)}, u32[]{:S(2)}) %collective-permute-start.1) | collective-permute-done | bytes 1966112 | tf_op jit(solution)/shard_map/ppermute | solution.py:22
  214.5 9.8 %fusion.45 = f32[2,128,32,128]{3,2,1,0:T(8,128)S(1)} fusion(f32[2,128,62,128]{3,1,2,0:T(8,128)S(1)} %pad_maximum_fusion.4, f32[2,62,32,1]{1,0,2,3:T(2,128)S(1)} %convolution_bitcast_fusion), kind=kOutput, calls=%fused_computation.56 | convolution fusion | flops 780140544 | bytes 12336640 | tf_op jit(solution)/shard_map/czjy,cji->cziy/dot_general | solution.py:51
  224.3 4.8 fusion.112
  245.3 5.3 collective-permute-done.2
  250.6 4.5 copy.30
  255.1 4.5 copy.31
  259.5 7.0 pad_maximum_fusion
  266.6 13.1 %fusion.7 = f32[2,128,32,128]{3,1,2,0:T(8,128)S(1)} fusion(f32[2,128,32,158]{3,2,1,0:T(8,128)S(1)} %pad_maximum_fusion, f32[2,158,128,1]{2,0,1,3:T(2,128)S(1)} %fusion.68), kind=kOutput, calls=%fused_computation.13 | convolution fusion | flops 1988100096 | bytes 9533440 | tf_op jit(solution)/shard_map/czxj,cji->czxi/dot_general | solution.py:55
  279.6 8.2 %fusion.28 = f32[2,128,32,128]{3,1,2,0:T(8,128)S(1)} fusion(f32[2,128,128,1]{1,2,3,0:T(8,128)S(1)} %copy.62, f32[2,128,32,128]{3,1,2,0:T(8,128)S(1)} %fusion.7, f32[128,2,1,32,128]{4,3,1,2,0:T(8,128)} %all-to-all-done), kind=kOutput, calls=%fused_computation.41 | convolution fusion | flops 1612709888 | bytes 12713984 | tf_op jit(solution)/shard_map/cjxy,cji->cixy/dot_general | solution.py:47
  293.5 5.8 collective-permute-start.5
  299.6 40.6 %collective-permute-done.4 = f32[2,128,15,128]{3,1,2,0:T(8,128)} collective-permute-done((f32[2,128,15,128]{3,1,2,0:T(8,128)}, f32[2,128,15,128]{3,1,2,0:T(8,128)}, u32[]{:S(2)}, u32[]{:S(2)}) %collective-permute-start.4) | collective-permute-done | bytes 1966112 | tf_op jit(solution)/shard_map/ppermute | solution.py:19
  340.2 42.3 %collective-permute-done.5 = f32[2,128,15,128]{3,1,2,0:T(8,128)} collective-permute-done((f32[2,128,15,128]{3,1,2,0:T(8,128)S(1)}, f32[2,128,15,128]{3,1,2,0:T(8,128)}, u32[]{:S(2)}, u32[]{:S(2)}) %collective-permute-start.5) | collective-permute-done | bytes 1966112 | tf_op jit(solution)/shard_map/ppermute | solution.py:22
  386.3 9.8 %fusion.48 = f32[2,128,32,128]{3,2,1,0:T(8,128)S(1)} fusion(f32[2,128,62,128]{3,1,2,0:T(8,128)S(1)} %pad_maximum_fusion.5, f32[2,62,32,1]{1,0,2,3:T(2,128)S(1)} %convolution_bitcast_fusion.1), kind=kOutput, calls=%fused_computation.57 | convolution fusion | flops 780140544 | bytes 12336640 | tf_op jit(solution)/shard_map/czjy,cji->cziy/dot_general | solution.py:51
  396.1 4.8 fusion.110
  405.1 5.1 collective-permute-start.6
  417.0 4.5 copy.37
  425.1 4.5 copy.38
  429.6 6.8 pad_maximum_fusion.1
  436.4 13.7 %bitcast_multiply_fusion = f32[2,128,32,128]{3,1,2,0:T(8,128)S(1)} fusion(f32[128,2,1,32,128]{4,3,1,2,0:T(8,128)} %all-to-all-done, f32[2,128,32,158]{3,2,1,0:T(8,128)S(1)} %pad_maximum_fusion.1, f32[2,158,128,1]{2,0,1,3:T(2,128)S(1)} %fusion.69), kind=kOutput, calls=%fused_computation.37 | convolution fusion | flops 1989148672 | bytes 13727744 | tf_op jit(solution)/shard_map/czxj,cji->czxi/dot_general | solution.py:55
  456.4 5.8 collective-permute-start.9
  462.1 38.2 %collective-permute-done.8 = f32[2,128,15,128]{3,1,2,0:T(8,128)S(1)} collective-permute-done((f32[2,128,15,128]{3,1,2,0:T(8,128)S(1)}, f32[2,128,15,128]{3,1,2,0:T(8,128)S(1)}, u32[]{:S(2)}, u32[]{:S(2)}) %collective-permute-start.8) | collective-permute-done | bytes 1966112 | tf_op jit(solution)/shard_map/ppermute | solution.py:19
  500.3 42.2 %collective-permute-done.9 = f32[2,128,15,128]{3,1,2,0:T(8,128)S(1)} collective-permute-done((f32[2,128,15,128]{3,1,2,0:T(8,128)S(1)}, f32[2,128,15,128]{3,1,2,0:T(8,128)S(1)}, u32[]{:S(2)}, u32[]{:S(2)}) %collective-permute-start.9) | collective-permute-done | bytes 1966112 | tf_op jit(solution)/shard_map/ppermute | solution.py:22
  543.1 9.8 %fusion.51 = f32[2,128,32,128]{3,2,1,0:T(8,128)S(1)} fusion(f32[2,128,62,128]{3,1,2,0:T(8,128)S(1)} %pad_maximum_fusion.6, f32[2,62,32,1]{1,0,2,3:T(2,128)S(1)} %convolution_bitcast_fusion), kind=kOutput, calls=%fused_computation.58 | convolution fusion | flops 780140544 | bytes 12336640 | tf_op jit(solution)/shard_map/czjy,cji->cziy/dot_general | solution.py:51
  552.9 4.7 fusion.108
  571.7 4.5 copy.46
  576.2 4.6 collective-permute-done.11
  580.8 4.5 copy.47
  585.3 7.2 pad_maximum_fusion.2
  592.5 12.2 %fusion.5 = f32[2,128,32,128]{3,1,2,0:T(8,128)S(1)} fusion(f32[2,128,32,158]{3,2,1,0:T(8,128)S(1)} %pad_maximum_fusion.2, f32[2,158,128,1]{2,0,1,3:T(2,128)S(1)} %fusion.68), kind=kOutput, calls=%fused_computation.11 | convolution fusion | flops 1988100096 | bytes 9533440 | tf_op jit(solution)/shard_map/czxj,cji->czxi/dot_general | solution.py:55
  604.7 8.3 %fusion.29 = f32[2,128,32,128]{3,1,2,0:T(8,128)S(1)} fusion(f32[2,128,128,1]{1,2,3,0:T(8,128)S(1)} %copy.62, f32[2,128,32,128]{3,1,2,0:T(8,128)S(1)} %fusion.5, f32[128,2,1,32,128]{4,3,1,2,0:T(8,128)} %all-to-all-done), kind=kOutput, calls=%fused_computation.42 | convolution fusion | flops 1612709888 | bytes 12713984 | tf_op jit(solution)/shard_map/cjxy,cji->cixy/dot_general | solution.py:47
  615.2 5.8 collective-permute-start.13
  621.0 38.7 %collective-permute-done.12 = f32[2,128,15,128]{3,1,2,0:T(8,128)S(1)} collective-permute-done((f32[2,128,15,128]{3,1,2,0:T(8,128)S(1)}, f32[2,128,15,128]{3,1,2,0:T(8,128)S(1)}, u32[]{:S(2)}, u32[]{:S(2)}) %collective-permute-start.12) | collective-permute-done | bytes 1966112 | tf_op jit(solution)/shard_map/ppermute | solution.py:19
  659.7 42.2 %collective-permute-done.13 = f32[2,128,15,128]{3,1,2,0:T(8,128)S(1)} collective-permute-done((f32[2,128,15,128]{3,1,2,0:T(8,128)S(1)}, f32[2,128,15,128]{3,1,2,0:T(8,128)S(1)}, u32[]{:S(2)}, u32[]{:S(2)}) %collective-permute-start.13) | collective-permute-done | bytes 1966112 | tf_op jit(solution)/shard_map/ppermute | solution.py:22
  703.1 9.8 %fusion.54 = f32[2,128,32,128]{3,2,1,0:T(8,128)S(1)} fusion(f32[2,128,62,128]{3,1,2,0:T(8,128)S(1)} %pad_maximum_fusion.7, f32[2,62,32,1]{1,0,2,3:T(2,128)S(1)} %convolution_bitcast_fusion.1), kind=kOutput, calls=%fused_computation.59 | convolution fusion | flops 780140544 | bytes 12336640 | tf_op jit(solution)/shard_map/czjy,cji->cziy/dot_general | solution.py:51
  712.9 4.7 fusion.106
  731.9 4.5 copy.53
  736.4 4.6 collective-permute-done.15
  741.0 4.5 copy.54
  745.6 7.1 pad_maximum_fusion.3
  752.7 13.0 %fusion.59 = f32[2,128,32,128]{3,1,2,0:T(8,128)S(1)} fusion(f32[2,128,32,128]{3,1,2,0:T(8,128)S(1)} %copy-done.5, f32[2,128,32,158]{3,2,1,0:T(8,128)S(1)} %pad_maximum_fusion.3, f32[2,158,128,1]{2,0,1,3:T(2,128)S(1)} %fusion.69), kind=kOutput, calls=%fused_computation.60 | convolution fusion | flops 1989148672 | bytes 13727744 | tf_op jit(solution)/shard_map/czxj,cji->czxi/dot_general | solution.py:55
  765.7 4.4 copy.57
  (72 shorter events, 92.2 us)
Async XLA Ops:
  0.0 8.2 %copy-start.7 = (f32[2,1,256,2048]{3,2,1,0:T(8,128)S(1)}, f32[2,1,256,2048]{3,2,1,0:T(8,128)}, u32[]{:S(2)}) copy-start(f32[2,1,256,2048]{3,2,1,0:T(8,128)} %param.2) | copy-start | bytes 12582916
  52.6 11.7 %copy-start.8 = (f32[3,2,31]{2,1,0:T(2,128)S(1)}, f32[3,2,31]{2,1,0:T(2,128)}, u32[]{:S(2)}) copy-start(f32[3,2,31]{2,1,0:T(2,128)} %param.3) | copy-start | bytes 2236
  52.6 61.5 %all-to-all-start = ((f32[128,2,1,32,128]{4,3,1,2,0:T(8,128)}), f32[128,2,1,32,128]{4,3,1,2,0:T(8,128)}, u32[]{:S(2)}, u32[]{:S(2)}) async-start(f32[128,2,1,32,128]{4,3,1,2,0:T(8,128)} %bitcast.106), calls=%async_computation | async-start | bytes 8388608 | tf_op jit(solution)/shard_map/all_to_all | solution.py:91
  122.8 48.0 %collective-permute-start = (f32[2,128,15,128]{3,1,2,0:T(8,128)S(1)}, f32[2,128,15,128]{3,1,2,0:T(8,128)S(1)}, u32[]{:S(2)}, u32[]{:S(2)}) collective-permute-start(f32[2,128,15,128]{3,1,2,0:T(8,128)S(1)} %get-tuple-element.19), channel_id=1, source_target_pairs={{0,1},{1,2},{2,3},{3,4},{4,5},{5,6},{6,7},{8,9},{9,10},{10,11},{11... | collective-permute-start | bytes 5898248 | tf_op jit(solution)/shard_map/ppermute | solution.py:19
  125.3 88.6 %collective-permute-start.1 = (f32[2,128,15,128]{3,1,2,0:T(8,128)S(1)}, f32[2,128,15,128]{3,1,2,0:T(8,128)S(1)}, u32[]{:S(2)}, u32[]{:S(2)}) collective-permute-start(f32[2,128,15,128]{3,1,2,0:T(8,128)S(1)} %get-tuple-element.20), channel_id=1, source_target_pairs={{1,0},{2,1},{3,2},{4,3},{5,4},{6,5},{7,6},{9,8},{10,9},{11,10},{12... | collective-permute-start | bytes 5898248 | tf_op jit(solution)/shard_map/ppermute | solution.py:22
  224.3 4.8 copy-start
  237.0 18.1 %collective-permute-start.3 = (f32[2,128,32,15]{1,2,3,0:T(8,128)S(1)}, f32[2,128,32,15]{1,2,3,0:T(8,128)S(1)}, u32[]{:S(2)}, u32[]{:S(2)}) collective-permute-start(f32[2,128,32,15]{1,2,3,0:T(8,128)S(1)} %copy.29), channel_id=1, source_target_pairs={{8,0},{16,8},{24,16},{32,24},{40,32},{48,40},{56,48},{64,56},{72,6... | collective-permute-start | bytes 1474568 | tf_op jit(solution)/shard_map/ppermute | solution.py:22
  239.4 11.2 %collective-permute-start.2 = (f32[2,128,32,15]{1,2,3,0:T(8,128)S(1)}, f32[2,128,32,15]{1,2,3,0:T(8,128)S(1)}, u32[]{:S(2)}, u32[]{:S(2)}) collective-permute-start(f32[2,128,32,15]{1,2,3,0:T(8,128)S(1)} %copy.28), channel_id=1, source_target_pairs={{0,8},{8,16},{16,24},{24,32},{32,40},{40,48},{48,56},{56,64},{64,7... | collective-permute-start | bytes 1474568 | tf_op jit(solution)/shard_map/ppermute | solution.py:19
  287.8 2.0 copy-start.6
  291.5 48.7 %collective-permute-start.4 = (f32[2,128,15,128]{3,1,2,0:T(8,128)}, f32[2,128,15,128]{3,1,2,0:T(8,128)}, u32[]{:S(2)}, u32[]{:S(2)}) collective-permute-start(f32[2,128,15,128]{3,1,2,0:T(8,128)} %get-tuple-element.15), channel_id=1, source_target_pairs={{0,1},{1,2},{2,3},{3,4},{4,5},{5,6},{6,7},{8,9},{9,10},{10,11},{11... | collective-permute-start | bytes 5898248 | tf_op jit(solution)/shard_map/ppermute | solution.py:19
  293.5 89.0 %collective-permute-start.5 = (f32[2,128,15,128]{3,1,2,0:T(8,128)S(1)}, f32[2,128,15,128]{3,1,2,0:T(8,128)}, u32[]{:S(2)}, u32[]{:S(2)}) collective-permute-start(f32[2,128,15,128]{3,1,2,0:T(8,128)S(1)} %get-tuple-element.16), channel_id=1, source_target_pairs={{1,0},{2,1},{3,2},{4,3},{5,4},{6,5},{7,6},{9,8},{10,9},{11,10},{12... | collective-permute-start | bytes 5898248 | tf_op jit(solution)/shard_map/ppermute | solution.py:22
  396.1 4.8 copy-start.1
  405.1 11.9 %collective-permute-start.6 = (f32[2,128,32,15]{1,2,3,0:T(8,128)S(1)}, f32[2,128,32,15]{1,2,3,0:T(8,128)S(1)}, u32[]{:S(2)}, u32[]{:S(2)}) collective-permute-start(f32[2,128,32,15]{1,2,3,0:T(8,128)S(1)} %copy.35), channel_id=1, source_target_pairs={{0,8},{8,16},{16,24},{24,32},{32,40},{40,48},{48,56},{56,64},{64,7... | collective-permute-start | bytes 1474568 | tf_op jit(solution)/shard_map/ppermute | solution.py:19
  414.0 11.0 %collective-permute-start.7 = (f32[2,128,32,15]{1,2,3,0:T(8,128)S(1)}, f32[2,128,32,15]{1,2,3,0:T(8,128)S(1)}, u32[]{:S(2)}, u32[]{:S(2)}) collective-permute-start(f32[2,128,32,15]{1,2,3,0:T(8,128)S(1)} %copy.36), channel_id=1, source_target_pairs={{8,0},{16,8},{24,16},{32,24},{40,32},{48,40},{56,48},{64,56},{72,6... | collective-permute-start | bytes 1474568 | tf_op jit(solution)/shard_map/ppermute | solution.py:22
  450.0 4.1 copy-start.4
  454.4 45.9 %collective-permute-start.8 = (f32[2,128,15,128]{3,1,2,0:T(8,128)S(1)}, f32[2,128,15,128]{3,1,2,0:T(8,128)S(1)}, u32[]{:S(2)}, u32[]{:S(2)}) collective-permute-start(f32[2,128,15,128]{3,1,2,0:T(8,128)S(1)} %get-tuple-element.11), channel_id=1, source_target_pairs={{0,1},{1,2},{2,3},{3,4},{4,5},{5,6},{6,7},{8,9},{9,10},{10,11},{11... | collective-permute-start | bytes 5898248 | tf_op jit(solution)/shard_map/ppermute | solution.py:19
  456.4 86.2 %collective-permute-start.9 = (f32[2,128,15,128]{3,1,2,0:T(8,128)S(1)}, f32[2,128,15,128]{3,1,2,0:T(8,128)S(1)}, u32[]{:S(2)}, u32[]{:S(2)}) collective-permute-start(f32[2,128,15,128]{3,1,2,0:T(8,128)S(1)} %get-tuple-element.12), channel_id=1, source_target_pairs={{1,0},{2,1},{3,2},{4,3},{5,4},{6,5},{7,6},{9,8},{10,9},{11,10},{12... | collective-permute-start | bytes 5898248 | tf_op jit(solution)/shard_map/ppermute | solution.py:22
  552.9 4.7 copy-start.2
  561.7 10.0 %collective-permute-start.10 = (f32[2,128,32,15]{1,2,3,0:T(8,128)S(1)}, f32[2,128,32,15]{1,2,3,0:T(8,128)S(1)}, u32[]{:S(2)}, u32[]{:S(2)}) collective-permute-start(f32[2,128,32,15]{1,2,3,0:T(8,128)S(1)} %copy.44), channel_id=1, source_target_pairs={{0,8},{8,16},{16,24},{24,32},{32,40},{40,48},{48,56},{56,64},{64,7... | collective-permute-start | bytes 1474568 | tf_op jit(solution)/shard_map/ppermute | solution.py:19
  569.8 11.0 %collective-permute-start.11 = (f32[2,128,32,15]{1,2,3,0:T(8,128)S(1)}, f32[2,128,32,15]{1,2,3,0:T(8,128)S(1)}, u32[]{:S(2)}, u32[]{:S(2)}) collective-permute-start(f32[2,128,32,15]{1,2,3,0:T(8,128)S(1)} %copy.45), channel_id=1, source_target_pairs={{8,0},{16,8},{24,16},{32,24},{40,32},{48,40},{56,48},{64,56},{72,6... | collective-permute-start | bytes 1474568 | tf_op jit(solution)/shard_map/ppermute | solution.py:22
  613.3 46.4 %collective-permute-start.12 = (f32[2,128,15,128]{3,1,2,0:T(8,128)S(1)}, f32[2,128,15,128]{3,1,2,0:T(8,128)S(1)}, u32[]{:S(2)}, u32[]{:S(2)}) collective-permute-start(f32[2,128,15,128]{3,1,2,0:T(8,128)S(1)} %get-tuple-element.7), channel_id=1, source_target_pairs={{0,1},{1,2},{2,3},{3,4},{4,5},{5,6},{6,7},{8,9},{9,10},{10,11},{11... | collective-permute-start | bytes 5898248 | tf_op jit(solution)/shard_map/ppermute | solution.py:19
  615.2 86.7 %collective-permute-start.13 = (f32[2,128,15,128]{3,1,2,0:T(8,128)S(1)}, f32[2,128,15,128]{3,1,2,0:T(8,128)S(1)}, u32[]{:S(2)}, u32[]{:S(2)}) collective-permute-start(f32[2,128,15,128]{3,1,2,0:T(8,128)S(1)} %get-tuple-element.8), channel_id=1, source_target_pairs={{1,0},{2,1},{3,2},{4,3},{5,4},{6,5},{7,6},{9,8},{10,9},{11,10},{12... | collective-permute-start | bytes 5898248 | tf_op jit(solution)/shard_map/ppermute | solution.py:22
  712.9 4.8 copy-start.3
  721.9 10.0 %collective-permute-start.14 = (f32[2,128,32,15]{1,2,3,0:T(8,128)S(1)}, f32[2,128,32,15]{1,2,3,0:T(8,128)S(1)}, u32[]{:S(2)}, u32[]{:S(2)}) collective-permute-start(f32[2,128,32,15]{1,2,3,0:T(8,128)S(1)} %copy.51), channel_id=1, source_target_pairs={{0,8},{8,16},{16,24},{24,32},{32,40},{40,48},{48,56},{56,64},{64,7... | collective-permute-start | bytes 1474568 | tf_op jit(solution)/shard_map/ppermute | solution.py:19
  730.0 11.0 %collective-permute-start.15 = (f32[2,128,32,15]{1,2,3,0:T(8,128)S(1)}, f32[2,128,32,15]{1,2,3,0:T(8,128)S(1)}, u32[]{:S(2)}, u32[]{:S(2)}) collective-permute-start(f32[2,128,32,15]{1,2,3,0:T(8,128)S(1)} %copy.52), channel_id=1, source_target_pairs={{8,0},{16,8},{24,16},{32,24},{40,32},{48,40},{56,48},{64,56},{72,6... | collective-permute-start | bytes 1474568 | tf_op jit(solution)/shard_map/ppermute | solution.py:22
  745.6 7.1 copy-start.5
where the time goes:
time: 776 us; the launch traced here: 770 us
  waiting for transfers between devices  394 us (51%)
  matrix products  164 us (21%)
  local copies, waits for them, and re-layouts  100 us (13%)
  starting transfers between devices  68.2 us (9%)
  other arithmetic  42.6 us (5%)
    ppermute x8, waiting for transfers between devices, padded(): lax.ppermute(lax.slice_in_dim(block, 0, width, axis=dim), axis, backward)  183 us
    ppermute x8, waiting for transfers between devices, padded(): lax.ppermute(lax.slice_in_dim(block, block.shape[dim] - width, None, axis...  163 us
    dot_general x4, matrix products, along_lines(): jnp.einsum('czxj,cji->czxi', volume, matrix, precision=lax.Precision.HIGH...  51.9 us
    all_to_all x1, waiting for transfers between devices, local(): lax.all_to_all(blocks, ('gx', 'gy'), split_axis=0, concat_axis=2, tiled=T...  48.7 us
    dot_general x4, matrix products, along_rows(): jnp.einsum('czjy,cji->cziy', volume, matrix, precision=lax.Precision.HIGH...  39.2 us
    slice x12, local copies, waits for them, and re-layouts, padded(): lax.slice_in_dim(block, block.shape[dim] - width, None, axis=dim)  37.9 us
    dot_general x1, matrix products, local(): jnp.einsum('czxj,jy->czxy', smoothed, along_table, precision=lax.Precisio...  36 us
    concatenate x8, other arithmetic, padded(): block = jnp.concatenate([low, block, high], axis=dim)  34.2 us
  transfers between devices with their start and end apart: 17, of which 13 were waited for; matrix products, arithmetic and copies ran while one was open for 4% of the time, Pallas kernels for 0%

commit v1 on v0

v1 whole, which is shorter than its diff:
```python
import functools

import jax
import jax.numpy as jnp
import numpy as np
from jax import lax
from jax.experimental import pallas as pl
from jax.experimental.pallas import tpu as pltpu
from jax.sharding import PartitionSpec as P

CH, NZ, NX, NY = 2, 128, 256, 2048
TAPS, HALF = 31, 15
ITERS = 2
BACKGROUND = 0.5
SIGMA_ACROSS = 48.0
SIGMA_ALONG = 96.0

LINES = 32
BLOCKS = NY // LINES
AXES = ("gx", "gy")
F32, BF16 = jnp.float32, jnp.bfloat16
VMEM_LIMIT = 60 * 1024 * 1024


def rank(x, yh, yl, z, core):
    return ((z * 2 + yl) * 2 + core) * 8 + x * 2 + yh


def place(block):
    core, row, step = block & 1, block >> 3, (block >> 1) & 3
    z, k = row >> 1, row & 1
    return (step if k == 0 else 3 - step), k ^ (z & 1), z, core


def device_of(channel, block):
    x, yl, z, core = place(block)
    return rank(x, channel, yl, z, core)


UP = [(device_of(c, b), device_of(c, (b + 1) % BLOCKS)) for c in range(CH) for b in range(BLOCKS)]
DOWN = [(target, source) for source, target in UP]

ROUNDS = 8


def final_target(channel, block, j):
    x, _, _, core = place(block)
    xd = (x + 2 * core + (j >> 1)) % 4
    x8 = 2 * xd + (channel ^ (j & 1) ^ core)
    return x8, (block >> 2) * 8 + x8


FINAL = [
    [(device_of(c, b), final_target(c, b, j)[1]) for c in range(CH) for b in range(BLOCKS)]
    for j in range(ROUNDS)
]


def meta_table():
    meta = np.zeros((128, 2 + 2 * ROUNDS), np.int32)
    for c in range(CH):
        for b in range(BLOCKS):
            me = device_of(c, b)
            meta[me, 0] = b > 0
            meta[me, 1] = b < BLOCKS - 1
            for j in range(ROUNDS):
                x8, target = final_target(c, b, j)
                meta[me, 2 + j] = x8
                meta[target, 2 + ROUNDS + j] = c * 4 + (b & 3)
    return meta


def np_split(table):
    high = table.astype(np.float32).astype(jnp.bfloat16)
    low = (table - high.astype(np.float64)).astype(np.float32).astype(jnp.bfloat16)
    return high, low


def destripe_tables():
    i = np.arange(NX, dtype=np.float64)
    across = np.exp(-0.5 * ((i[:, None] - i[None, :]) / SIGMA_ACROSS) ** 2)
    across = across / across.sum(axis=1, keepdims=True)
    n = np.arange(NY, dtype=np.float64)
    c = np.minimum(n, NY - n)
    ring = np.exp(-0.5 * (c / SIGMA_ALONG) ** 2)
    ring = ring / ring.sum()
    along = ring[(np.arange(NY)[:, None] - np.arange(NY)[None, :]) % NY]
    h, q = NY // 2, NY // 4
    even = along[:h, :h] + along[:h, h:]
    odd = along[:h, :h] - along[:h, h:]
    even_even = even[:q, :q] + even[:q, q:]
    even_odd = even[:q, :q] - even[:q, q:]
    out = []
    for table in (across.T, odd, even_even, even_odd):
        out.extend(np_split(table))
    return out


def split(v):
    high = v.astype(BF16)
    return high, (v - high.astype(F32)).astype(BF16)


def dot(a, b):
    return jnp.dot(a, b, preferred_element_type=F32)


def dot3(a_high, a_low, b_high, b_low):
    return dot(a_high, b_high) + (dot(a_high, b_low) + dot(a_low, b_high))


def destripe_kernel(raw, ah, al, oh, ol, eeh, eel, eoh, eol, out, rt, sm, dh, dl, s1h, s1l, d1h, d1l):
    h, q = NY // 2, NY // 4

    @pl.loop(0, NY // 256)
    def _(i):
        r = pl.multiple_of(i * 256, 256)
        tile = raw[0, 0, :, pl.ds(r, 256)].T
        rt[pl.ds(r, 256), :] = tile
        th, tl = split(tile)
        sm[pl.ds(r, 256), :] = dot3(th, tl, ah[...], al[...])

    @pl.loop(0, q // 128)
    def _(i):
        r = pl.multiple_of(i * 128, 128)
        parts = [sm[pl.ds(r + m * q, 128), :] for m in range(4)]
        for m in range(2):
            hi, lo = split(0.5 * (parts[m] - parts[m + 2]))
            dh[pl.ds(r + m * q, 128), :] = hi
            dl[pl.ds(r + m * q, 128), :] = lo
        top = 0.5 * (parts[0] + parts[2])
        bottom = 0.5 * (parts[1] + parts[3])
        hi, lo = split(0.5 * (top + bottom))
        s1h[pl.ds(r, 128), :] = hi
        s1l[pl.ds(r, 128), :] = lo
        hi, lo = split(0.5 * (top - bottom))
        d1h[pl.ds(r, 128), :] = hi
        d1l[pl.ds(r, 128), :] = lo

    def emit(row, smooth):
        for m in range(8):
            x, yl, z, core = place(row // LINES + m)
            at = pl.ds(row + m * LINES, LINES)
            part = smooth[m * LINES : (m + 1) * LINES, :]
            clean = jnp.maximum(rt[at, :] - (sm[at, :] - part), 0.0)
            gx = (z * 2 + yl) * 2 + core
            out[gx, x, 0, 0:LINES, :] = clean[:, :128]
            out[gx, x, 0, LINES : 2 * LINES, :] = clean[:, 128:]

    for i in range(2):
        at = slice(i * 256, (i + 1) * 256)
        ee = dot3(eeh[at, :], eel[at, :], s1h[...], s1l[...])
        eo = dot3(eoh[at, :], eol[at, :], d1h[...], d1l[...])
        for m in range(2):
            row = m * q + i * 256
            even = ee + eo if m == 0 else ee - eo
            rows = slice(row, row + 256)
            odd = dot3(oh[rows, :], ol[rows, :], dh[...], dl[...])
            emit(row, even + odd)
            emit(h + row, even - odd)


def destripe(raw_stack):
    tables = [jnp.asarray(t) for t in destripe_tables()]
    whole = pl.BlockSpec(memory_space=pltpu.VMEM)
    return pl.pallas_call(
        destripe_kernel,
        grid=(CH,),
        in_specs=[pl.BlockSpec((1, 1, NX, NY), lambda c: (c, 0, 0, 0))] + [whole] * 8,
        out_specs=pl.BlockSpec((16, 4, 1, 64, 128), lambda c: (0, 0, c, 0, 0)),
        out_shape=jax.ShapeDtypeStruct((16, 4, CH, 64, 128), F32),
        scratch_shapes=[
            pltpu.VMEM((NY, NX), F32),
            pltpu.VMEM((NY, NX), F32),
            pltpu.VMEM((NY // 2, NX), BF16),
            pltpu.VMEM((NY // 2, NX), BF16),
        ]
        + [pltpu.VMEM((NY // 4, NX), BF16)] * 4,
        compiler_params=pltpu.CompilerParams(vmem_limit_bytes=VMEM_LIMIT),
        name="destripe",
    )(raw_stack, *tables)


def band(weights, size):
    shape = (size, size)
    lag = lax.broadcasted_iota(jnp.int32, shape, 1) - lax.broadcasted_iota(jnp.int32, shape, 0)
    out = jnp.zeros(shape, F32)
    for k in range(TAPS):
        out = jnp.where(lag == k - HALF, weights[k], out)
    return out


def tables_kernel(taps, *outs):
    for way in range(2):
        z_table, xh, xl = outs[3 * way : 3 * way + 3]
        hi, lo = split(band(tap_list(taps, 0, 1 - way), NZ))
        for half in range(2):
            rows = slice(half * NZ, (half + 1) * NZ)
            z_table[rows, :NZ] = hi
            z_table[rows, NZ:] = lo
        hi, lo = split(band(tap_list(taps, 1, way), NX))
        xh[...] = hi
        xl[...] = lo


def filter_tables(taps):
    square = jax.ShapeDtypeStruct((256, 256), BF16)
    outs = pl.pallas_call(
        tables_kernel,
        in_specs=[pl.BlockSpec(memory_space=pltpu.SMEM)],
        out_shape=[square] * 6,
        compiler_params=pltpu.CompilerParams(vmem_limit_bytes=VMEM_LIMIT),
        cost_estimate=pl.CostEstimate(flops=10**10, bytes_accessed=10**6, transcendentals=0),
        name="tables",
    )(taps)
    return outs[:3], outs[3:]


def tap_list(taps, axis, way):
    return [taps[axis, k if way == 0 else TAPS - 1 - k] for k in range(TAPS)]


def filter_z(v, z_table):
    hi, lo = split(v)
    both = dot(jnp.concatenate([hi, lo], axis=1), z_table)
    return both[:, :NZ] + both[:, NZ:]


def filter_x_pair(hi, lo, xh, xl):
    return dot(xh, hi) + (dot(xh, lo) + dot(xl, hi))


EDGE_SHAPES = ((HALF, NX, NZ), (LINES - 2 * HALF, NX, NZ), (HALF, NX, NZ))


def for_pairs(pair, low, mid, high):
    @pl.loop(0, HALF // 2)
    def _(i):
        a, b = pair(2 * i)
        low[2 * i] = a
        low[2 * i + 1] = b

    a, b = pair(HALF - 1)
    low[HALF - 1] = a
    mid[0] = b
    a, b = pair(HALF + 1)
    mid[1] = a
    high[0] = b

    @pl.loop(0, HALF // 2)
    def _(i):
        a, b = pair(HALF + 3 + 2 * i)
        high[1 + 2 * i] = a
        high[2 + 2 * i] = b


def arrive_kernel(got, z_table, xh, xl, cleaned, low, mid, high):
    def pair(y):
        his, los = [], []
        for m in range(2):
            for half in range(2):
                tile = got[pl.ds(half * LINES + y + m, NZ, stride=2 * LINES), :].T
                cleaned[y + m, half * 128 : (half + 1) * 128, :] = tile
            hi, lo = split(filter_z(cleaned[y + m], z_table[...]))
            his.append(hi)
            los.append(lo)
        both = filter_x_pair(
            jnp.concatenate(his, axis=1), jnp.concatenate(los, axis=1), xh[...], xl[...]
        )
        return both[:, :NZ], both[:, NZ:]

    for_pairs(pair, low, mid, high)


def arrive(got, tables):
    whole = pl.BlockSpec(memory_space=pltpu.VMEM)
    return pl.pallas_call(
        arrive_kernel,
        in_specs=[whole] * 4,
        out_specs=[whole] * 4,
        out_shape=[jax.ShapeDtypeStruct((LINES, NX, NZ), F32)]
        + [jax.ShapeDtypeStruct(s, F32) for s in EDGE_SHAPES],
        compiler_params=pltpu.CompilerParams(vmem_limit_bytes=VMEM_LIMIT),
        name="arrive",
    )(got, *tables)


XB = 64


def own_kernel(way, taps, low, mid, high, out):
    weights = [jnp.full((8, NZ), tap, F32) for tap in tap_list(taps, 2, way)]

    def line(j, at):
        if j < HALF:
            return low[j, at, :]
        if j < LINES - HALF:
            return mid[j - HALF, at, :]
        return high[j - (LINES - HALF), at, :]

    @pl.loop(0, XB // 8)
    def _(t):
        at = pl.ds(pl.multiple_of(t * 8, 8), 8)
        for first in range(0, LINES, 8):
            sums = [None] * 8
            for j in range(max(0, first - HALF), min(LINES, first + 8 + HALF)):
                v = line(j, at)
                for m in range(8):
                    k = j - (first + m) + HALF
                    if 0 <= k < TAPS:
                        term = weights[k] * v
                        sums[m] = term if sums[m] is None else sums[m] + term
            for m in range(8):
                out[first + m, at, :] = sums[m]


def own_lines(way, taps, low, mid, high):
    return pl.pallas_call(
        functools.partial(own_kernel, way),
        grid=(NX // XB,),
        in_specs=[pl.BlockSpec(memory_space=pltpu.SMEM)]
        + [pl.BlockSpec((s[0], XB, NZ), lambda i: (0, i, 0)) for s in EDGE_SHAPES],
        out_specs=pl.BlockSpec((LINES, XB, NZ), lambda i: (0, i, 0)),
        out_shape=jax.ShapeDtypeStruct((LINES, NX, NZ), F32),
        compiler_params=pltpu.CompilerParams(vmem_limit_bytes=VMEM_LIMIT),
        cost_estimate=pl.CostEstimate(
            flops=2 * 31 * LINES * NX * NZ * 100, bytes_accessed=2 * LINES * NX * NZ * 4, transcendentals=0
        ),
        name="own_lines",
    )(taps, low, mid, high)


def add_halo(way, taps, meta, partial, below, above, at, use):
    weights = [jnp.full((8, NZ), tap, F32) for tap in tap_list(taps, 2, way)]
    has_below, has_above = meta[0] != 0, meta[1] != 0
    for first in range(0, LINES, 8):
        sums = [partial[first + m, at, :] for m in range(8)]
        for j in range(HALF):
            if j >= first:
                v = jnp.where(has_below, below[j, at, :], 0.0)
                for m in range(8):
                    k = j - (first + m)
                    if 0 <= k < HALF:
                        sums[m] = sums[m] + weights[k] * v
        for j in range(HALF):
            if LINES + j - (first + 7) <= HALF:
                v = jnp.where(has_above, above[j, at, :], 0.0)
                for m in range(8):
                    k = LINES + j - (first + m) + HALF
                    if k < TAPS:
                        sums[m] = sums[m] + weights[k] * v
        for m in range(8):
            use(first + m, sums[m])


def step_kernel(ratio, taps, meta, partial, below, above, other, z_table, xh, xl, *rest):
    if ratio:
        low, mid, high, work, zhi, zlo = rest
    else:
        work, low, mid, high, zhi, zlo = rest
    i = pl.program_id(0)

    @pl.loop(0, XB // 8)
    def _(t):
        at = pl.ds(pl.multiple_of(t * 8, 8), 8)

        def use(y, total):
            if ratio:
                work[y, at, :] = other[y, at, :] / (total + BACKGROUND)
            else:
                work[y, at, :] = other[y, at, :] * total

        add_halo(0 if ratio else 1, taps, meta, partial, below, above, at, use)

    to = pl.ds(pl.multiple_of(i * XB, XB), XB)

    @pl.loop(0, LINES // 4)
    def _(g):
        v = work[pl.ds(g * 4, 4)].reshape(4 * XB, NZ)
        hi, lo = split(filter_z(v, z_table[...]))
        zhi[pl.ds(g * 4, 4), to, :] = hi.reshape(4, XB, NZ)
        zlo[pl.ds(g * 4, 4), to, :] = lo.reshape(4, XB, NZ)

    @pl.when(i == NX // XB - 1)
    def _():
        def pair(y):
            hi = jnp.concatenate([zhi[y], zhi[y + 1]], axis=1)
            lo = jnp.concatenate([zlo[y], zlo[y + 1]], axis=1)
            both = filter_x_pair(hi, lo, xh[...], xl[...])
            return both[:, :NZ], both[:, NZ:]

        for_pairs(pair, low, mid, high)


def step(ratio, taps, meta, partial, below, above, other, tables):
    smem = pl.BlockSpec(memory_space=pltpu.SMEM)
    whole = pl.BlockSpec(memory_space=pltpu.VMEM)
    lines = pl.BlockSpec((LINES, XB, NZ), lambda i: (0, i, 0))
    edge = pl.BlockSpec((HALF, XB, NZ), lambda i: (0, i, 0))
    full = jax.ShapeDtypeStruct((LINES, NX, NZ), F32)
    edges = [jax.ShapeDtypeStruct(s, F32) for s in EDGE_SHAPES]
    scratch = [pltpu.VMEM((LINES, NX, NZ), BF16)] * 2
    return pl.pallas_call(
        functools.partial(step_kernel, ratio),
        grid=(NX // XB,),
        in_specs=[smem, smem, lines, edge, edge, lines] + [whole] * 3,
        out_specs=([] if ratio else [lines]) + [whole] * 3,
        out_shape=([] if ratio else [full]) + edges,
        scratch_shapes=([pltpu.VMEM((LINES, XB, NZ), F32)] if ratio else []) + scratch,
        compiler_params=pltpu.CompilerParams(vmem_limit_bytes=VMEM_LIMIT),
        name="ratio_step" if ratio else "estimate_step",
    )(taps, meta, partial, below, above, other, *tables)


def last_kernel(meta, taps, partial, below, above, other, out):
    @pl.loop(0, LINES // 8)
    def _(t):
        at = pl.ds(pl.multiple_of(t * 8, 8), 8)

        def use(y, total):
            out[0, y, at, :] = other[y, at, :] * total

        add_halo(1, taps, meta, partial, below, above, at, use)


def last(taps, meta, partial, below, above, other, first, count):
    smem = pl.BlockSpec(memory_space=pltpu.SMEM)

    def at(i, meta):
        return (0, meta[2 + first + i], 0)

    lines = pl.BlockSpec((LINES, 32, NZ), at)
    edge = pl.BlockSpec((HALF, 32, NZ), at)
    return pl.pallas_call(
        last_kernel,
        grid_spec=pltpu.PrefetchScalarGridSpec(
            num_scalar_prefetch=1,
            grid=(count,),
            in_specs=[smem, lines, edge, edge, lines],
            out_specs=pl.BlockSpec((1, LINES, 32, NZ), lambda i, *_: (i, 0, 0, 0)),
        ),
        out_shape=jax.ShapeDtypeStruct((count, LINES, 32, NZ), F32),
        compiler_params=pltpu.CompilerParams(vmem_limit_bytes=VMEM_LIMIT),
        name="last_step",
    )(meta, taps, partial, below, above, other)


def leave_kernel(meta, *refs):
    parts, out, held = refs[:ROUNDS], refs[ROUNDS], refs[ROUNDS + 1]
    rows = LINES * 32
    for j in range(ROUNDS):
        base = meta[2 + ROUNDS + j] * rows

        @pl.loop(0, LINES)
        def _(y):
            held[pl.ds(pl.multiple_of(base + y * 32, 32), 32), :] = parts[j][0, y]

    @pl.loop(0, CH * 32)
    def _(i):
        start = (i // 32) * (128 * 32) + lax.rem(i, 32)
        tile = held[pl.ds(start, 128, stride=32), :].T
        out[pl.ds(start, 128, stride=32), :] = tile


def leave(meta, parts):
    whole = pl.BlockSpec(memory_space=pltpu.VMEM)
    return pl.pallas_call(
        leave_kernel,
        in_specs=[pl.BlockSpec(memory_space=pltpu.SMEM)] + [whole] * ROUNDS,
        out_specs=whole,
        out_shape=jax.ShapeDtypeStruct((CH * NZ * 32, 128), F32),
        scratch_shapes=[pltpu.VMEM((CH * 128 * 32, NZ), F32)],
        compiler_params=pltpu.CompilerParams(vmem_limit_bytes=VMEM_LIMIT),
        name="leave",
    )(meta, *parts)


def local(raw_stack, psf_taps):
    me = lax.axis_index("gx") * 8 + lax.axis_index("gy")
    channel = lax.rem(lax.axis_index("gy"), 2)
    meta = lax.dynamic_index_in_dim(jnp.asarray(meta_table()), me, keepdims=False)
    taps = lax.dynamic_index_in_dim(psf_taps, channel, axis=1, keepdims=False)
    taps = taps / jnp.sum(taps, axis=1, keepdims=True)

    blocks = destripe(raw_stack).reshape(128, 64, 128)
    got = lax.all_to_all(blocks, AXES, split_axis=0, concat_axis=0, tiled=True)
    tables = filter_tables(taps)
    cleaned, low, mid, high = arrive(got.reshape(128 * 64, 128), tables[0])

    estimate = cleaned
    for blur in range(2 * ITERS):
        way = blur % 2
        below = lax.ppermute(high, AXES, UP)
        above = lax.ppermute(low, AXES, DOWN)
        partial = own_lines(way, taps, low, mid, high)
        if blur == 2 * ITERS - 1:
            parts = [last(taps, meta, partial, below, above, estimate, j, 1) for j in range(ROUNDS)]
        elif way == 0:
            low, mid, high = step(True, taps, meta, partial, below, above, cleaned, tables[1])
        else:
            estimate, low, mid, high = step(
                False, taps, meta, partial, below, above, estimate, tables[0]
            )
    parts = [lax.ppermute(part, AXES, FINAL[j]) for j, part in enumerate(parts)]
    return leave(meta, parts).reshape(CH, NZ, 32, 128)


def solution(mesh):
    in_specs = (P(None, AXES, None, None), P())
    out_specs = P(None, None, "gy", "gx")
    return jax.shard_map(local, mesh=mesh, in_specs=in_specs, out_specs=out_specs, check_vma=False)
```

time: 776 us -> 341 us (0.44)
  the two profiles are of different devices: /device:TPU:15 before, /device:TPU:104 now
where the time goes in v1:
time: 341 us; the launch traced here: 340 us
  Pallas kernels  170 us (50%)
  waiting for transfers between devices  127 us (37%)
  starting transfers between devices  36.4 us (11%)
  local copies, waits for them, and re-layouts  5.12 us (2%)
    pallas_call x3, Pallas kernels, step(): pl.pallas_call(functools.partial(step_kernel, ratio), grid=(NX // XB,), i...  53.6 us
    ppermute x4, waiting for transfers between devices, local(): above = lax.ppermute(low, AXES, DOWN)  48.8 us
    all_to_all x1, waiting for transfers between devices, local(): got = lax.all_to_all(blocks, AXES, split_axis=0, concat_axis=0, tiled=True)  44.5 us
    pallas_call x4, Pallas kernels, own_lines(): pl.pallas_call(functools.partial(own_kernel, way), grid=(NX // XB,), in_s...  38.8 us
    ppermute x8, waiting for transfers between devices, local(): parts = [lax.ppermute(part, AXES, FINAL[j]) for j, part in enumerate(parts)]  26.5 us
    pallas_call x8, Pallas kernels, last(): pl.pallas_call(last_kernel, grid_spec=pltpu.PrefetchScalarGridSpec(num_sc...  25.8 us
    ppermute x8, starting transfers between devices, local(): parts = [lax.ppermute(part, AXES, FINAL[j]) for j, part in enumerate(parts)]  19.7 us
    pallas_call x1, Pallas kernels, leave(): pl.pallas_call(leave_kernel, in_specs=[pl.BlockSpec(memory_space=pltpu.SM...  16.7 us
  transfers between devices with their start and end apart: 17, of which 12 were waited for; matrix products, arithmetic and copies ran while one was open for 1% of the time, Pallas kernels for 19%

profile of v1, /device:TPU:104, one launch (start us, length us, event | category | flops | bytes accessed | tf_op | source)
XLA Modules:
  0.0 340.0 jit_solution(7179917841860315252)
XLA Ops:
  0.0 16.7 %destripe.1 = f32[16,4,2,64,128]{4,3,2,1,0:T(8,128)} custom-call(f32[2,1,256,2048]{3,2,1,0:T(8,128)} %raw.1, bf16[256,256]{1,0:T(8,128)(2,1)} %constant.47.clone.ah, bf16[256,256]{1,0:T(8,128)(2,1)} %constant.48.clone.al, bf16[1024,1024]{1,0:T(8,128)(2,1)} %constant.49.clone.oh, bf16[1024,1024]{1,0:T(8,128)(2,1)} %constant.50.clone.ol, ...), custom_call_target="tpu_custom_call" | custom-call | tf_op jit(solution)/shard_map/destripe/pallas_call | solution.py:166
  16.7 10.3 %all-to-all-start = ((f32[128,64,128]{2,1,0:T(8,128)}), f32[128,64,128]{2,1,0:T(8,128)}, u32[]{:S(2)}, u32[]{:S(2)}) async-start(f32[128,64,128]{2,1,0:T(8,128)} %bitcast.7), calls=%async_computation | async-start | bytes 8388608 | tf_op jit(solution)/shard_map/all_to_all | solution.py:486
  27.1 0.7 bitcast_divide_fusion.taps
  27.7 2.3 tables.1
  30.0 44.5 %all-to-all-done = f32[128,64,128]{2,1,0:T(8,128)} async-done(((f32[128,64,128]{2,1,0:T(8,128)}), f32[128,64,128]{2,1,0:T(8,128)}, u32[]{:S(2)}, u32[]{:S(2)}) %all-to-all-start) | async-done | bytes 4194336 | tf_op jit(solution)/shard_map/all_to_all | solution.py:486
  74.5 16.5 %arrive.1 = (f32[32,256,128]{2,1,0:T(8,128)}, f32[15,256,128]{2,1,0:T(8,128)}, f32[2,256,128]{2,1,0:T(8,128)}, f32[15,256,128]{2,1,0:T(8,128)}) custom-call(f32[8192,128]{1,0:T(8,128)} %bitcast.2.got, bf16[256,256]{1,0:T(8,128)(2,1)} %get-tuple-element.25.z_table, bf16[256,256]{1,0:T(8,128)(2,1)} %get-tuple-element.26.xh, bf16[256,256]{1,0:T(8,128)(2,1)} %get-tuple-element.27.xl), custom_call_target="tpu_custom_call" | custom-call | tf_op jit(solution)/shard_map/arrive/pallas_call | solution.py:277
  91.1 0.6 collective-permute-start.1
  91.7 0.6 collective-permute-start
  92.3 1.2 dynamic-slice_bitcast_fusion.meta
  93.5 9.7 %own_lines.4.partial = f32[32,256,128]{2,1,0:T(8,128)} custom-call(f32[3,31]{1,0:T(4,128)} %bitcast_divide_fusion.taps, f32[15,256,128]{2,1,0:T(8,128)} %get-tuple-element.28.low, f32[2,256,128]{2,1,0:T(8,128)} %get-tuple-element.29.mid, f32[15,256,128]{2,1,0:T(8,128)} %get-tuple-element.30.high), custom_call_target="tpu_custom_call" | custom-call | flops 6501171200 | bytes 8388608 | tf_op jit(solution)/shard_map/own_lines/pallas_call | solution.py:318
  103.2 11.0 %collective-permute-done.1.above = f32[15,256,128]{2,1,0:T(8,128)S(1)} collective-permute-done((f32[15,256,128]{2,1,0:T(8,128)}, f32[15,256,128]{2,1,0:T(8,128)S(1)}, u32[]{:S(2)}, u32[]{:S(2)}) %collective-permute-start.1) | collective-permute-done | bytes 1966112 | tf_op jit(solution)/shard_map/ppermute | solution.py:494
  114.2 1.9 collective-permute-done.below
  116.1 17.9 %ratio_step.2 = (f32[15,256,128]{2,1,0:T(8,128)}, f32[2,256,128]{2,1,0:T(8,128)}, f32[15,256,128]{2,1,0:T(8,128)}) custom-call(f32[3,31]{1,0:T(4,128)} %bitcast_divide_fusion.taps, s32[18]{0:T(128)} %dynamic-slice_bitcast_fusion.meta, f32[32,256,128]{2,1,0:T(8,128)} %own_lines.4.partial, f32[15,256,128]{2,1,0:T(8,128)} %collective-permute-done.below, ...), custom_call_target="tpu_custom_call" | custom-call | tf_op jit(solution)/shard_map/ratio_step/pallas_call | solution.py:403
  133.9 1.6 collective-permute-start.3
  135.8 9.7 %own_lines.5.partial = f32[32,256,128]{2,1,0:T(8,128)} custom-call(f32[3,31]{1,0:T(4,128)} %bitcast_divide_fusion.taps, f32[15,256,128]{2,1,0:T(8,128)} %get-tuple-element.35.low, f32[2,256,128]{2,1,0:T(8,128)} %get-tuple-element.36.mid, f32[15,256,128]{2,1,0:T(8,128)} %get-tuple-element.37.high), custom_call_target="tpu_custom_call" | custom-call | flops 6501171200 | bytes 8388608 | tf_op jit(solution)/shard_map/own_lines/pallas_call | solution.py:318
  145.5 12.5 %collective-permute-done.3.above = f32[15,256,128]{2,1,0:T(8,128)S(1)} collective-permute-done((f32[15,256,128]{2,1,0:T(8,128)}, f32[15,256,128]{2,1,0:T(8,128)S(1)}, u32[]{:S(2)}, u32[]{:S(2)}) %collective-permute-start.3) | collective-permute-done | bytes 1966112 | tf_op jit(solution)/shard_map/ppermute | solution.py:494
  158.0 1.8 collective-permute-done.2.below
  159.8 1.3 copy-done.5
  161.0 17.8 %estimate_step.1 = (f32[32,256,128]{2,1,0:T(8,128)}, f32[15,256,128]{2,1,0:T(8,128)}, f32[2,256,128]{2,1,0:T(8,128)}, f32[15,256,128]{2,1,0:T(8,128)}) custom-call(f32[3,31]{1,0:T(4,128)} %bitcast_divide_fusion.taps, s32[18]{0:T(128)} %dynamic-slice_bitcast_fusion.meta, f32[32,256,128]{2,1,0:T(8,128)} %own_lines.5.partial, f32[15,256,128]{2,1,0:T(8,128)} %copy-done.5, ...), custom_call_target="tpu_custom_call" | custom-call | tf_op jit(solution)/shard_map/estimate_step/pallas_call | solution.py:403
  178.9 1.7 collective-permute-start.5
  180.7 9.7 %own_lines.6.partial = f32[32,256,128]{2,1,0:T(8,128)} custom-call(f32[3,31]{1,0:T(4,128)} %bitcast_divide_fusion.taps, f32[15,256,128]{2,1,0:T(8,128)} %get-tuple-element.38.low, f32[2,256,128]{2,1,0:T(8,128)} %get-tuple-element.39.mid, f32[15,256,128]{2,1,0:T(8,128)} %get-tuple-element.40.high), custom_call_target="tpu_custom_call" | custom-call | flops 6501171200 | bytes 8388608 | tf_op jit(solution)/shard_map/own_lines/pallas_call | solution.py:318
  190.4 12.6 %collective-permute-done.5.above = f32[15,256,128]{2,1,0:T(8,128)S(1)} collective-permute-done((f32[15,256,128]{2,1,0:T(8,128)}, f32[15,256,128]{2,1,0:T(8,128)S(1)}, u32[]{:S(2)}, u32[]{:S(2)}) %collective-permute-start.5) | collective-permute-done | bytes 1966112 | tf_op jit(solution)/shard_map/ppermute | solution.py:494
  203.0 1.8 collective-permute-done.4.below
  204.8 1.3 copy-done.6
  206.1 17.9 %ratio_step.3 = (f32[15,256,128]{2,1,0:T(8,128)}, f32[2,256,128]{2,1,0:T(8,128)}, f32[15,256,128]{2,1,0:T(8,128)}) custom-call(f32[3,31]{1,0:T(4,128)} %bitcast_divide_fusion.taps, s32[18]{0:T(128)} %dynamic-slice_bitcast_fusion.meta, f32[32,256,128]{2,1,0:T(8,128)} %own_lines.6.partial, f32[15,256,128]{2,1,0:T(8,128)} %copy-done.6, ...), custom_call_target="tpu_custom_call" | custom-call | tf_op jit(solution)/shard_map/ratio_step/pallas_call | solution.py:403
  224.0 1.6 collective-permute-start.7
  225.6 9.7 %own_lines.7.partial = f32[32,256,128]{2,1,0:T(8,128)} custom-call(f32[3,31]{1,0:T(4,128)} %bitcast_divide_fusion.taps, f32[15,256,128]{2,1,0:T(8,128)} %get-tuple-element.41.low, f32[2,256,128]{2,1,0:T(8,128)} %get-tuple-element.42.mid, f32[15,256,128]{2,1,0:T(8,128)} %get-tuple-element.43.high), custom_call_target="tpu_custom_call" | custom-call | flops 6501171200 | bytes 8388608 | tf_op jit(solution)/shard_map/own_lines/pallas_call | solution.py:318
  235.2 12.8 %collective-permute-done.7.above = f32[15,256,128]{2,1,0:T(8,128)S(1)} collective-permute-done((f32[15,256,128]{2,1,0:T(8,128)}, f32[15,256,128]{2,1,0:T(8,128)S(1)}, u32[]{:S(2)}, u32[]{:S(2)}) %collective-permute-start.7) | collective-permute-done | bytes 1966112 | tf_op jit(solution)/shard_map/ppermute | solution.py:494
  248.0 1.8 collective-permute-done.6.below
  249.8 1.3 copy-done.1
  251.1 3.2 last_step.8
  254.3 3.5 %collective-permute-start.8 = (f32[1,32,32,128]{3,2,1,0:T(8,128)}, f32[1,32,32,128]{3,2,1,0:T(8,128)S(1)}, u32[]{:S(2)}, u32[]{:S(2)}) collective-permute-start(f32[1,32,32,128]{3,2,1,0:T(8,128)} %last_step.8), channel_id=1, source_target_pairs={{0,0},{8,5},{2,2},{10,7},{4,12},{12,9},{6,14},{14,11},{22,22},{30,... | collective-permute-start | bytes 1572872 | tf_op jit(solution)/shard_map/ppermute | solution.py:504
  257.8 3.2 last_step.9
  261.0 1.3 collective-permute-start.9
  262.3 3.2 last_step.10
  265.5 3.0 collective-permute-start.10
  268.4 3.2 last_step.11
  271.6 4.0 %collective-permute-start.11 = (f32[1,32,32,128]{3,2,1,0:T(8,128)}, f32[1,32,32,128]{3,2,1,0:T(8,128)S(1)}, u32[]{:S(2)}, u32[]{:S(2)}) collective-permute-start(f32[1,32,32,128]{3,2,1,0:T(8,128)} %last_step.11), channel_id=1, source_target_pairs={{0,3},{8,6},{2,5},{10,0},{4,15},{12,10},{6,9},{14,12},{22,17},{30,... | collective-permute-start | bytes 1572872 | tf_op jit(solution)/shard_map/ppermute | solution.py:504
  275.6 3.2 last_step.12
  278.8 6.0 %collective-permute-start.12 = (f32[1,32,32,128]{3,2,1,0:T(8,128)}, f32[1,32,32,128]{3,2,1,0:T(8,128)S(1)}, u32[]{:S(2)}, u32[]{:S(2)}) collective-permute-start(f32[1,32,32,128]{3,2,1,0:T(8,128)} %last_step.12), channel_id=1, source_target_pairs={{0,4},{8,1},{2,6},{10,3},{4,8},{12,13},{6,10},{14,15},{22,18},{30,... | collective-permute-start | bytes 1572872 | tf_op jit(solution)/shard_map/ppermute | solution.py:504
  284.8 3.2 last_step.15
  288.0 3.3 last_step.14
  291.2 3.3 last_step.13
  294.6 1.9 collective-permute-start.13
  296.8 19.0 %collective-permute-done.13.refs_5_ = f32[1,32,32,128]{3,2,1,0:T(8,128)S(1)} collective-permute-done((f32[1,32,32,128]{3,2,1,0:T(8,128)}, f32[1,32,32,128]{3,2,1,0:T(8,128)S(1)}, u32[]{:S(2)}, u32[]{:S(2)}) %collective-permute-start.13) | collective-permute-done | bytes 524320 | tf_op jit(solution)/shard_map/ppermute | solution.py:504
  315.7 3.1 collective-permute-done.14.refs_6_
  318.8 4.4 %collective-permute-done.15.refs_7_ = f32[1,32,32,128]{3,2,1,0:T(8,128)} collective-permute-done((f32[1,32,32,128]{3,2,1,0:T(8,128)S(1)}, f32[1,32,32,128]{3,2,1,0:T(8,128)}, u32[]{:S(2)}, u32[]{:S(2)}) %collective-permute-start.15) | collective-permute-done | bytes 524320 | tf_op jit(solution)/shard_map/ppermute | solution.py:504
  323.3 16.7 %leave.1 = f32[8192,128]{1,0:T(8,128)} custom-call(s32[18]{0:T(128)} %dynamic-slice_bitcast_fusion.meta, f32[1,32,32,128]{3,2,1,0:T(8,128)} %copy-done.7, f32[1,32,32,128]{3,2,1,0:T(8,128)} %copy-done.8, f32[1,32,32,128]{3,2,1,0:T(8,128)} %copy-done.9, f32[1,32,32,128]{3,2,1,0:T(8,128)} %copy-done.10, f32[1,32,32,128]{3,2,1,0:T(8,128)} %copy-done.11, ...), custom_call_target="tpu_custom_call" | custom-call | tf_op jit(solution)/shard_map/leave/pallas_call | solution.py:467
  (38 shorter events, 0.7 us)
Async XLA Ops:
  16.7 10.3 %copy-start.14 = (f32[3,2,31]{2,1,0:T(2,128)S(1)}, f32[3,2,31]{2,1,0:T(2,128)}, u32[]{:S(2)}) copy-start(f32[3,2,31]{2,1,0:T(2,128)} %param.12) | copy-start | bytes 2236
  16.7 57.9 %all-to-all-start = ((f32[128,64,128]{2,1,0:T(8,128)}), f32[128,64,128]{2,1,0:T(8,128)}, u32[]{:S(2)}, u32[]{:S(2)}) async-start(f32[128,64,128]{2,1,0:T(8,128)} %bitcast.7), calls=%async_computation | async-start | bytes 8388608 | tf_op jit(solution)/shard_map/all_to_all | solution.py:486
  91.1 23.1 %collective-permute-start.1 = (f32[15,256,128]{2,1,0:T(8,128)}, f32[15,256,128]{2,1,0:T(8,128)S(1)}, u32[]{:S(2)}, u32[]{:S(2)}) collective-permute-start(f32[15,256,128]{2,1,0:T(8,128)} %get-tuple-element.28.low), channel_id=1, source_target_pairs={{8,0},{2,8},{10,2},{4,10},{12,4},{6,12},{14,6},{22,14},{30,22},{20... | collective-permute-start | bytes 5898248 | tf_op jit(solution)/shard_map/ppermute | solution.py:494
  91.7 24.4 %collective-permute-start = (f32[15,256,128]{2,1,0:T(8,128)}, f32[15,256,128]{2,1,0:T(8,128)}, u32[]{:S(2)}, u32[]{:S(2)}) collective-permute-start(f32[15,256,128]{2,1,0:T(8,128)} %get-tuple-element.30.high), channel_id=1, source_target_pairs={{0,8},{8,2},{2,10},{10,4},{4,12},{12,6},{6,14},{14,22},{22,30},{30... | collective-permute-start | bytes 5898248 | tf_op jit(solution)/shard_map/ppermute | solution.py:493
  114.2 1.9 copy-start.2
  133.9 24.0 %collective-permute-start.3 = (f32[15,256,128]{2,1,0:T(8,128)}, f32[15,256,128]{2,1,0:T(8,128)S(1)}, u32[]{:S(2)}, u32[]{:S(2)}) collective-permute-start(f32[15,256,128]{2,1,0:T(8,128)} %get-tuple-element.35.low), channel_id=1, source_target_pairs={{8,0},{2,8},{10,2},{4,10},{12,4},{6,12},{14,6},{22,14},{30,22},{20... | collective-permute-start | bytes 5898248 | tf_op jit(solution)/shard_map/ppermute | solution.py:494
  135.5 24.3 %collective-permute-start.2 = (f32[15,256,128]{2,1,0:T(8,128)}, f32[15,256,128]{2,1,0:T(8,128)S(1)}, u32[]{:S(2)}, u32[]{:S(2)}) collective-permute-start(f32[15,256,128]{2,1,0:T(8,128)} %get-tuple-element.37.high), channel_id=1, source_target_pairs={{0,8},{8,2},{2,10},{10,4},{4,12},{12,6},{6,14},{14,22},{22,30},{30... | collective-permute-start | bytes 5898248 | tf_op jit(solution)/shard_map/ppermute | solution.py:493
  158.0 1.8 copy-start.3
  159.8 1.3 copy-start.5
  178.9 24.1 %collective-permute-start.5 = (f32[15,256,128]{2,1,0:T(8,128)}, f32[15,256,128]{2,1,0:T(8,128)S(1)}, u32[]{:S(2)}, u32[]{:S(2)}) collective-permute-start(f32[15,256,128]{2,1,0:T(8,128)} %get-tuple-element.38.low), channel_id=1, source_target_pairs={{8,0},{2,8},{10,2},{4,10},{12,4},{6,12},{14,6},{22,14},{30,22},{20... | collective-permute-start | bytes 5898248 | tf_op jit(solution)/shard_map/ppermute | solution.py:494
  180.6 24.3 %collective-permute-start.4 = (f32[15,256,128]{2,1,0:T(8,128)}, f32[15,256,128]{2,1,0:T(8,128)S(1)}, u32[]{:S(2)}, u32[]{:S(2)}) collective-permute-start(f32[15,256,128]{2,1,0:T(8,128)} %get-tuple-element.40.high), channel_id=1, source_target_pairs={{0,8},{8,2},{2,10},{10,4},{4,12},{12,6},{6,14},{14,22},{22,30},{30... | collective-permute-start | bytes 5898248 | tf_op jit(solution)/shard_map/ppermute | solution.py:493
  203.0 1.8 copy-start.4
  204.8 1.3 copy-start.6
  224.0 24.0 %collective-permute-start.7 = (f32[15,256,128]{2,1,0:T(8,128)}, f32[15,256,128]{2,1,0:T(8,128)S(1)}, u32[]{:S(2)}, u32[]{:S(2)}) collective-permute-start(f32[15,256,128]{2,1,0:T(8,128)} %get-tuple-element.41.low), channel_id=1, source_target_pairs={{8,0},{2,8},{10,2},{4,10},{12,4},{6,12},{14,6},{22,14},{30,22},{20... | collective-permute-start | bytes 5898248 | tf_op jit(solution)/shard_map/ppermute | solution.py:494
  225.6 24.3 %collective-permute-start.6 = (f32[15,256,128]{2,1,0:T(8,128)}, f32[15,256,128]{2,1,0:T(8,128)S(1)}, u32[]{:S(2)}, u32[]{:S(2)}) collective-permute-start(f32[15,256,128]{2,1,0:T(8,128)} %get-tuple-element.43.high), channel_id=1, source_target_pairs={{0,8},{8,2},{2,10},{10,4},{4,12},{12,6},{6,14},{14,22},{22,30},{30... | collective-permute-start | bytes 5898248 | tf_op jit(solution)/shard_map/ppermute | solution.py:493
  248.0 1.8 copy-start
  249.8 1.3 copy-start.1
  254.3 40.2 %collective-permute-start.8 = (f32[1,32,32,128]{3,2,1,0:T(8,128)}, f32[1,32,32,128]{3,2,1,0:T(8,128)S(1)}, u32[]{:S(2)}, u32[]{:S(2)}) collective-permute-start(f32[1,32,32,128]{3,2,1,0:T(8,128)} %last_step.8), channel_id=1, source_target_pairs={{0,0},{8,5},{2,2},{10,7},{4,12},{12,9},{6,14},{14,11},{22,22},{30,... | collective-permute-start | bytes 1572872 | tf_op jit(solution)/shard_map/ppermute | solution.py:504
  261.0 35.5 %collective-permute-start.9 = (f32[1,32,32,128]{3,2,1,0:T(8,128)}, f32[1,32,32,128]{3,2,1,0:T(8,128)S(1)}, u32[]{:S(2)}, u32[]{:S(2)}) collective-permute-start(f32[1,32,32,128]{3,2,1,0:T(8,128)} %last_step.9), channel_id=1, source_target_pairs={{0,1},{8,4},{2,3},{10,6},{4,13},{12,8},{6,15},{14,10},{22,23},{30,... | collective-permute-start | bytes 1572872 | tf_op jit(solution)/shard_map/ppermute | solution.py:504
  265.5 31.1 %collective-permute-start.10 = (f32[1,32,32,128]{3,2,1,0:T(8,128)}, f32[1,32,32,128]{3,2,1,0:T(8,128)S(1)}, u32[]{:S(2)}, u32[]{:S(2)}) collective-permute-start(f32[1,32,32,128]{3,2,1,0:T(8,128)} %last_step.10), channel_id=1, source_target_pairs={{0,2},{8,7},{2,4},{10,1},{4,14},{12,11},{6,8},{14,13},{22,16},{30,... | collective-permute-start | bytes 1572872 | tf_op jit(solution)/shard_map/ppermute | solution.py:504
  271.6 25.1 %collective-permute-start.11 = (f32[1,32,32,128]{3,2,1,0:T(8,128)}, f32[1,32,32,128]{3,2,1,0:T(8,128)S(1)}, u32[]{:S(2)}, u32[]{:S(2)}) collective-permute-start(f32[1,32,32,128]{3,2,1,0:T(8,128)} %last_step.11), channel_id=1, source_target_pairs={{0,3},{8,6},{2,5},{10,0},{4,15},{12,10},{6,9},{14,12},{22,17},{30,... | collective-permute-start | bytes 1572872 | tf_op jit(solution)/shard_map/ppermute | solution.py:504
  278.8 17.9 %collective-permute-start.12 = (f32[1,32,32,128]{3,2,1,0:T(8,128)}, f32[1,32,32,128]{3,2,1,0:T(8,128)S(1)}, u32[]{:S(2)}, u32[]{:S(2)}) collective-permute-start(f32[1,32,32,128]{3,2,1,0:T(8,128)} %last_step.12), channel_id=1, source_target_pairs={{0,4},{8,1},{2,6},{10,3},{4,8},{12,13},{6,10},{14,15},{22,18},{30,... | collective-permute-start | bytes 1572872 | tf_op jit(solution)/shard_map/ppermute | solution.py:504
  291.2 5.4 %copy-start.12 = (f32[1,32,32,128]{3,2,1,0:T(8,128)S(1)}, f32[1,32,32,128]{3,2,1,0:T(8,128)}, u32[]{:S(2)}) copy-start(f32[1,32,32,128]{3,2,1,0:T(8,128)} %last_step.15) | copy-start | bytes 1572868
  294.6 28.7 %copy-start.7 = (f32[1,32,32,128]{3,2,1,0:T(8,128)}, f32[1,32,32,128]{3,2,1,0:T(8,128)S(1)}, u32[]{:S(2)}) copy-start(f32[1,32,32,128]{3,2,1,0:T(8,128)S(1)} %collective-permute-done.8.refs_0_) | copy-start | bytes 1572868
  294.6 21.2 %collective-permute-start.13 = (f32[1,32,32,128]{3,2,1,0:T(8,128)}, f32[1,32,32,128]{3,2,1,0:T(8,128)S(1)}, u32[]{:S(2)}, u32[]{:S(2)}) collective-permute-start(f32[1,32,32,128]{3,2,1,0:T(8,128)} %last_step.13), channel_id=1, source_target_pairs={{0,5},{8,0},{2,7},{10,2},{4,9},{12,12},{6,11},{14,14},{22,19},{30,... | collective-permute-start | bytes 1572872 | tf_op jit(solution)/shard_map/ppermute | solution.py:504
  296.5 26.8 %copy-start.8 = (f32[1,32,32,128]{3,2,1,0:T(8,128)}, f32[1,32,32,128]{3,2,1,0:T(8,128)S(1)}, u32[]{:S(2)}) copy-start(f32[1,32,32,128]{3,2,1,0:T(8,128)S(1)} %collective-permute-done.9.refs_1_) | copy-start | bytes 1572868
  296.5 22.3 %collective-permute-start.14 = (f32[1,32,32,128]{3,2,1,0:T(8,128)}, f32[1,32,32,128]{3,2,1,0:T(8,128)}, u32[]{:S(2)}, u32[]{:S(2)}) collective-permute-start(f32[1,32,32,128]{3,2,1,0:T(8,128)} %last_step.14), channel_id=1, source_target_pairs={{0,6},{8,3},{2,0},{10,5},{4,10},{12,15},{6,12},{14,9},{22,20},{30,... | collective-permute-start | bytes 1572872 | tf_op jit(solution)/shard_map/ppermute | solution.py:504
  296.6 26.7 %copy-start.9 = (f32[1,32,32,128]{3,2,1,0:T(8,128)}, f32[1,32,32,128]{3,2,1,0:T(8,128)S(1)}, u32[]{:S(2)}) copy-start(f32[1,32,32,128]{3,2,1,0:T(8,128)S(1)} %collective-permute-done.10.refs_2_) | copy-start | bytes 1572868
  296.6 26.7 %collective-permute-start.15 = (f32[1,32,32,128]{3,2,1,0:T(8,128)S(1)}, f32[1,32,32,128]{3,2,1,0:T(8,128)}, u32[]{:S(2)}, u32[]{:S(2)}) collective-permute-start(f32[1,32,32,128]{3,2,1,0:T(8,128)S(1)} %copy-done.12), channel_id=1, source_target_pairs={{0,7},{8,2},{2,1},{10,4},{4,11},{12,14},{6,13},{14,8},{22,21},{30,... | collective-permute-start | bytes 1572872 | tf_op jit(solution)/shard_map/ppermute | solution.py:504
  296.7 26.6 %copy-start.10 = (f32[1,32,32,128]{3,2,1,0:T(8,128)}, f32[1,32,32,128]{3,2,1,0:T(8,128)S(1)}, u32[]{:S(2)}) copy-start(f32[1,32,32,128]{3,2,1,0:T(8,128)S(1)} %collective-permute-done.11.refs_3_) | copy-start | bytes 1572868
  296.7 26.6 %copy-start.11 = (f32[1,32,32,128]{3,2,1,0:T(8,128)}, f32[1,32,32,128]{3,2,1,0:T(8,128)S(1)}, u32[]{:S(2)}) copy-start(f32[1,32,32,128]{3,2,1,0:T(8,128)S(1)} %collective-permute-done.12.refs_4_) | copy-start | bytes 1572868
  315.7 7.6 %copy-start.13 = (f32[1,32,32,128]{3,2,1,0:T(8,128)}, f32[1,32,32,128]{3,2,1,0:T(8,128)S(1)}, u32[]{:S(2)}) copy-start(f32[1,32,32,128]{3,2,1,0:T(8,128)S(1)} %collective-permute-done.13.refs_5_) | copy-start | bytes 1572868

commit v2 on v1

v2 whole, which is shorter than its diff:
```python
import functools

import jax
import jax.numpy as jnp
import numpy as np
from jax import lax
from jax.experimental import pallas as pl
from jax.experimental.pallas import tpu as pltpu
from jax.sharding import PartitionSpec as P

CH, NZ, NX, NY = 2, 128, 256, 2048
TAPS, HALF = 31, 15
ITERS = 2
BACKGROUND = 0.5
SIGMA_ACROSS = 48.0
SIGMA_ALONG = 96.0

LINES = 32
BLOCKS = NY // LINES
AXES = ("gx", "gy")
F32, BF16 = jnp.float32, jnp.bfloat16
VMEM_LIMIT = 24 * 1024 * 1024
HL = LINES // 2


def rank(x, yh, yl, z, core):
    return ((z * 2 + yl) * 2 + core) * 8 + x * 2 + yh


def place(block):
    core, row, step = block & 1, block >> 3, (block >> 1) & 3
    z, k = row >> 1, row & 1
    return (step if k == 0 else 3 - step), k ^ (z & 1), z, core


def device_of(channel, block):
    x, yl, z, core = place(block)
    return rank(x, channel, yl, z, core)


UP = [(device_of(c, b), device_of(c, (b + 1) % BLOCKS)) for c in range(CH) for b in range(BLOCKS)]
DOWN = [(target, source) for source, target in UP]

ROUNDS = 8


def final_target(channel, block, j):
    x, _, _, core = place(block)
    xd = (x + 2 * core + (j >> 1)) % 4
    x8 = 2 * xd + (channel ^ (j & 1) ^ core)
    return x8, (block >> 2) * 8 + x8


FINAL = [
    [(device_of(c, b), final_target(c, b, j)[1]) for c in range(CH) for b in range(BLOCKS)]
    for j in range(ROUNDS)
]


def meta_table():
    meta = np.zeros((128, 2 + 2 * ROUNDS), np.int32)
    for c in range(CH):
        for b in range(BLOCKS):
            me = device_of(c, b)
            meta[me, 0] = b > 0
            meta[me, 1] = b < BLOCKS - 1
            for j in range(ROUNDS):
                x8, target = final_target(c, b, j)
                meta[me, 2 + j] = x8
                meta[target, 2 + ROUNDS + j] = c * 4 + (b & 3)
    return meta


def np_split(table):
    high = table.astype(np.float32).astype(jnp.bfloat16)
    low = (table - high.astype(np.float64)).astype(np.float32).astype(jnp.bfloat16)
    return high, low


def destripe_tables():
    i = np.arange(NX, dtype=np.float64)
    across = np.exp(-0.5 * ((i[:, None] - i[None, :]) / SIGMA_ACROSS) ** 2)
    across = across / across.sum(axis=1, keepdims=True)
    n = np.arange(NY, dtype=np.float64)
    c = np.minimum(n, NY - n)
    ring = np.exp(-0.5 * (c / SIGMA_ALONG) ** 2)
    ring = ring / ring.sum()
    along = ring[(np.arange(NY)[:, None] - np.arange(NY)[None, :]) % NY]
    h, q = NY // 2, NY // 4
    even = along[:h, :h] + along[:h, h:]
    odd = along[:h, :h] - along[:h, h:]
    even_even = even[:q, :q] + even[:q, q:]
    even_odd = even[:q, :q] - even[:q, q:]
    out = []
    for table in (across.T, odd, even_even, even_odd):
        out.extend(np_split(table))
    return out


def split(v):
    high = v.astype(BF16)
    return high, (v - high.astype(F32)).astype(BF16)


def dot(a, b):
    return jnp.dot(a, b, preferred_element_type=F32)


def dot3(a_high, a_low, b_high, b_low):
    return dot(a_high, b_high) + (dot(a_high, b_low) + dot(a_low, b_high))


def destripe_kernel(raw, ah, al, oh, ol, eeh, eel, eoh, eol, out, rt, sm, dh, dl, s1h, s1l, d1h, d1l):
    h, q = NY // 2, NY // 4

    @pl.loop(0, NY // 256)
    def _(i):
        r = pl.multiple_of(i * 256, 256)
        tile = raw[0, 0, :, pl.ds(r, 256)].T
        rt[pl.ds(r, 256), :] = tile
        th, tl = split(tile)
        sm[pl.ds(r, 256), :] = dot3(th, tl, ah[...], al[...])

    @pl.loop(0, q // 128)
    def _(i):
        r = pl.multiple_of(i * 128, 128)
        parts = [sm[pl.ds(r + m * q, 128), :] for m in range(4)]
        for m in range(2):
            hi, lo = split(0.5 * (parts[m] - parts[m + 2]))
            dh[pl.ds(r + m * q, 128), :] = hi
            dl[pl.ds(r + m * q, 128), :] = lo
        top = 0.5 * (parts[0] + parts[2])
        bottom = 0.5 * (parts[1] + parts[3])
        hi, lo = split(0.5 * (top + bottom))
        s1h[pl.ds(r, 128), :] = hi
        s1l[pl.ds(r, 128), :] = lo
        hi, lo = split(0.5 * (top - bottom))
        d1h[pl.ds(r, 128), :] = hi
        d1l[pl.ds(r, 128), :] = lo

    def emit(row, smooth):
        for m in range(8):
            x, yl, z, core = place(row // LINES + m)
            at = pl.ds(row + m * LINES, LINES)
            part = smooth[m * LINES : (m + 1) * LINES, :]
            clean = jnp.maximum(rt[at, :] - (sm[at, :] - part), 0.0)
            gx = (z * 2 + yl) * 2 + core
            out[gx, x, 0, 0:LINES, :] = clean[:, :128]
            out[gx, x, 0, LINES : 2 * LINES, :] = clean[:, 128:]

    for i in range(2):
        at = slice(i * 256, (i + 1) * 256)
        ee = dot3(eeh[at, :], eel[at, :], s1h[...], s1l[...])
        eo = dot3(eoh[at, :], eol[at, :], d1h[...], d1l[...])
        for m in range(2):
            row = m * q + i * 256
            even = ee + eo if m == 0 else ee - eo
            rows = slice(row, row + 256)
            odd = dot3(oh[rows, :], ol[rows, :], dh[...], dl[...])
            emit(row, even + odd)
            emit(h + row, even - odd)


def destripe(raw_stack):
    tables = [jnp.asarray(t) for t in destripe_tables()]
    whole = pl.BlockSpec(memory_space=pltpu.VMEM)
    return pl.pallas_call(
        destripe_kernel,
        grid=(CH,),
        in_specs=[pl.BlockSpec((1, 1, NX, NY), lambda c: (c, 0, 0, 0))] + [whole] * 8,
        out_specs=pl.BlockSpec((16, 4, 1, 64, 128), lambda c: (0, 0, c, 0, 0)),
        out_shape=jax.ShapeDtypeStruct((16, 4, CH, 64, 128), F32),
        scratch_shapes=[
            pltpu.VMEM((NY, NX), F32),
            pltpu.VMEM((NY, NX), F32),
            pltpu.VMEM((NY // 2, NX), BF16),
            pltpu.VMEM((NY // 2, NX), BF16),
        ]
        + [pltpu.VMEM((NY // 4, NX), BF16)] * 4,
        compiler_params=pltpu.CompilerParams(vmem_limit_bytes=60 * 1024 * 1024),
        name="destripe",
    )(raw_stack, *tables)


def band(weights, size):
    shape = (size, size)
    lag = lax.broadcasted_iota(jnp.int32, shape, 1) - lax.broadcasted_iota(jnp.int32, shape, 0)
    out = jnp.zeros(shape, F32)
    for k in range(TAPS):
        out = jnp.where(lag == k - HALF, weights[k], out)
    return out


def tables_kernel(taps, *outs):
    for way in range(2):
        z_table, x_table = outs[2 * way : 2 * way + 2]
        hi, lo = split(band(tap_list(taps, 0, 1 - way), NZ))
        for half in range(2):
            rows = slice(half * NZ, (half + 1) * NZ)
            z_table[rows, :NZ] = hi
            z_table[rows, NZ:] = lo
        hi, lo = split(band(tap_list(taps, 1, way), NX))
        x_table[:, :NX] = hi
        x_table[:, NX : 2 * NX] = hi
        x_table[:, 2 * NX :] = lo


def filter_tables(taps):
    shapes = [jax.ShapeDtypeStruct(s, BF16) for s in ((2 * NZ, 2 * NZ), (NX, 3 * NX))]
    outs = pl.pallas_call(
        tables_kernel,
        in_specs=[pl.BlockSpec(memory_space=pltpu.SMEM)],
        out_shape=shapes * 2,
        compiler_params=pltpu.CompilerParams(vmem_limit_bytes=VMEM_LIMIT),
        cost_estimate=pl.CostEstimate(flops=10**10, bytes_accessed=10**6, transcendentals=0),
        name="tables",
    )(taps)
    return outs[:2], outs[2:]


def tap_list(taps, axis, way):
    return [taps[axis, k if way == 0 else TAPS - 1 - k] for k in range(TAPS)]


def filter_z(v, z_table):
    hi, lo = split(v)
    both = dot(jnp.concatenate([hi, lo], axis=1), z_table)
    return both[:, :NZ] + both[:, NZ:]


def filter_zx(pair, z_table, x_table):
    v = filter_z(jnp.concatenate(pair, axis=0), z_table)
    hi, lo = split(jnp.concatenate([v[:NX], v[NX:]], axis=1))
    both = dot(x_table, jnp.concatenate([hi, lo, hi], axis=0))
    return both[:, :NZ], both[:, NZ:]


HALF_SHAPES = ((HALF, NX, NZ), (1, NX, NZ))


def store_pair(side, i, pair, outer, inner):
    for m in range(2):
        y = 2 * i + m
        if side == 0:
            ref, at = (inner, 0) if y == HALF else (outer, y)
        else:
            ref, at = (inner, 0) if y == 0 else (outer, y - 1)
        ref[at] = pair[m]


def calls(kernel, name, shapes, scratch=(), cost=None, **more):
    params = pltpu.CompilerParams(vmem_limit_bytes=VMEM_LIMIT)
    if cost:
        more["cost_estimate"] = pl.CostEstimate(flops=cost, bytes_accessed=10**6, transcendentals=0)
    return pl.pallas_call(
        kernel,
        out_shape=[jax.ShapeDtypeStruct(s, F32) for s in shapes],
        scratch_shapes=list(scratch),
        compiler_params=params,
        name=name,
        **more,
    )


WHOLE = pl.BlockSpec(memory_space=pltpu.VMEM)
SCALARS = pl.BlockSpec(memory_space=pltpu.SMEM)


def arrive_kernel(side, got, z_table, x_table, cleaned, outer, inner):
    for i in range(HL // 2):
        for m in range(2):
            for half in range(2):
                row = half * LINES + side * HL + 2 * i + m
                tile = got[pl.ds(row, NZ, stride=2 * LINES), :].T
                cleaned[2 * i + m, half * 128 : (half + 1) * 128, :] = tile
        lines = [cleaned[2 * i], cleaned[2 * i + 1]]
        store_pair(side, i, filter_zx(lines, z_table[...], x_table[...]), outer, inner)


def arrive(side, got, tables):
    return calls(
        functools.partial(arrive_kernel, side),
        f"arrive_{side}",
        ((HL, NX, NZ),) + HALF_SHAPES,
        in_specs=[WHOLE] * 3,
    )(got, *tables)


def own_kernel(way, side, taps, low, low_mid, high_mid, high, out):
    weights = [jnp.full((8, NZ), tap, F32) for tap in tap_list(taps, 2, way)]

    def line(j, at):
        if j < HALF:
            return low[j, at, :]
        if j < LINES - HALF:
            return (low_mid, high_mid)[j - HALF][0, at, :]
        return high[j - (LINES - HALF), at, :]

    @pl.loop(0, NX // 8)
    def _(t):
        at = pl.ds(pl.multiple_of(t * 8, 8), 8)
        for first in range(0, HL, 8):
            base = side * HL + first
            sums = [None] * 8
            for j in range(max(0, base - HALF), min(LINES, base + 8 + HALF)):
                v = line(j, at)
                for m in range(8):
                    k = j - (base + m) + HALF
                    if 0 <= k < TAPS:
                        term = weights[k] * v
                        sums[m] = term if sums[m] is None else sums[m] + term
            for m in range(8):
                out[first + m, at, :] = sums[m]


def own_lines(way, side, taps, halves):
    (low, low_mid), (high, high_mid) = halves
    return calls(
        functools.partial(own_kernel, way, side),
        f"own_lines_{side}",
        ((HL, NX, NZ),),
        cost=4 * 10**9,
        in_specs=[SCALARS] + [WHOLE] * 4,
    )(taps, low, low_mid, high_mid, high)[0]


def add_halo(way, side, taps, meta, partial, halo, at, use):
    weights = [jnp.full((8, NZ), tap, F32) for tap in tap_list(taps, 2, way)]
    there = meta[side] != 0
    for first in range(0, HL, 8):
        sums = [partial[first + m, at, :] for m in range(8)]
        for j in range(HALF):
            ks = [j - (first + m) if side == 0 else 2 * HL - 1 + j - (first + m) for m in range(8)]
            if any(0 <= k < TAPS for k in ks):
                v = jnp.where(there, halo[j, at, :], 0.0)
                for m in range(8):
                    if 0 <= ks[m] < TAPS:
                        sums[m] = sums[m] + weights[ks[m]] * v
        for m in range(8):
            use(first + m, sums[m])


def step_kernel(ratio, side, taps, meta, partial, halo, other, z_table, x_table, *rest):
    if ratio:
        outer, inner, work = rest
    else:
        work, outer, inner = rest

    @pl.loop(0, NX // 8)
    def _(t):
        at = pl.ds(pl.multiple_of(t * 8, 8), 8)

        def use(y, total):
            if ratio:
                work[y, at, :] = other[y, at, :] / (total + BACKGROUND)
            else:
                work[y, at, :] = other[y, at, :] * total

        add_halo(0 if ratio else 1, side, taps, meta, partial, halo, at, use)

    for i in range(HL // 2):
        lines = [work[2 * i], work[2 * i + 1]]
        store_pair(side, i, filter_zx(lines, z_table[...], x_table[...]), outer, inner)


def step(ratio, side, taps, meta, partial, halo, other, tables):
    return calls(
        functools.partial(step_kernel, ratio, side),
        f"ratio_step_{side}" if ratio else f"estimate_step_{side}",
        HALF_SHAPES if ratio else ((HL, NX, NZ),) + HALF_SHAPES,
        [pltpu.VMEM((HL, NX, NZ), F32)] if ratio else [],
        in_specs=[SCALARS] * 2 + [WHOLE] * 5,
    )(taps, meta, partial, halo, other, *tables)


def last_kernel(j, meta, taps, *refs):
    partials, halos, others, out = refs[:2], refs[2:4], refs[4:6], refs[6]

    @pl.loop(0, 4)
    def _(t):
        to = pl.ds(pl.multiple_of(t * 8, 8), 8)
        at = pl.ds(pl.multiple_of(meta[2 + j] * 32 + t * 8, 8), 8)
        for side in range(2):

            def use(y, total):
                out[side * HL + y, to, :] = others[side][y, at, :] * total

            add_halo(1, side, taps, meta, partials[side], halos[side], at, use)


def last(j, taps, meta, partials, halos, others):
    return calls(
        functools.partial(last_kernel, j),
        "last_step",
        ((LINES, 32, NZ),),
        in_specs=[SCALARS] * 2 + [WHOLE] * 6,
    )(meta, taps, *partials, *halos, *others)[0]


def leave_kernel(meta, *refs):
    parts, out, held = refs[:ROUNDS], refs[ROUNDS], refs[ROUNDS + 1]
    rows = LINES * 32
    for j in range(ROUNDS):
        base = meta[2 + ROUNDS + j] * rows

        @pl.loop(0, LINES, unroll=8)
        def _(y):
            held[pl.ds(pl.multiple_of(base + y * 32, 32), 32), :] = parts[j][y]

    @pl.loop(0, CH * 32, unroll=8)
    def _(i):
        start = (i // 32) * (128 * 32) + lax.rem(i, 32)
        tile = held[pl.ds(start, 128, stride=32), :].T
        out[pl.ds(start, 128, stride=32), :] = tile


def leave(meta, parts):
    return calls(
        leave_kernel,
        "leave",
        ((CH * NZ * 32, 128),),
        [pltpu.VMEM((CH * 128 * 32, NZ), F32)],
        in_specs=[SCALARS] + [WHOLE] * ROUNDS,
    )(meta, *parts)[0]


def local(raw_stack, psf_taps):
    me = lax.axis_index("gx") * 8 + lax.axis_index("gy")
    channel = lax.rem(lax.axis_index("gy"), 2)
    meta = lax.dynamic_index_in_dim(jnp.asarray(meta_table()), me, keepdims=False)
    taps = lax.dynamic_index_in_dim(psf_taps, channel, axis=1, keepdims=False)
    taps = taps / jnp.sum(taps, axis=1, keepdims=True)

    blocks = destripe(raw_stack).reshape(128, 64, 128)
    got = lax.all_to_all(blocks, AXES, split_axis=0, concat_axis=0, tiled=True)
    tables = filter_tables(taps)
    got = got.reshape(128 * 64, 128)
    cleaned, halves, halos = [None, None], [None, None], [None, None]

    def exchange(side):
        halos[1 - side] = lax.ppermute(halves[side][0], AXES, DOWN if side == 0 else UP)

    first = 0
    for side in (first, 1 - first):
        cleaned[side], *halves[side] = arrive(side, got, tables[0])
        exchange(side)

    estimate = list(cleaned)
    for blur in range(2 * ITERS):
        way = blur % 2
        first = 1 - first
        partials = [None, None]
        for side in (first, 1 - first):
            partials[side] = own_lines(way, side, taps, halves)
        if blur == 2 * ITERS - 1:
            parts = [last(j, taps, meta, partials, halos, estimate) for j in range(ROUNDS)]
            break
        arrived = list(halos)
        halves = [None, None]
        for side in (first, 1 - first):
            args = (side, taps, meta, partials[side], arrived[side])
            if way == 0:
                halves[side] = step(True, *args, cleaned[side], tables[1])
            else:
                estimate[side], *halves[side] = step(False, *args, estimate[side], tables[0])
            exchange(side)
    parts = [lax.ppermute(part, AXES, FINAL[j]) for j, part in enumerate(parts)]
    return leave(meta, parts).reshape(CH, NZ, 32, 128)


def solution(mesh):
    in_specs = (P(None, AXES, None, None), P())
    out_specs = P(None, None, "gy", "gx")
    return jax.shard_map(local, mesh=mesh, in_specs=in_specs, out_specs=out_specs, check_vma=False)
```

time: 341 us -> 272 us (0.80)
  the two profiles are of different devices: /device:TPU:104 before, /device:TPU:97 now
where the time goes in v2:
time: 272 us
  waiting for transfers between devices  122 us (45%)
  Pallas kernels  118 us (43%)
  starting transfers between devices  30 us (11%)
    all_to_all x1, waiting for transfers between devices, local(): got = lax.all_to_all(blocks, AXES, split_axis=0, concat_axis=0, tiled=True)  47.9 us
    ppermute x8, waiting for transfers between devices, exchange(): lax.ppermute(halves[side][0], AXES, DOWN if side == 0 else UP)  40.5 us
    pallas_call x8, Pallas kernels, own_lines(): calls(functools.partial(own_kernel, way, side), f'own_lines_{side}', ((HL...  39 us
    ppermute x8, waiting for transfers between devices, local(): parts = [lax.ppermute(part, AXES, FINAL[j]) for j, part in enumerate(parts)]  33.6 us
    pallas_call x6, Pallas kernels, step(): calls(functools.partial(step_kernel, ratio, side), f'ratio_step_{side}' i...  29.6 us
    pallas_call x1, Pallas kernels, destripe(): pl.pallas_call(destripe_kernel, grid=(CH,), in_specs=[pl.BlockSpec((1, 1,...  16.7 us
    ppermute x8, starting transfers between devices, local(): parts = [lax.ppermute(part, AXES, FINAL[j]) for j, part in enumerate(parts)]  15.7 us
    pallas_call x2, Pallas kernels, arrive(): calls(functools.partial(arrive_kernel, side), f'arrive_{side}', ((HL, NX,...  13.4 us
  transfers between devices with their start and end apart: 17, of which 13 were waited for; matrix products, arithmetic and copies ran while one was open for 0% of the time, Pallas kernels for 31%

profile of v2, /device:TPU:97, one launch (start us, length us, event | category | flops | bytes accessed | tf_op | source)
XLA Modules:
  0.0 272.0 jit_solution(14757134687327951547)
XLA Ops:
  0.0 16.7 %destripe.1 = f32[16,4,2,64,128]{4,3,2,1,0:T(8,128)} custom-call(f32[2,1,256,2048]{3,2,1,0:T(8,128)} %raw.1, bf16[256,256]{1,0:T(8,128)(2,1)} %constant.47.clone.ah, bf16[256,256]{1,0:T(8,128)(2,1)} %constant.48.clone.al, bf16[1024,1024]{1,0:T(8,128)(2,1)} %constant.49.clone.oh, bf16[1024,1024]{1,0:T(8,128)(2,1)} %constant.50.clone.ol, ...), custom_call_target="tpu_custom_call" | custom-call | tf_op jit(solution)/shard_map/destripe/pallas_call | solution.py:167
  16.7 10.6 %all-to-all-start = ((f32[128,64,128]{2,1,0:T(8,128)}), f32[128,64,128]{2,1,0:T(8,128)}, u32[]{:S(2)}, u32[]{:S(2)}) async-start(f32[128,64,128]{2,1,0:T(8,128)} %bitcast.7), calls=%async_computation | async-start | bytes 8388608 | tf_op jit(solution)/shard_map/all_to_all | solution.py:435
  27.5 1.4 tables.1
  29.0 47.9 %all-to-all-done = f32[128,64,128]{2,1,0:T(8,128)} async-done(((f32[128,64,128]{2,1,0:T(8,128)}), f32[128,64,128]{2,1,0:T(8,128)}, u32[]{:S(2)}, u32[]{:S(2)}) %all-to-all-start) | async-done | bytes 4194336 | tf_op jit(solution)/shard_map/all_to_all | solution.py:435
  76.9 6.7 %arrive_0.1 = (f32[16,256,128]{2,1,0:T(8,128)S(1)}, f32[15,256,128]{2,1,0:T(8,128)}, f32[1,256,128]{2,1,0:T(8,128)S(1)}) custom-call(f32[8192,128]{1,0:T(8,128)} %bitcast.2.got, bf16[256,256]{1,0:T(8,128)(2,1)S(1)} %get-tuple-element.29.z_table, bf16[256,768]{1,0:T(8,128)(2,1)S(1)} %get-tuple-element.30.x_table), custom_call_target="tpu_custom_call" | custom-call | tf_op jit(solution)/shard_map/arrive_0/pallas_call | solution.py:281
  83.7 6.7 %arrive_1.1 = (f32[16,256,128]{2,1,0:T(8,128)S(1)}, f32[15,256,128]{2,1,0:T(8,128)}, f32[1,256,128]{2,1,0:T(8,128)S(1)}) custom-call(f32[8192,128]{1,0:T(8,128)} %bitcast.2.got, bf16[256,256]{1,0:T(8,128)(2,1)S(1)} %get-tuple-element.29.z_table, bf16[256,768]{1,0:T(8,128)(2,1)S(1)} %get-tuple-element.30.x_table), custom_call_target="tpu_custom_call" | custom-call | tf_op jit(solution)/shard_map/arrive_1/pallas_call | solution.py:281
  90.4 1.3 copy-done
  91.7 2.8 %collective-permute-start = (f32[15,256,128]{2,1,0:T(8,128)}, f32[15,256,128]{2,1,0:T(8,128)}, u32[]{:S(2)}, u32[]{:S(2)}) collective-permute-start(f32[15,256,128]{2,1,0:T(8,128)} %get-tuple-element.34.high), channel_id=1, source_target_pairs={{0,8},{8,2},{2,10},{10,4},{4,12},{12,6},{6,14},{14,22},{22,30},{30... | collective-permute-start | bytes 5898248 | tf_op jit(solution)/shard_map/ppermute | solution.py:441
  94.6 0.7 dynamic-slice_bitcast_fusion.meta
  95.3 6.1 %own_lines_1.4.partial = f32[16,256,128]{2,1,0:T(8,128)S(1)} custom-call(f32[3,31]{1,0:T(4,128)S(1)} %bitcast_divide_fusion.taps, f32[15,256,128]{2,1,0:T(8,128)} %get-tuple-element.31.low, f32[1,256,128]{2,1,0:T(8,128)S(1)} %get-tuple-element.32.low_mid, f32[1,256,128]{2,1,0:T(8,128)S(1)} %get-tuple-element.33.high_mid, f32[15,256,128]{2,1,0:T(8,128)} %get-tuple-element.34.high), custom_call_target="tpu_custom_call" | custom-call | flops 4000000000 | bytes 1000000 | tf_op jit(solution)/shard_map/own_lines_1/pallas_call | solution.py:318
  101.4 6.1 %own_lines_0.4.partial = f32[16,256,128]{2,1,0:T(8,128)S(1)} custom-call(f32[3,31]{1,0:T(4,128)S(1)} %bitcast_divide_fusion.taps, f32[15,256,128]{2,1,0:T(8,128)} %get-tuple-element.31.low, f32[1,256,128]{2,1,0:T(8,128)S(1)} %get-tuple-element.32.low_mid, f32[1,256,128]{2,1,0:T(8,128)S(1)} %get-tuple-element.33.high_mid, f32[15,256,128]{2,1,0:T(8,128)} %get-tuple-element.34.high), custom_call_target="tpu_custom_call" | custom-call | flops 4000000000 | bytes 1000000 | tf_op jit(solution)/shard_map/own_lines_0/pallas_call | solution.py:318
  107.5 1.7 collective-permute-done.1.halo
  109.2 5.8 %ratio_step_1.2 = (f32[15,256,128]{2,1,0:T(8,128)S(1)}, f32[1,256,128]{2,1,0:T(8,128)S(1)}) custom-call(f32[3,31]{1,0:T(4,128)S(1)} %bitcast_divide_fusion.taps, s32[18]{0:T(128)S(1)} %dynamic-slice_bitcast_fusion.meta, f32[16,256,128]{2,1,0:T(8,128)S(1)} %own_lines_1.4.partial, f32[15,256,128]{2,1,0:T(8,128)} %collective-permute-done.1.halo, ...), custom_call_target="tpu_custom_call" | custom-call | tf_op jit(solution)/shard_map/ratio_step_1/pallas_call | solution.py:367
  115.0 1.4 collective-permute-done.halo
  116.5 5.6 %ratio_step_0.2 = (f32[15,256,128]{2,1,0:T(8,128)S(1)}, f32[1,256,128]{2,1,0:T(8,128)S(1)}) custom-call(f32[3,31]{1,0:T(4,128)S(1)} %bitcast_divide_fusion.taps, s32[18]{0:T(128)S(1)} %dynamic-slice_bitcast_fusion.meta, f32[16,256,128]{2,1,0:T(8,128)S(1)} %own_lines_0.4.partial, f32[15,256,128]{2,1,0:T(8,128)} %collective-permute-done.halo, ...), custom_call_target="tpu_custom_call" | custom-call | tf_op jit(solution)/shard_map/ratio_step_0/pallas_call | solution.py:367
  122.2 4.5 %own_lines_1.5.partial = f32[16,256,128]{2,1,0:T(8,128)S(1)} custom-call(f32[3,31]{1,0:T(4,128)S(1)} %bitcast_divide_fusion.taps, f32[15,256,128]{2,1,0:T(8,128)S(1)} %get-tuple-element.38.low, f32[1,256,128]{2,1,0:T(8,128)S(1)} %get-tuple-element.39.low_mid, f32[1,256,128]{2,1,0:T(8,128)S(1)} %get-tuple-element.41.high_mid, ...), custom_call_target="tpu_custom_call" | custom-call | flops 4000000000 | bytes 1000000 | tf_op jit(solution)/shard_map/own_lines_1/pallas_call | solution.py:318
  126.7 4.4 %own_lines_0.5.partial = f32[16,256,128]{2,1,0:T(8,128)S(1)} custom-call(f32[3,31]{1,0:T(4,128)S(1)} %bitcast_divide_fusion.taps, f32[15,256,128]{2,1,0:T(8,128)S(1)} %get-tuple-element.38.low, f32[1,256,128]{2,1,0:T(8,128)S(1)} %get-tuple-element.39.low_mid, f32[1,256,128]{2,1,0:T(8,128)S(1)} %get-tuple-element.41.high_mid, ...), custom_call_target="tpu_custom_call" | custom-call | flops 4000000000 | bytes 1000000 | tf_op jit(solution)/shard_map/own_lines_0/pallas_call | solution.py:318
  131.1 6.3 %collective-permute-done.2.halo = f32[15,256,128]{2,1,0:T(8,128)S(1)} collective-permute-done((f32[15,256,128]{2,1,0:T(8,128)S(1)}, f32[15,256,128]{2,1,0:T(8,128)S(1)}, u32[]{:S(2)}, u32[]{:S(2)}) %collective-permute-start.2) | collective-permute-done | bytes 1966112 | tf_op jit(solution)/shard_map/ppermute | solution.py:441
  137.4 4.4 %estimate_step_0.1 = (f32[16,256,128]{2,1,0:T(8,128)S(1)}, f32[15,256,128]{2,1,0:T(8,128)S(1)}, f32[1,256,128]{2,1,0:T(8,128)S(1)}) custom-call(f32[3,31]{1,0:T(4,128)S(1)} %bitcast_divide_fusion.taps, s32[18]{0:T(128)S(1)} %dynamic-slice_bitcast_fusion.meta, f32[16,256,128]{2,1,0:T(8,128)S(1)} %own_lines_0.5.partial, ...), custom_call_target="tpu_custom_call" | custom-call | tf_op jit(solution)/shard_map/estimate_step_0/pallas_call | solution.py:367
  141.9 6.3 %collective-permute-done.3.halo = f32[15,256,128]{2,1,0:T(8,128)S(1)} collective-permute-done((f32[15,256,128]{2,1,0:T(8,128)S(1)}, f32[15,256,128]{2,1,0:T(8,128)S(1)}, u32[]{:S(2)}, u32[]{:S(2)}) %collective-permute-start.3) | collective-permute-done | bytes 1966112 | tf_op jit(solution)/shard_map/ppermute | solution.py:441
  148.1 4.5 %estimate_step_1.1 = (f32[16,256,128]{2,1,0:T(8,128)S(1)}, f32[15,256,128]{2,1,0:T(8,128)S(1)}, f32[1,256,128]{2,1,0:T(8,128)S(1)}) custom-call(f32[3,31]{1,0:T(4,128)S(1)} %bitcast_divide_fusion.taps, s32[18]{0:T(128)S(1)} %dynamic-slice_bitcast_fusion.meta, f32[16,256,128]{2,1,0:T(8,128)S(1)} %own_lines_1.5.partial, ...), custom_call_target="tpu_custom_call" | custom-call | tf_op jit(solution)/shard_map/estimate_step_1/pallas_call | solution.py:367
  152.9 4.5 %own_lines_1.6.partial = f32[16,256,128]{2,1,0:T(8,128)S(1)} custom-call(f32[3,31]{1,0:T(4,128)S(1)} %bitcast_divide_fusion.taps, f32[15,256,128]{2,1,0:T(8,128)S(1)} %get-tuple-element.43.low, f32[1,256,128]{2,1,0:T(8,128)S(1)} %get-tuple-element.44.low_mid, f32[1,256,128]{2,1,0:T(8,128)S(1)} %get-tuple-element.45.high_mid, ...), custom_call_target="tpu_custom_call" | custom-call | flops 4000000000 | bytes 1000000 | tf_op jit(solution)/shard_map/own_lines_1/pallas_call | solution.py:318
  157.5 4.4 %own_lines_0.6.partial = f32[16,256,128]{2,1,0:T(8,128)S(1)} custom-call(f32[3,31]{1,0:T(4,128)S(1)} %bitcast_divide_fusion.taps, f32[15,256,128]{2,1,0:T(8,128)S(1)} %get-tuple-element.43.low, f32[1,256,128]{2,1,0:T(8,128)S(1)} %get-tuple-element.44.low_mid, f32[1,256,128]{2,1,0:T(8,128)S(1)} %get-tuple-element.45.high_mid, ...), custom_call_target="tpu_custom_call" | custom-call | flops 4000000000 | bytes 1000000 | tf_op jit(solution)/shard_map/own_lines_0/pallas_call | solution.py:318
  161.9 7.3 %collective-permute-done.5.halo = f32[15,256,128]{2,1,0:T(8,128)S(1)} collective-permute-done((f32[15,256,128]{2,1,0:T(8,128)S(1)}, f32[15,256,128]{2,1,0:T(8,128)S(1)}, u32[]{:S(2)}, u32[]{:S(2)}) %collective-permute-start.5) | collective-permute-done | bytes 1966112 | tf_op jit(solution)/shard_map/ppermute | solution.py:441
  169.2 4.8 %ratio_step_1.3 = (f32[15,256,128]{2,1,0:T(8,128)S(1)}, f32[1,256,128]{2,1,0:T(8,128)S(1)}) custom-call(f32[3,31]{1,0:T(4,128)S(1)} %bitcast_divide_fusion.taps, s32[18]{0:T(128)S(1)} %dynamic-slice_bitcast_fusion.meta, f32[16,256,128]{2,1,0:T(8,128)S(1)} %own_lines_1.6.partial, f32[15,256,128]{2,1,0:T(8,128)S(1)} %collective-permute-done.5.halo, ...), custom_call_target="tpu_custom_call" | custom-call | tf_op jit(solution)/shard_map/ratio_step_1/pallas_call | solution.py:367
  174.1 0.4 collective-permute-done.4.halo
  174.5 4.6 %ratio_step_0.3 = (f32[15,256,128]{2,1,0:T(8,128)S(1)}, f32[1,256,128]{2,1,0:T(8,128)S(1)}) custom-call(f32[3,31]{1,0:T(4,128)S(1)} %bitcast_divide_fusion.taps, s32[18]{0:T(128)S(1)} %dynamic-slice_bitcast_fusion.meta, f32[16,256,128]{2,1,0:T(8,128)S(1)} %own_lines_0.6.partial, f32[15,256,128]{2,1,0:T(8,128)S(1)} %collective-permute-done.4.halo, ...), custom_call_target="tpu_custom_call" | custom-call | tf_op jit(solution)/shard_map/ratio_step_0/pallas_call | solution.py:367
  179.3 4.5 %own_lines_1.7.refs_1_ = f32[16,256,128]{2,1,0:T(8,128)S(1)} custom-call(f32[3,31]{1,0:T(4,128)S(1)} %bitcast_divide_fusion.taps, f32[15,256,128]{2,1,0:T(8,128)S(1)} %get-tuple-element.47.low, f32[1,256,128]{2,1,0:T(8,128)S(1)} %get-tuple-element.48.low_mid, f32[1,256,128]{2,1,0:T(8,128)S(1)} %get-tuple-element.49.high_mid, ...), custom_call_target="tpu_custom_call" | custom-call | flops 4000000000 | bytes 1000000 | tf_op jit(solution)/shard_map/own_lines_1/pallas_call | solution.py:318
  183.8 4.4 %own_lines_0.7.refs_0_ = f32[16,256,128]{2,1,0:T(8,128)S(1)} custom-call(f32[3,31]{1,0:T(4,128)S(1)} %bitcast_divide_fusion.taps, f32[15,256,128]{2,1,0:T(8,128)S(1)} %get-tuple-element.47.low, f32[1,256,128]{2,1,0:T(8,128)S(1)} %get-tuple-element.48.low_mid, f32[1,256,128]{2,1,0:T(8,128)S(1)} %get-tuple-element.49.high_mid, ...), custom_call_target="tpu_custom_call" | custom-call | flops 4000000000 | bytes 1000000 | tf_op jit(solution)/shard_map/own_lines_0/pallas_call | solution.py:318
  188.2 7.4 %collective-permute-done.6.refs_2_ = f32[15,256,128]{2,1,0:T(8,128)S(1)} collective-permute-done((f32[15,256,128]{2,1,0:T(8,128)S(1)}, f32[15,256,128]{2,1,0:T(8,128)S(1)}, u32[]{:S(2)}, u32[]{:S(2)}) %collective-permute-start.6) | collective-permute-done | bytes 1966112 | tf_op jit(solution)/shard_map/ppermute | solution.py:441
  195.7 9.6 %collective-permute-done.7.refs_3_ = f32[15,256,128]{2,1,0:T(8,128)S(1)} collective-permute-done((f32[15,256,128]{2,1,0:T(8,128)S(1)}, f32[15,256,128]{2,1,0:T(8,128)S(1)}, u32[]{:S(2)}, u32[]{:S(2)}) %collective-permute-start.7) | collective-permute-done | bytes 1966112 | tf_op jit(solution)/shard_map/ppermute | solution.py:441
  205.2 0.9 last_step.15
  206.3 0.9 last_step.14
  207.3 0.9 last_step.13
  208.3 1.9 collective-permute-start.13
  210.2 0.9 last_step.12
  211.1 5.7 %collective-permute-start.12 = (f32[32,32,128]{2,1,0:T(8,128)S(1)}, f32[32,32,128]{2,1,0:T(8,128)S(1)}, u32[]{:S(2)}, u32[]{:S(2)}) collective-permute-start(f32[32,32,128]{2,1,0:T(8,128)S(1)} %last_step.12), channel_id=1, source_target_pairs={{0,4},{8,1},{2,6},{10,3},{4,8},{12,13},{6,10},{14,15},{22,18},{30,... | collective-permute-start | bytes 1572872 | tf_op jit(solution)/shard_map/ppermute | solution.py:467
  216.9 0.9 last_step.11
  217.9 0.9 last_step.10
  218.9 0.9 last_step.9
  219.8 0.9 last_step.8
  220.8 0.4 collective-permute-start.10
  221.2 20.0 %collective-permute-done.14.refs_6_ = f32[32,32,128]{2,1,0:T(8,128)S(1)} collective-permute-done((f32[32,32,128]{2,1,0:T(8,128)S(1)}, f32[32,32,128]{2,1,0:T(8,128)S(1)}, u32[]{:S(2)}, u32[]{:S(2)}) %collective-permute-start.14) | collective-permute-done | bytes 524320 | tf_op jit(solution)/shard_map/ppermute | solution.py:467
  241.2 7.4 %collective-permute-start.8 = (f32[32,32,128]{2,1,0:T(8,128)S(1)}, f32[32,32,128]{2,1,0:T(8,128)S(1)}, u32[]{:S(2)}, u32[]{:S(2)}) collective-permute-start(f32[32,32,128]{2,1,0:T(8,128)S(1)} %last_step.8), channel_id=1, source_target_pairs={{0,0},{8,5},{2,2},{10,7},{4,12},{12,9},{6,14},{14,11},{22,22},{30,... | collective-permute-start | bytes 1572872 | tf_op jit(solution)/shard_map/ppermute | solution.py:467
  248.6 1.7 collective-permute-done.10.refs_2_
  250.2 5.1 %collective-permute-done.9.refs_1_ = f32[32,32,128]{2,1,0:T(8,128)S(1)} collective-permute-done((f32[32,32,128]{2,1,0:T(8,128)S(1)}, f32[32,32,128]{2,1,0:T(8,128)S(1)}, u32[]{:S(2)}, u32[]{:S(2)}) %collective-permute-start.9) | collective-permute-done | bytes 524320 | tf_op jit(solution)/shard_map/ppermute | solution.py:467
  255.3 6.8 %collective-permute-done.8.refs_0_ = f32[32,32,128]{2,1,0:T(8,128)S(1)} collective-permute-done((f32[32,32,128]{2,1,0:T(8,128)S(1)}, f32[32,32,128]{2,1,0:T(8,128)S(1)}, u32[]{:S(2)}, u32[]{:S(2)}) %collective-permute-start.8) | collective-permute-done | bytes 524320 | tf_op jit(solution)/shard_map/ppermute | solution.py:467
  262.1 9.9 %leave.1 = f32[8192,128]{1,0:T(8,128)} custom-call(s32[18]{0:T(128)S(1)} %dynamic-slice_bitcast_fusion.meta, f32[32,32,128]{2,1,0:T(8,128)S(1)} %collective-permute-done.8.refs_0_, f32[32,32,128]{2,1,0:T(8,128)S(1)} %collective-permute-done.9.refs_1_, f32[32,32,128]{2,1,0:T(8,128)S(1)} %collective-permute-done.10.refs_2_, ...), custom_call_target="tpu_custom_call" | custom-call | tf_op jit(solution)/shard_map/leave/pallas_call | solution.py:418
  (22 shorter events, 1.3 us)
Async XLA Ops:
  16.7 10.7 %copy-start.2 = (f32[3,2,31]{2,1,0:T(2,128)S(1)}, f32[3,2,31]{2,1,0:T(2,128)}, u32[]{:S(2)}) copy-start(f32[3,2,31]{2,1,0:T(2,128)} %param.12) | copy-start | bytes 2236
  16.7 60.2 %all-to-all-start = ((f32[128,64,128]{2,1,0:T(8,128)}), f32[128,64,128]{2,1,0:T(8,128)}, u32[]{:S(2)}, u32[]{:S(2)}) async-start(f32[128,64,128]{2,1,0:T(8,128)} %bitcast.7), calls=%async_computation | async-start | bytes 8388608 | tf_op jit(solution)/shard_map/all_to_all | solution.py:435
  83.6 25.6 %collective-permute-start.1 = (f32[15,256,128]{2,1,0:T(8,128)}, f32[15,256,128]{2,1,0:T(8,128)}, u32[]{:S(2)}, u32[]{:S(2)}) collective-permute-start(f32[15,256,128]{2,1,0:T(8,128)} %get-tuple-element.31.low), channel_id=1, source_target_pairs={{8,0},{2,8},{10,2},{4,10},{12,4},{6,12},{14,6},{22,14},{30,22},{20... | collective-permute-start | bytes 5898248 | tf_op jit(solution)/shard_map/ppermute | solution.py:441
  90.4 1.3 copy-start
  91.7 24.7 %collective-permute-start = (f32[15,256,128]{2,1,0:T(8,128)}, f32[15,256,128]{2,1,0:T(8,128)}, u32[]{:S(2)}, u32[]{:S(2)}) collective-permute-start(f32[15,256,128]{2,1,0:T(8,128)} %get-tuple-element.34.high), channel_id=1, source_target_pairs={{0,8},{8,2},{2,10},{10,4},{4,12},{12,6},{6,14},{14,22},{22,30},{30... | collective-permute-start | bytes 5898248 | tf_op jit(solution)/shard_map/ppermute | solution.py:441
  101.3 7.8 %copy-start.1 = (f32[16,256,128]{2,1,0:T(8,128)S(1)}, f32[16,256,128]{2,1,0:T(8,128)}, u32[]{:S(2)}) copy-start(f32[16,256,128]{2,1,0:T(8,128)} %copy-done) | copy-start | bytes 6291460
  114.9 22.5 %collective-permute-start.2 = (f32[15,256,128]{2,1,0:T(8,128)S(1)}, f32[15,256,128]{2,1,0:T(8,128)S(1)}, u32[]{:S(2)}, u32[]{:S(2)}) collective-permute-start(f32[15,256,128]{2,1,0:T(8,128)S(1)} %get-tuple-element.42.high), channel_id=1, source_target_pairs={{0,8},{8,2},{2,10},{10,4},{4,12},{12,6},{6,14},{14,22},{22,30},{30... | collective-permute-start | bytes 5898248 | tf_op jit(solution)/shard_map/ppermute | solution.py:441
  122.1 26.1 %collective-permute-start.3 = (f32[15,256,128]{2,1,0:T(8,128)S(1)}, f32[15,256,128]{2,1,0:T(8,128)S(1)}, u32[]{:S(2)}, u32[]{:S(2)}) collective-permute-start(f32[15,256,128]{2,1,0:T(8,128)S(1)} %get-tuple-element.38.low), channel_id=1, source_target_pairs={{8,0},{2,8},{10,2},{4,10},{12,4},{6,12},{14,6},{22,14},{30,22},{20... | collective-permute-start | bytes 5898248 | tf_op jit(solution)/shard_map/ppermute | solution.py:441
  141.8 27.4 %collective-permute-start.5 = (f32[15,256,128]{2,1,0:T(8,128)S(1)}, f32[15,256,128]{2,1,0:T(8,128)S(1)}, u32[]{:S(2)}, u32[]{:S(2)}) collective-permute-start(f32[15,256,128]{2,1,0:T(8,128)S(1)} %get-tuple-element.43.low), channel_id=1, source_target_pairs={{8,0},{2,8},{10,2},{4,10},{12,4},{6,12},{14,6},{22,14},{30,22},{20... | collective-permute-start | bytes 5898248 | tf_op jit(solution)/shard_map/ppermute | solution.py:441
  152.6 21.9 %collective-permute-start.4 = (f32[15,256,128]{2,1,0:T(8,128)S(1)}, f32[15,256,128]{2,1,0:T(8,128)S(1)}, u32[]{:S(2)}, u32[]{:S(2)}) collective-permute-start(f32[15,256,128]{2,1,0:T(8,128)S(1)} %get-tuple-element.46.high), channel_id=1, source_target_pairs={{0,8},{8,2},{2,10},{10,4},{4,12},{12,6},{6,14},{14,22},{22,30},{30... | collective-permute-start | bytes 5898248 | tf_op jit(solution)/shard_map/ppermute | solution.py:441
  174.0 21.6 %collective-permute-start.6 = (f32[15,256,128]{2,1,0:T(8,128)S(1)}, f32[15,256,128]{2,1,0:T(8,128)S(1)}, u32[]{:S(2)}, u32[]{:S(2)}) collective-permute-start(f32[15,256,128]{2,1,0:T(8,128)S(1)} %get-tuple-element.50.high), channel_id=1, source_target_pairs={{0,8},{8,2},{2,10},{10,4},{4,12},{12,6},{6,14},{14,22},{22,30},{30... | collective-permute-start | bytes 5898248 | tf_op jit(solution)/shard_map/ppermute | solution.py:441
  179.1 26.1 %collective-permute-start.7 = (f32[15,256,128]{2,1,0:T(8,128)S(1)}, f32[15,256,128]{2,1,0:T(8,128)S(1)}, u32[]{:S(2)}, u32[]{:S(2)}) collective-permute-start(f32[15,256,128]{2,1,0:T(8,128)S(1)} %get-tuple-element.47.low), channel_id=1, source_target_pairs={{8,0},{2,8},{10,2},{4,10},{12,4},{6,12},{14,6},{22,14},{30,22},{20... | collective-permute-start | bytes 5898248 | tf_op jit(solution)/shard_map/ppermute | solution.py:441
  206.2 14.6 %collective-permute-start.15 = (f32[32,32,128]{2,1,0:T(8,128)S(1)}, f32[32,32,128]{2,1,0:T(8,128)S(1)}, u32[]{:S(2)}, u32[]{:S(2)}) collective-permute-start(f32[32,32,128]{2,1,0:T(8,128)S(1)} %last_step.15), channel_id=1, source_target_pairs={{0,7},{8,2},{2,1},{10,4},{4,11},{12,14},{6,13},{14,8},{22,21},{30,... | collective-permute-start | bytes 1572872 | tf_op jit(solution)/shard_map/ppermute | solution.py:467
  207.2 34.0 %collective-permute-start.14 = (f32[32,32,128]{2,1,0:T(8,128)S(1)}, f32[32,32,128]{2,1,0:T(8,128)S(1)}, u32[]{:S(2)}, u32[]{:S(2)}) collective-permute-start(f32[32,32,128]{2,1,0:T(8,128)S(1)} %last_step.14), channel_id=1, source_target_pairs={{0,6},{8,3},{2,0},{10,5},{4,10},{12,15},{6,12},{14,9},{22,20},{30,... | collective-permute-start | bytes 1572872 | tf_op jit(solution)/shard_map/ppermute | solution.py:467
  208.3 32.9 %collective-permute-start.13 = (f32[32,32,128]{2,1,0:T(8,128)S(1)}, f32[32,32,128]{2,1,0:T(8,128)S(1)}, u32[]{:S(2)}, u32[]{:S(2)}) collective-permute-start(f32[32,32,128]{2,1,0:T(8,128)S(1)} %last_step.13), channel_id=1, source_target_pairs={{0,5},{8,0},{2,7},{10,2},{4,9},{12,12},{6,11},{14,14},{22,19},{30,... | collective-permute-start | bytes 1572872 | tf_op jit(solution)/shard_map/ppermute | solution.py:467
  211.1 37.4 %collective-permute-start.12 = (f32[32,32,128]{2,1,0:T(8,128)S(1)}, f32[32,32,128]{2,1,0:T(8,128)S(1)}, u32[]{:S(2)}, u32[]{:S(2)}) collective-permute-start(f32[32,32,128]{2,1,0:T(8,128)S(1)} %last_step.12), channel_id=1, source_target_pairs={{0,4},{8,1},{2,6},{10,3},{4,8},{12,13},{6,10},{14,15},{22,18},{30,... | collective-permute-start | bytes 1572872 | tf_op jit(solution)/shard_map/ppermute | solution.py:467
  217.8 30.7 %collective-permute-start.11 = (f32[32,32,128]{2,1,0:T(8,128)S(1)}, f32[32,32,128]{2,1,0:T(8,128)S(1)}, u32[]{:S(2)}, u32[]{:S(2)}) collective-permute-start(f32[32,32,128]{2,1,0:T(8,128)S(1)} %last_step.11), channel_id=1, source_target_pairs={{0,3},{8,6},{2,5},{10,0},{4,15},{12,10},{6,9},{14,12},{22,17},{30,... | collective-permute-start | bytes 1572872 | tf_op jit(solution)/shard_map/ppermute | solution.py:467
  220.8 29.5 %collective-permute-start.10 = (f32[32,32,128]{2,1,0:T(8,128)S(1)}, f32[32,32,128]{2,1,0:T(8,128)S(1)}, u32[]{:S(2)}, u32[]{:S(2)}) collective-permute-start(f32[32,32,128]{2,1,0:T(8,128)S(1)} %last_step.10), channel_id=1, source_target_pairs={{0,2},{8,7},{2,4},{10,1},{4,14},{12,11},{6,8},{14,13},{22,16},{30,... | collective-permute-start | bytes 1572872 | tf_op jit(solution)/shard_map/ppermute | solution.py:467
  241.2 14.2 %collective-permute-start.9 = (f32[32,32,128]{2,1,0:T(8,128)S(1)}, f32[32,32,128]{2,1,0:T(8,128)S(1)}, u32[]{:S(2)}, u32[]{:S(2)}) collective-permute-start(f32[32,32,128]{2,1,0:T(8,128)S(1)} %last_step.9), channel_id=1, source_target_pairs={{0,1},{8,4},{2,3},{10,6},{4,13},{12,8},{6,15},{14,10},{22,23},{30,... | collective-permute-start | bytes 1572872 | tf_op jit(solution)/shard_map/ppermute | solution.py:467
  241.2 21.0 %collective-permute-start.8 = (f32[32,32,128]{2,1,0:T(8,128)S(1)}, f32[32,32,128]{2,1,0:T(8,128)S(1)}, u32[]{:S(2)}, u32[]{:S(2)}) collective-permute-start(f32[32,32,128]{2,1,0:T(8,128)S(1)} %last_step.8), channel_id=1, source_target_pairs={{0,0},{8,5},{2,2},{10,7},{4,12},{12,9},{6,14},{14,11},{22,22},{30,... | collective-permute-start | bytes 1572872 | tf_op jit(solution)/shard_map/ppermute | solution.py:467

commit v3 on v2

--- a/solution.py
+++ b/solution.py
@@ -19,7 +19,7 @@
 BLOCKS = NY // LINES
 AXES = ("gx", "gy")
 F32, BF16 = jnp.float32, jnp.bfloat16
-VMEM_LIMIT = 24 * 1024 * 1024
+VMEM_LIMIT = 16 * 1024 * 1024
 HL = LINES // 2
 
 
@@ -46,8 +46,8 @@
 
 def final_target(channel, block, j):
     x, _, _, core = place(block)
-    xd = (x + 2 * core + (j >> 1)) % 4
-    x8 = 2 * xd + (channel ^ (j & 1) ^ core)
+    xd = (x + 2 * core + (j & 3)) % 4
+    x8 = 2 * xd + (channel ^ (j >> 2) ^ ((block >> 2) & 1))
     return x8, (block >> 2) * 8 + x8
 
 
@@ -58,7 +58,7 @@
 
 
 def meta_table():
-    meta = np.zeros((128, 2 + 2 * ROUNDS), np.int32)
+    meta = np.zeros((128, 4 + 2 * ROUNDS), np.int32)
     for c in range(CH):
         for b in range(BLOCKS):
             me = device_of(c, b)
@@ -67,7 +67,8 @@
             for j in range(ROUNDS):
                 x8, target = final_target(c, b, j)
                 meta[me, 2 + j] = x8
-                meta[target, 2 + ROUNDS + j] = c * 4 + (b & 3)
+                meta[target, 2 + ROUNDS + j] = b & 3
+                meta[target, 2 + 2 * ROUNDS + (j >> 2)] = c
     return meta
 
 
@@ -91,10 +92,8 @@
     odd = along[:h, :h] - along[:h, h:]
     even_even = even[:q, :q] + even[:q, q:]
     even_odd = even[:q, :q] - even[:q, q:]
-    out = []
-    for table in (across.T, odd, even_even, even_odd):
-        out.extend(np_split(table))
-    return out
+    ah, al = np_split(across.T)
+    return ah, al, np.stack(np_split(odd)), np.stack(np_split(even_even) + np_split(even_odd))
 
 
 def split(v):
@@ -110,10 +109,19 @@
     return dot(a_high, b_high) + (dot(a_high, b_low) + dot(a_low, b_high))
 
 
-def destripe_kernel(raw, ah, al, oh, ol, eeh, eel, eoh, eol, out, rt, sm, dh, dl, s1h, s1l, d1h, d1l):
+def destripe_kernel(raw, ah, al, odd_in, even_in, out, rt, sm, dh, dl, s1h, s1l, d1h, d1l, odd, even, sems):
     h, q = NY // 2, NY // 4
-
-    @pl.loop(0, NY // 256)
+    copies = [
+        pltpu.make_async_copy(odd_in, odd, sems.at[0]),
+        pltpu.make_async_copy(even_in, even, sems.at[1]),
+    ]
+
+    @pl.when(pl.program_id(0) == 0)
+    def _():
+        for copy in copies:
+            copy.start()
+
+    @pl.loop(0, NY // 256, unroll=4)
     def _(i):
         r = pl.multiple_of(i * 256, 256)
         tile = raw[0, 0, :, pl.ds(r, 256)].T
@@ -138,6 +146,11 @@
         d1h[pl.ds(r, 128), :] = hi
         d1l[pl.ds(r, 128), :] = lo
 
+    @pl.when(pl.program_id(0) == 0)
+    def _():
+        for copy in copies:
+            copy.wait()
+
     def emit(row, smooth):
         for m in range(8):
             x, yl, z, core = place(row // LINES + m)
@@ -145,29 +158,32 @@
             part = smooth[m * LINES : (m + 1) * LINES, :]
             clean = jnp.maximum(rt[at, :] - (sm[at, :] - part), 0.0)
             gx = (z * 2 + yl) * 2 + core
-            out[gx, x, 0, 0:LINES, :] = clean[:, :128]
-            out[gx, x, 0, LINES : 2 * LINES, :] = clean[:, 128:]
+            for side in range(2):
+                for half in range(2):
+                    to = (2 * side + half) * HL
+                    tile = clean[side * HL : (side + 1) * HL, half * 128 : (half + 1) * 128]
+                    out[gx, x, 0, to : to + HL, :] = tile
 
     for i in range(2):
         at = slice(i * 256, (i + 1) * 256)
-        ee = dot3(eeh[at, :], eel[at, :], s1h[...], s1l[...])
-        eo = dot3(eoh[at, :], eol[at, :], d1h[...], d1l[...])
+        ee = dot3(even[0, at, :], even[1, at, :], s1h[...], s1l[...])
+        eo = dot3(even[2, at, :], even[3, at, :], d1h[...], d1l[...])
         for m in range(2):
             row = m * q + i * 256
-            even = ee + eo if m == 0 else ee - eo
             rows = slice(row, row + 256)
-            odd = dot3(oh[rows, :], ol[rows, :], dh[...], dl[...])
-            emit(row, even + odd)
-            emit(h + row, even - odd)
+            smooth_even = ee + eo if m == 0 else ee - eo
+            smooth_odd = dot3(odd[0, rows, :], odd[1, rows, :], dh[...], dl[...])
+            emit(row, smooth_even + smooth_odd)
+            emit(h + row, smooth_even - smooth_odd)
 
 
 def destripe(raw_stack):
     tables = [jnp.asarray(t) for t in destripe_tables()]
-    whole = pl.BlockSpec(memory_space=pltpu.VMEM)
+    whole, anywhere = (pl.BlockSpec(memory_space=m) for m in (pltpu.VMEM, pl.ANY))
     return pl.pallas_call(
         destripe_kernel,
         grid=(CH,),
-        in_specs=[pl.BlockSpec((1, 1, NX, NY), lambda c: (c, 0, 0, 0))] + [whole] * 8,
+        in_specs=[pl.BlockSpec((1, 1, NX, NY), lambda c: (c, 0, 0, 0)), whole, whole, anywhere, anywhere],
         out_specs=pl.BlockSpec((16, 4, 1, 64, 128), lambda c: (0, 0, c, 0, 0)),
         out_shape=jax.ShapeDtypeStruct((16, 4, CH, 64, 128), F32),
         scratch_shapes=[
@@ -176,7 +192,12 @@
             pltpu.VMEM((NY // 2, NX), BF16),
             pltpu.VMEM((NY // 2, NX), BF16),
         ]
-        + [pltpu.VMEM((NY // 4, NX), BF16)] * 4,
+        + [pltpu.VMEM((NY // 4, NX), BF16)] * 4
+        + [
+            pltpu.VMEM((2, NY // 2, NY // 2), BF16),
+            pltpu.VMEM((4, NY // 4, NY // 4), BF16),
+            pltpu.SemaphoreType.DMA((2,)),
+        ],
         compiler_params=pltpu.CompilerParams(vmem_limit_bytes=60 * 1024 * 1024),
         name="destripe",
     )(raw_stack, *tables)
@@ -224,8 +245,7 @@
 
 def filter_z(v, z_table):
     hi, lo = split(v)
-    both = dot(jnp.concatenate([hi, lo], axis=1), z_table)
-    return both[:, :NZ] + both[:, NZ:]
+    return dot(jnp.concatenate([hi, lo], axis=1), z_table[:, :NZ]) + dot(hi, z_table[:NZ, NZ:])
 
 
 def filter_zx(pair, z_table, x_table):
@@ -270,19 +290,24 @@
     for i in range(HL // 2):
         for m in range(2):
             for half in range(2):
-                row = half * LINES + side * HL + 2 * i + m
-                tile = got[pl.ds(row, NZ, stride=2 * LINES), :].T
+                row = half * HL + 2 * i + m
+                tile = got[pl.ds(row, NZ, stride=LINES), :].T
                 cleaned[2 * i + m, half * 128 : (half + 1) * 128, :] = tile
         lines = [cleaned[2 * i], cleaned[2 * i + 1]]
         store_pair(side, i, filter_zx(lines, z_table[...], x_table[...]), outer, inner)
 
 
 def arrive(side, got, tables):
+    def kernel(got, *refs):
+        arrive_kernel(side, got.reshape(NZ * LINES, 128), *refs)
+
     return calls(
-        functools.partial(arrive_kernel, side),
+        kernel,
         f"arrive_{side}",
         ((HL, NX, NZ),) + HALF_SHAPES,
-        in_specs=[WHOLE] * 3,
+        grid=(1,),
+        in_specs=[pl.BlockSpec((NZ, LINES, 128), lambda i: (0, side, 0)), WHOLE, WHOLE],
+        out_specs=[WHOLE] * 3,
     )(got, *tables)
 
 
@@ -397,31 +422,39 @@
     )(meta, taps, *partials, *halos, *others)[0]
 
 
-def leave_kernel(meta, *refs):
-    parts, out, held = refs[:ROUNDS], refs[ROUNDS], refs[ROUNDS + 1]
-    rows = LINES * 32
-    for j in range(ROUNDS):
-        base = meta[2 + ROUNDS + j] * rows
+def leave_kernel(group, meta, *refs):
+    parts, out, held, turned, sem = refs[:4], refs[-4], refs[-3], refs[-2], refs[-1]
+    for j in range(4):
+        base = meta[2 + ROUNDS + 4 * group + j] * (LINES * 32)
 
         @pl.loop(0, LINES, unroll=8)
         def _(y):
             held[pl.ds(pl.multiple_of(base + y * 32, 32), 32), :] = parts[j][y]
 
-    @pl.loop(0, CH * 32, unroll=8)
+    @pl.loop(0, 32, unroll=16)
     def _(i):
-        start = (i // 32) * (128 * 32) + lax.rem(i, 32)
-        tile = held[pl.ds(start, 128, stride=32), :].T
-        out[pl.ds(start, 128, stride=32), :] = tile
-
-
-def leave(meta, parts):
-    return calls(
-        leave_kernel,
-        "leave",
-        ((CH * NZ * 32, 128),),
-        [pltpu.VMEM((CH * 128 * 32, NZ), F32)],
-        in_specs=[SCALARS] + [WHOLE] * ROUNDS,
-    )(meta, *parts)[0]
+        turned[pl.ds(i, NZ, stride=32), :] = held[pl.ds(i, 128, stride=32), :].T
+
+    rows = NZ * 32
+    at = pl.ds(pl.multiple_of(meta[2 + 2 * ROUNDS + group] * rows, rows), rows)
+    copy = pltpu.make_async_copy(turned, out.at[at, :], sem)
+    copy.start()
+    copy.wait()
+
+
+def leave(group, meta, parts, out=None):
+    rows = NZ * 32
+    anywhere = pl.BlockSpec(memory_space=pl.ANY)
+    return pl.pallas_call(
+        functools.partial(leave_kernel, group),
+        in_specs=[SCALARS] + [WHOLE] * 4 + ([] if out is None else [anywhere]),
+        out_specs=anywhere,
+        out_shape=jax.ShapeDtypeStruct((CH * rows, 128), F32),
+        input_output_aliases={} if out is None else {5: 0},
+        scratch_shapes=[pltpu.VMEM((rows, NZ), F32)] * 2 + [pltpu.SemaphoreType.DMA],
+        compiler_params=pltpu.CompilerParams(vmem_limit_bytes=VMEM_LIMIT),
+        name=f"leave_{group}",
+    )(meta, *parts, *([] if out is None else [out]))
 
 
 def local(raw_stack, psf_taps):
@@ -434,7 +467,6 @@
     blocks = destripe(raw_stack).reshape(128, 64, 128)
     got = lax.all_to_all(blocks, AXES, split_axis=0, concat_axis=0, tiled=True)
     tables = filter_tables(taps)
-    got = got.reshape(128 * 64, 128)
     cleaned, halves, halos = [None, None], [None, None], [None, None]
 
     def exchange(side):
@@ -453,7 +485,6 @@
         for side in (first, 1 - first):
             partials[side] = own_lines(way, side, taps, halves)
         if blur == 2 * ITERS - 1:
-            parts = [last(j, taps, meta, partials, halos, estimate) for j in range(ROUNDS)]
             break
         arrived = list(halos)
         halves = [None, None]
@@ -464,8 +495,13 @@
             else:
                 estimate[side], *halves[side] = step(False, *args, estimate[side], tables[0])
             exchange(side)
-    parts = [lax.ppermute(part, AXES, FINAL[j]) for j, part in enumerate(parts)]
-    return leave(meta, parts).reshape(CH, NZ, 32, 128)
+    parts = []
+    for j in range(ROUNDS):
+        part = last(j, taps, meta, partials, halos, estimate)
+        parts.append(lax.ppermute(part, AXES, FINAL[j]))
+    out = leave(0, meta, parts[:4])
+    out = leave(1, meta, parts[4:], out)
+    return out.reshape(CH, NZ, 32, 128)
 
 
 def solution(mesh):

time: 272 us -> 267 us (0.982)
  the two profiles are of different devices: /device:TPU:97 before, /device:TPU:15 now
where the time goes in v3:
time: 267 us
  waiting for transfers between devices  122 us (46%)
  Pallas kernels  109 us (41%)
  starting transfers between devices  33.4 us (13%)
    all_to_all x1, waiting for transfers between devices, local(): got = lax.all_to_all(blocks, AXES, split_axis=0, concat_axis=0, tiled=True)  47.5 us
    ppermute x8, waiting for transfers between devices, local(): parts.append(lax.ppermute(part, AXES, FINAL[j]))  39.6 us
    pallas_call x8, Pallas kernels, own_lines(): calls(functools.partial(own_kernel, way, side), f'own_lines_{side}', ((HL...  39 us
    ppermute x8, waiting for transfers between devices, exchange(): lax.ppermute(halves[side][0], AXES, DOWN if side == 0 else UP)  34.5 us
    pallas_call x6, Pallas kernels, step(): calls(functools.partial(step_kernel, ratio, side), f'ratio_step_{side}' i...  28 us
    ppermute x8, starting transfers between devices, local(): parts.append(lax.ppermute(part, AXES, FINAL[j]))  15 us
    pallas_call x1, Pallas kernels, destripe(): pl.pallas_call(destripe_kernel, grid=(CH,), in_specs=[pl.BlockSpec((1, 1,...  13.4 us
    pallas_call x2, Pallas kernels, arrive(): calls(kernel, f'arrive_{side}', ((HL, NX, NZ),) + HALF_SHAPES, grid=(1,),...  11.3 us
  transfers between devices with their start and end apart: 17, of which 16 were waited for; matrix products, arithmetic and copies ran while one was open for 0% of the time, Pallas kernels for 32%

profile of v3, /device:TPU:15, one launch (start us, length us, event | category | flops | bytes accessed | tf_op | source)
XLA Modules:
  0.0 266.9 jit_solution(9429298744041715375)
XLA Ops:
  0.0 13.4 %destripe.1 = f32[16,4,2,64,128]{4,3,2,1,0:T(8,128)} custom-call(f32[2,1,256,2048]{3,2,1,0:T(8,128)} %raw.1, bf16[256,256]{1,0:T(8,128)(2,1)} %constant.39.clone.ah, bf16[256,256]{1,0:T(8,128)(2,1)} %constant.40.clone.al, bf16[2,1024,1024]{2,1,0:T(8,128)(2,1)} %constant.41.clone.odd_in, bf16[4,512,512]{2,1,0:T(8,128)(2,1)} %constant.42.clone.even_in), custom_call_target="tpu_custom_call" | custom-call | tf_op jit(solution)/shard_map/destripe/pallas_call | solution.py:183
  13.4 11.1 %all-to-all-start = ((f32[128,64,128]{2,1,0:T(8,128)}), f32[128,64,128]{2,1,0:T(8,128)}, u32[]{:S(2)}, u32[]{:S(2)}) async-start(f32[128,64,128]{2,1,0:T(8,128)} %bitcast.6), calls=%async_computation | async-start | bytes 8388608 | tf_op jit(solution)/shard_map/all_to_all | solution.py:468
  24.8 1.4 tables.1
  26.3 47.5 %all-to-all-done.got = f32[128,64,128]{2,1,0:T(8,128)} async-done(((f32[128,64,128]{2,1,0:T(8,128)}), f32[128,64,128]{2,1,0:T(8,128)}, u32[]{:S(2)}, u32[]{:S(2)}) %all-to-all-start) | async-done | bytes 4194336 | tf_op jit(solution)/shard_map/all_to_all | solution.py:468
  73.8 5.7 %arrive_0.1 = (f32[16,256,128]{2,1,0:T(8,128)S(1)}, f32[15,256,128]{2,1,0:T(8,128)}, f32[1,256,128]{2,1,0:T(8,128)S(1)}) custom-call(f32[128,64,128]{2,1,0:T(8,128)} %all-to-all-done.got, bf16[256,256]{1,0:T(8,128)(2,1)S(1)} %get-tuple-element.29.refs_0_.z_table, bf16[256,768]{1,0:T(8,128)(2,1)S(1)} %get-tuple-element.30.refs_1_.x_table), custom_call_target="tpu_custom_call" | custom-call | tf_op jit(solution)/shard_map/arrive_0/pallas_call | solution.py:304
  79.4 1.1 collective-permute-start.1
  80.6 5.6 %arrive_1.1 = (f32[16,256,128]{2,1,0:T(8,128)S(1)}, f32[15,256,128]{2,1,0:T(8,128)}, f32[1,256,128]{2,1,0:T(8,128)S(1)}) custom-call(f32[128,64,128]{2,1,0:T(8,128)} %all-to-all-done.got, bf16[256,256]{1,0:T(8,128)(2,1)S(1)} %get-tuple-element.29.refs_0_.z_table, bf16[256,768]{1,0:T(8,128)(2,1)S(1)} %get-tuple-element.30.refs_1_.x_table), custom_call_target="tpu_custom_call" | custom-call | tf_op jit(solution)/shard_map/arrive_1/pallas_call | solution.py:304
  86.2 1.3 copy-done
  87.5 1.0 collective-permute-start
  89.2 6.1 %own_lines_1.4.partial = f32[16,256,128]{2,1,0:T(8,128)S(1)} custom-call(f32[3,31]{1,0:T(4,128)S(1)} %bitcast_divide_fusion.taps, f32[15,256,128]{2,1,0:T(8,128)} %get-tuple-element.31.low, f32[1,256,128]{2,1,0:T(8,128)S(1)} %get-tuple-element.32.low_mid, f32[1,256,128]{2,1,0:T(8,128)S(1)} %get-tuple-element.33.high_mid, f32[15,256,128]{2,1,0:T(8,128)} %get-tuple-element.34.high), custom_call_target="tpu_custom_call" | custom-call | flops 4000000000 | bytes 1000000 | tf_op jit(solution)/shard_map/own_lines_1/pallas_call | solution.py:343
  95.2 6.2 %own_lines_0.4.partial = f32[16,256,128]{2,1,0:T(8,128)S(1)} custom-call(f32[3,31]{1,0:T(4,128)S(1)} %bitcast_divide_fusion.taps, f32[15,256,128]{2,1,0:T(8,128)} %get-tuple-element.31.low, f32[1,256,128]{2,1,0:T(8,128)S(1)} %get-tuple-element.32.low_mid, f32[1,256,128]{2,1,0:T(8,128)S(1)} %get-tuple-element.33.high_mid, f32[15,256,128]{2,1,0:T(8,128)} %get-tuple-element.34.high), custom_call_target="tpu_custom_call" | custom-call | flops 4000000000 | bytes 1000000 | tf_op jit(solution)/shard_map/own_lines_0/pallas_call | solution.py:343
  101.4 3.0 %collective-permute-done.1.halo = f32[15,256,128]{2,1,0:T(8,128)} collective-permute-done((f32[15,256,128]{2,1,0:T(8,128)}, f32[15,256,128]{2,1,0:T(8,128)}, u32[]{:S(2)}, u32[]{:S(2)}) %collective-permute-start.1) | collective-permute-done | bytes 1966112 | tf_op jit(solution)/shard_map/ppermute | solution.py:473
  104.5 5.5 %ratio_step_1.2 = (f32[15,256,128]{2,1,0:T(8,128)S(1)}, f32[1,256,128]{2,1,0:T(8,128)S(1)}) custom-call(f32[3,31]{1,0:T(4,128)S(1)} %bitcast_divide_fusion.taps, s32[20]{0:T(128)S(1)} %dynamic-slice_bitcast_fusion.meta, f32[16,256,128]{2,1,0:T(8,128)S(1)} %own_lines_1.4.partial, f32[15,256,128]{2,1,0:T(8,128)} %collective-permute-done.1.halo, ...), custom_call_target="tpu_custom_call" | custom-call | tf_op jit(solution)/shard_map/ratio_step_1/pallas_call | solution.py:392
  110.4 5.3 %ratio_step_0.2 = (f32[15,256,128]{2,1,0:T(8,128)S(1)}, f32[1,256,128]{2,1,0:T(8,128)S(1)}) custom-call(f32[3,31]{1,0:T(4,128)S(1)} %bitcast_divide_fusion.taps, s32[20]{0:T(128)S(1)} %dynamic-slice_bitcast_fusion.meta, f32[16,256,128]{2,1,0:T(8,128)S(1)} %own_lines_0.4.partial, f32[15,256,128]{2,1,0:T(8,128)} %collective-permute-done.halo, ...), custom_call_target="tpu_custom_call" | custom-call | tf_op jit(solution)/shard_map/ratio_step_0/pallas_call | solution.py:392
  115.7 1.6 collective-permute-start.3
  117.3 4.5 %own_lines_1.5.partial = f32[16,256,128]{2,1,0:T(8,128)S(1)} custom-call(f32[3,31]{1,0:T(4,128)S(1)} %bitcast_divide_fusion.taps, f32[15,256,128]{2,1,0:T(8,128)S(1)} %get-tuple-element.38.low, f32[1,256,128]{2,1,0:T(8,128)S(1)} %get-tuple-element.39.low_mid, f32[1,256,128]{2,1,0:T(8,128)S(1)} %get-tuple-element.41.high_mid, ...), custom_call_target="tpu_custom_call" | custom-call | flops 4000000000 | bytes 1000000 | tf_op jit(solution)/shard_map/own_lines_1/pallas_call | solution.py:343
  121.8 4.4 %own_lines_0.5.partial = f32[16,256,128]{2,1,0:T(8,128)S(1)} custom-call(f32[3,31]{1,0:T(4,128)S(1)} %bitcast_divide_fusion.taps, f32[15,256,128]{2,1,0:T(8,128)S(1)} %get-tuple-element.38.low, f32[1,256,128]{2,1,0:T(8,128)S(1)} %get-tuple-element.39.low_mid, f32[1,256,128]{2,1,0:T(8,128)S(1)} %get-tuple-element.41.high_mid, ...), custom_call_target="tpu_custom_call" | custom-call | flops 4000000000 | bytes 1000000 | tf_op jit(solution)/shard_map/own_lines_0/pallas_call | solution.py:343
  126.2 5.4 %collective-permute-done.2.halo = f32[15,256,128]{2,1,0:T(8,128)S(1)} collective-permute-done((f32[15,256,128]{2,1,0:T(8,128)S(1)}, f32[15,256,128]{2,1,0:T(8,128)S(1)}, u32[]{:S(2)}, u32[]{:S(2)}) %collective-permute-start.2) | collective-permute-done | bytes 1966112 | tf_op jit(solution)/shard_map/ppermute | solution.py:473
  131.6 4.1 %estimate_step_0.1 = (f32[16,256,128]{2,1,0:T(8,128)S(1)}, f32[15,256,128]{2,1,0:T(8,128)S(1)}, f32[1,256,128]{2,1,0:T(8,128)S(1)}) custom-call(f32[3,31]{1,0:T(4,128)S(1)} %bitcast_divide_fusion.taps, s32[20]{0:T(128)S(1)} %dynamic-slice_bitcast_fusion.meta, f32[16,256,128]{2,1,0:T(8,128)S(1)} %own_lines_0.5.partial, ...), custom_call_target="tpu_custom_call" | custom-call | tf_op jit(solution)/shard_map/estimate_step_0/pallas_call | solution.py:392
  135.7 1.6 collective-permute-start.5
  137.3 3.3 %collective-permute-done.3.halo = f32[15,256,128]{2,1,0:T(8,128)S(1)} collective-permute-done((f32[15,256,128]{2,1,0:T(8,128)S(1)}, f32[15,256,128]{2,1,0:T(8,128)S(1)}, u32[]{:S(2)}, u32[]{:S(2)}) %collective-permute-start.3) | collective-permute-done | bytes 1966112 | tf_op jit(solution)/shard_map/ppermute | solution.py:473
  140.6 4.2 %estimate_step_1.1 = (f32[16,256,128]{2,1,0:T(8,128)S(1)}, f32[15,256,128]{2,1,0:T(8,128)S(1)}, f32[1,256,128]{2,1,0:T(8,128)S(1)}) custom-call(f32[3,31]{1,0:T(4,128)S(1)} %bitcast_divide_fusion.taps, s32[20]{0:T(128)S(1)} %dynamic-slice_bitcast_fusion.meta, f32[16,256,128]{2,1,0:T(8,128)S(1)} %own_lines_1.5.partial, ...), custom_call_target="tpu_custom_call" | custom-call | tf_op jit(solution)/shard_map/estimate_step_1/pallas_call | solution.py:392
  145.1 4.5 %own_lines_1.6.partial = f32[16,256,128]{2,1,0:T(8,128)S(1)} custom-call(f32[3,31]{1,0:T(4,128)S(1)} %bitcast_divide_fusion.taps, f32[15,256,128]{2,1,0:T(8,128)S(1)} %get-tuple-element.43.low, f32[1,256,128]{2,1,0:T(8,128)S(1)} %get-tuple-element.44.low_mid, f32[1,256,128]{2,1,0:T(8,128)S(1)} %get-tuple-element.45.high_mid, ...), custom_call_target="tpu_custom_call" | custom-call | flops 4000000000 | bytes 1000000 | tf_op jit(solution)/shard_map/own_lines_1/pallas_call | solution.py:343
  149.6 4.4 %own_lines_0.6.partial = f32[16,256,128]{2,1,0:T(8,128)S(1)} custom-call(f32[3,31]{1,0:T(4,128)S(1)} %bitcast_divide_fusion.taps, f32[15,256,128]{2,1,0:T(8,128)S(1)} %get-tuple-element.43.low, f32[1,256,128]{2,1,0:T(8,128)S(1)} %get-tuple-element.44.low_mid, f32[1,256,128]{2,1,0:T(8,128)S(1)} %get-tuple-element.45.high_mid, ...), custom_call_target="tpu_custom_call" | custom-call | flops 4000000000 | bytes 1000000 | tf_op jit(solution)/shard_map/own_lines_0/pallas_call | solution.py:343
  154.0 7.9 %collective-permute-done.5.halo = f32[15,256,128]{2,1,0:T(8,128)S(1)} collective-permute-done((f32[15,256,128]{2,1,0:T(8,128)S(1)}, f32[15,256,128]{2,1,0:T(8,128)S(1)}, u32[]{:S(2)}, u32[]{:S(2)}) %collective-permute-start.5) | collective-permute-done | bytes 1966112 | tf_op jit(solution)/shard_map/ppermute | solution.py:473
  161.9 4.5 %ratio_step_1.3 = (f32[15,256,128]{2,1,0:T(8,128)S(1)}, f32[1,256,128]{2,1,0:T(8,128)S(1)}) custom-call(f32[3,31]{1,0:T(4,128)S(1)} %bitcast_divide_fusion.taps, s32[20]{0:T(128)S(1)} %dynamic-slice_bitcast_fusion.meta, f32[16,256,128]{2,1,0:T(8,128)S(1)} %own_lines_1.6.partial, f32[15,256,128]{2,1,0:T(8,128)S(1)} %collective-permute-done.5.halo, ...), custom_call_target="tpu_custom_call" | custom-call | tf_op jit(solution)/shard_map/ratio_step_1/pallas_call | solution.py:392
  166.7 4.3 %ratio_step_0.3 = (f32[15,256,128]{2,1,0:T(8,128)S(1)}, f32[1,256,128]{2,1,0:T(8,128)S(1)}) custom-call(f32[3,31]{1,0:T(4,128)S(1)} %bitcast_divide_fusion.taps, s32[20]{0:T(128)S(1)} %dynamic-slice_bitcast_fusion.meta, f32[16,256,128]{2,1,0:T(8,128)S(1)} %own_lines_0.6.partial, f32[15,256,128]{2,1,0:T(8,128)S(1)} %collective-permute-done.4.halo, ...), custom_call_target="tpu_custom_call" | custom-call | tf_op jit(solution)/shard_map/ratio_step_0/pallas_call | solution.py:392
  171.0 1.6 collective-permute-start.7
  172.6 4.5 %own_lines_1.7.refs_1_ = f32[16,256,128]{2,1,0:T(8,128)S(1)} custom-call(f32[3,31]{1,0:T(4,128)S(1)} %bitcast_divide_fusion.taps, f32[15,256,128]{2,1,0:T(8,128)S(1)} %get-tuple-element.47.low, f32[1,256,128]{2,1,0:T(8,128)S(1)} %get-tuple-element.48.low_mid, f32[1,256,128]{2,1,0:T(8,128)S(1)} %get-tuple-element.49.high_mid, ...), custom_call_target="tpu_custom_call" | custom-call | flops 4000000000 | bytes 1000000 | tf_op jit(solution)/shard_map/own_lines_1/pallas_call | solution.py:343
  177.1 4.4 %own_lines_0.7.refs_0_ = f32[16,256,128]{2,1,0:T(8,128)S(1)} custom-call(f32[3,31]{1,0:T(4,128)S(1)} %bitcast_divide_fusion.taps, f32[15,256,128]{2,1,0:T(8,128)S(1)} %get-tuple-element.47.low, f32[1,256,128]{2,1,0:T(8,128)S(1)} %get-tuple-element.48.low_mid, f32[1,256,128]{2,1,0:T(8,128)S(1)} %get-tuple-element.49.high_mid, ...), custom_call_target="tpu_custom_call" | custom-call | flops 4000000000 | bytes 1000000 | tf_op jit(solution)/shard_map/own_lines_0/pallas_call | solution.py:343
  181.5 6.6 %collective-permute-done.6.refs_2_ = f32[15,256,128]{2,1,0:T(8,128)S(1)} collective-permute-done((f32[15,256,128]{2,1,0:T(8,128)S(1)}, f32[15,256,128]{2,1,0:T(8,128)S(1)}, u32[]{:S(2)}, u32[]{:S(2)}) %collective-permute-start.6) | collective-permute-done | bytes 1966112 | tf_op jit(solution)/shard_map/ppermute | solution.py:473
  188.1 7.7 %collective-permute-done.7.refs_3_ = f32[15,256,128]{2,1,0:T(8,128)S(1)} collective-permute-done((f32[15,256,128]{2,1,0:T(8,128)S(1)}, f32[15,256,128]{2,1,0:T(8,128)S(1)}, u32[]{:S(2)}, u32[]{:S(2)}) %collective-permute-start.7) | collective-permute-done | bytes 1966112 | tf_op jit(solution)/shard_map/ppermute | solution.py:473
  196.9 0.9 last_step.14
  199.1 4.5 %collective-permute-start.13 = (f32[32,32,128]{2,1,0:T(8,128)S(1)}, f32[32,32,128]{2,1,0:T(8,128)S(1)}, u32[]{:S(2)}, u32[]{:S(2)}) collective-permute-start(f32[32,32,128]{2,1,0:T(8,128)S(1)} %last_step.13), channel_id=1, source_target_pairs={{0,2},{8,6},{2,4},{10,0},{4,15},{12,11},{6,9},{14,13},{22,16},{30,... | collective-permute-start | bytes 1572872 | tf_op jit(solution)/shard_map/ppermute | solution.py:501
  204.6 2.1 collective-permute-start.12
  206.7 0.9 last_step.11
  207.6 3.2 %collective-permute-start.11 = (f32[32,32,128]{2,1,0:T(8,128)S(1)}, f32[32,32,128]{2,1,0:T(8,128)S(1)}, u32[]{:S(2)}, u32[]{:S(2)}) collective-permute-start(f32[32,32,128]{2,1,0:T(8,128)S(1)} %last_step.11), channel_id=1, source_target_pairs={{0,7},{8,3},{2,1},{10,5},{4,10},{12,14},{6,12},{14,8},{22,21},{30,... | collective-permute-start | bytes 1572872 | tf_op jit(solution)/shard_map/ppermute | solution.py:501
  211.8 0.9 last_step.9
  212.7 0.9 last_step.8
  213.7 1.9 collective-permute-start.10
  215.6 7.3 %collective-permute-done.14.refs_2_ = f32[32,32,128]{2,1,0:T(8,128)S(1)} collective-permute-done((f32[32,32,128]{2,1,0:T(8,128)S(1)}, f32[32,32,128]{2,1,0:T(8,128)S(1)}, u32[]{:S(2)}, u32[]{:S(2)}) %collective-permute-start.14) | collective-permute-done | bytes 524320 | tf_op jit(solution)/shard_map/ppermute | solution.py:501
  222.9 4.6 %collective-permute-done.13.refs_1_ = f32[32,32,128]{2,1,0:T(8,128)S(1)} collective-permute-done((f32[32,32,128]{2,1,0:T(8,128)S(1)}, f32[32,32,128]{2,1,0:T(8,128)S(1)}, u32[]{:S(2)}, u32[]{:S(2)}) %collective-permute-start.13) | collective-permute-done | bytes 524320 | tf_op jit(solution)/shard_map/ppermute | solution.py:501
  227.5 2.9 %collective-permute-start.8 = (f32[32,32,128]{2,1,0:T(8,128)S(1)}, f32[32,32,128]{2,1,0:T(8,128)S(1)}, u32[]{:S(2)}, u32[]{:S(2)}) collective-permute-start(f32[32,32,128]{2,1,0:T(8,128)S(1)} %last_step.8), channel_id=1, source_target_pairs={{0,1},{8,5},{2,3},{10,7},{4,12},{12,8},{6,14},{14,10},{22,23},{30,... | collective-permute-start | bytes 1572872 | tf_op jit(solution)/shard_map/ppermute | solution.py:501
  231.3 4.3 %leave_0.1.refs_4_ = f32[8192,128]{1,0:T(8,128)} custom-call(s32[20]{0:T(128)S(1)} %dynamic-slice_bitcast_fusion.meta, f32[32,32,128]{2,1,0:T(8,128)S(1)} %collective-permute-done.12.refs_0_, f32[32,32,128]{2,1,0:T(8,128)S(1)} %collective-permute-done.13.refs_1_, f32[32,32,128]{2,1,0:T(8,128)S(1)} %collective-permute-done.14.refs_2_, ...), custom_call_target="tpu_custom_call" | custom-call | tf_op jit(solution)/shard_map/leave_0/pallas_call | solution.py:448
  236.0 9.5 %collective-permute-done.10.refs_2_ = f32[32,32,128]{2,1,0:T(8,128)S(1)} collective-permute-done((f32[32,32,128]{2,1,0:T(8,128)S(1)}, f32[32,32,128]{2,1,0:T(8,128)S(1)}, u32[]{:S(2)}, u32[]{:S(2)}) %collective-permute-start.10) | collective-permute-done | bytes 524320 | tf_op jit(solution)/shard_map/ppermute | solution.py:501
  245.5 10.1 %collective-permute-done.9.refs_1_ = f32[32,32,128]{2,1,0:T(8,128)S(1)} collective-permute-done((f32[32,32,128]{2,1,0:T(8,128)S(1)}, f32[32,32,128]{2,1,0:T(8,128)S(1)}, u32[]{:S(2)}, u32[]{:S(2)}) %collective-permute-start.9) | collective-permute-done | bytes 524320 | tf_op jit(solution)/shard_map/ppermute | solution.py:501
  255.6 6.8 %collective-permute-done.8.refs_0_ = f32[32,32,128]{2,1,0:T(8,128)S(1)} collective-permute-done((f32[32,32,128]{2,1,0:T(8,128)S(1)}, f32[32,32,128]{2,1,0:T(8,128)S(1)}, u32[]{:S(2)}, u32[]{:S(2)}) %collective-permute-start.8) | collective-permute-done | bytes 524320 | tf_op jit(solution)/shard_map/ppermute | solution.py:501
  262.4 4.3 %leave_1.1 = f32[8192,128]{1,0:T(8,128)} custom-call(s32[20]{0:T(128)S(1)} %dynamic-slice_bitcast_fusion.meta, f32[32,32,128]{2,1,0:T(8,128)S(1)} %collective-permute-done.8.refs_0_, f32[32,32,128]{2,1,0:T(8,128)S(1)} %collective-permute-done.9.refs_1_, f32[32,32,128]{2,1,0:T(8,128)S(1)} %collective-permute-done.10.refs_2_, ...), custom_call_target="tpu_custom_call", output_to_operand_aliasing={{}: (5, {})} | custom-call | tf_op jit(solution)/shard_map/leave_1/pallas_call | solution.py:448
  (23 shorter events, 7.2 us)
Async XLA Ops:
  13.4 11.2 %copy-start.2 = (f32[3,2,31]{2,1,0:T(2,128)S(1)}, f32[3,2,31]{2,1,0:T(2,128)}, u32[]{:S(2)}) copy-start(f32[3,2,31]{2,1,0:T(2,128)} %param.8) | copy-start | bytes 2236
  13.4 60.3 %all-to-all-start = ((f32[128,64,128]{2,1,0:T(8,128)}), f32[128,64,128]{2,1,0:T(8,128)}, u32[]{:S(2)}, u32[]{:S(2)}) async-start(f32[128,64,128]{2,1,0:T(8,128)} %bitcast.6), calls=%async_computation | async-start | bytes 8388608 | tf_op jit(solution)/shard_map/all_to_all | solution.py:468
  79.4 25.0 %collective-permute-start.1 = (f32[15,256,128]{2,1,0:T(8,128)}, f32[15,256,128]{2,1,0:T(8,128)}, u32[]{:S(2)}, u32[]{:S(2)}) collective-permute-start(f32[15,256,128]{2,1,0:T(8,128)} %get-tuple-element.31.low), channel_id=1, source_target_pairs={{8,0},{2,8},{10,2},{4,10},{12,4},{6,12},{14,6},{22,14},{30,22},{20... | collective-permute-start | bytes 5898248 | tf_op jit(solution)/shard_map/ppermute | solution.py:473
  86.2 1.3 copy-start
  87.5 22.9 %collective-permute-start = (f32[15,256,128]{2,1,0:T(8,128)}, f32[15,256,128]{2,1,0:T(8,128)}, u32[]{:S(2)}, u32[]{:S(2)}) collective-permute-start(f32[15,256,128]{2,1,0:T(8,128)} %get-tuple-element.34.high), channel_id=1, source_target_pairs={{0,8},{8,2},{2,10},{10,4},{4,12},{12,6},{6,14},{14,22},{22,30},{30... | collective-permute-start | bytes 5898248 | tf_op jit(solution)/shard_map/ppermute | solution.py:473
  95.2 9.2 %copy-start.1 = (f32[16,256,128]{2,1,0:T(8,128)S(1)}, f32[16,256,128]{2,1,0:T(8,128)}, u32[]{:S(2)}) copy-start(f32[16,256,128]{2,1,0:T(8,128)} %copy-done) | copy-start | bytes 6291460
  110.0 21.6 %collective-permute-start.2 = (f32[15,256,128]{2,1,0:T(8,128)S(1)}, f32[15,256,128]{2,1,0:T(8,128)S(1)}, u32[]{:S(2)}, u32[]{:S(2)}) collective-permute-start(f32[15,256,128]{2,1,0:T(8,128)S(1)} %get-tuple-element.42.high), channel_id=1, source_target_pairs={{0,8},{8,2},{2,10},{10,4},{4,12},{12,6},{6,14},{14,22},{22,30},{30... | collective-permute-start | bytes 5898248 | tf_op jit(solution)/shard_map/ppermute | solution.py:473
  115.7 24.9 %collective-permute-start.3 = (f32[15,256,128]{2,1,0:T(8,128)S(1)}, f32[15,256,128]{2,1,0:T(8,128)S(1)}, u32[]{:S(2)}, u32[]{:S(2)}) collective-permute-start(f32[15,256,128]{2,1,0:T(8,128)S(1)} %get-tuple-element.38.low), channel_id=1, source_target_pairs={{8,0},{2,8},{10,2},{4,10},{12,4},{6,12},{14,6},{22,14},{30,22},{20... | collective-permute-start | bytes 5898248 | tf_op jit(solution)/shard_map/ppermute | solution.py:473
  135.7 26.3 %collective-permute-start.5 = (f32[15,256,128]{2,1,0:T(8,128)S(1)}, f32[15,256,128]{2,1,0:T(8,128)S(1)}, u32[]{:S(2)}, u32[]{:S(2)}) collective-permute-start(f32[15,256,128]{2,1,0:T(8,128)S(1)} %get-tuple-element.43.low), channel_id=1, source_target_pairs={{8,0},{2,8},{10,2},{4,10},{12,4},{6,12},{14,6},{22,14},{30,22},{20... | collective-permute-start | bytes 5898248 | tf_op jit(solution)/shard_map/ppermute | solution.py:473
  144.8 21.9 %collective-permute-start.4 = (f32[15,256,128]{2,1,0:T(8,128)S(1)}, f32[15,256,128]{2,1,0:T(8,128)S(1)}, u32[]{:S(2)}, u32[]{:S(2)}) collective-permute-start(f32[15,256,128]{2,1,0:T(8,128)S(1)} %get-tuple-element.46.high), channel_id=1, source_target_pairs={{0,8},{8,2},{2,10},{10,4},{4,12},{12,6},{6,14},{14,22},{22,30},{30... | collective-permute-start | bytes 5898248 | tf_op jit(solution)/shard_map/ppermute | solution.py:473
  166.5 21.6 %collective-permute-start.6 = (f32[15,256,128]{2,1,0:T(8,128)S(1)}, f32[15,256,128]{2,1,0:T(8,128)S(1)}, u32[]{:S(2)}, u32[]{:S(2)}) collective-permute-start(f32[15,256,128]{2,1,0:T(8,128)S(1)} %get-tuple-element.50.high), channel_id=1, source_target_pairs={{0,8},{8,2},{2,10},{10,4},{4,12},{12,6},{6,14},{14,22},{22,30},{30... | collective-permute-start | bytes 5898248 | tf_op jit(solution)/shard_map/ppermute | solution.py:473
  171.0 24.9 %collective-permute-start.7 = (f32[15,256,128]{2,1,0:T(8,128)S(1)}, f32[15,256,128]{2,1,0:T(8,128)S(1)}, u32[]{:S(2)}, u32[]{:S(2)}) collective-permute-start(f32[15,256,128]{2,1,0:T(8,128)S(1)} %get-tuple-element.47.low), channel_id=1, source_target_pairs={{8,0},{2,8},{10,2},{4,10},{12,4},{6,12},{14,6},{22,14},{30,22},{20... | collective-permute-start | bytes 5898248 | tf_op jit(solution)/shard_map/ppermute | solution.py:473
  196.8 16.9 %collective-permute-start.15 = (f32[32,32,128]{2,1,0:T(8,128)S(1)}, f32[32,32,128]{2,1,0:T(8,128)S(1)}, u32[]{:S(2)}, u32[]{:S(2)}) collective-permute-start(f32[32,32,128]{2,1,0:T(8,128)S(1)} %last_step.15), channel_id=1, source_target_pairs={{0,6},{8,2},{2,0},{10,4},{4,11},{12,15},{6,13},{14,9},{22,20},{30,... | collective-permute-start | bytes 1572872 | tf_op jit(solution)/shard_map/ppermute | solution.py:501
  197.9 25.1 %collective-permute-start.14 = (f32[32,32,128]{2,1,0:T(8,128)S(1)}, f32[32,32,128]{2,1,0:T(8,128)S(1)}, u32[]{:S(2)}, u32[]{:S(2)}) collective-permute-start(f32[32,32,128]{2,1,0:T(8,128)S(1)} %last_step.14), channel_id=1, source_target_pairs={{0,4},{8,0},{2,6},{10,2},{4,9},{12,13},{6,11},{14,15},{22,18},{30,... | collective-permute-start | bytes 1572872 | tf_op jit(solution)/shard_map/ppermute | solution.py:501
  199.1 28.4 %collective-permute-start.13 = (f32[32,32,128]{2,1,0:T(8,128)S(1)}, f32[32,32,128]{2,1,0:T(8,128)S(1)}, u32[]{:S(2)}, u32[]{:S(2)}) collective-permute-start(f32[32,32,128]{2,1,0:T(8,128)S(1)} %last_step.13), channel_id=1, source_target_pairs={{0,2},{8,6},{2,4},{10,0},{4,15},{12,11},{6,9},{14,13},{22,16},{30,... | collective-permute-start | bytes 1572872 | tf_op jit(solution)/shard_map/ppermute | solution.py:501
  204.6 26.7 %collective-permute-start.12 = (f32[32,32,128]{2,1,0:T(8,128)S(1)}, f32[32,32,128]{2,1,0:T(8,128)S(1)}, u32[]{:S(2)}, u32[]{:S(2)}) collective-permute-start(f32[32,32,128]{2,1,0:T(8,128)S(1)} %last_step.12), channel_id=1, source_target_pairs={{0,0},{8,4},{2,2},{10,6},{4,13},{12,9},{6,15},{14,11},{22,22},{30,... | collective-permute-start | bytes 1572872 | tf_op jit(solution)/shard_map/ppermute | solution.py:501
  207.6 28.3 %collective-permute-start.11 = (f32[32,32,128]{2,1,0:T(8,128)S(1)}, f32[32,32,128]{2,1,0:T(8,128)S(1)}, u32[]{:S(2)}, u32[]{:S(2)}) collective-permute-start(f32[32,32,128]{2,1,0:T(8,128)S(1)} %last_step.11), channel_id=1, source_target_pairs={{0,7},{8,3},{2,1},{10,5},{4,10},{12,14},{6,12},{14,8},{22,21},{30,... | collective-permute-start | bytes 1572872 | tf_op jit(solution)/shard_map/ppermute | solution.py:501
  213.7 31.8 %collective-permute-start.10 = (f32[32,32,128]{2,1,0:T(8,128)S(1)}, f32[32,32,128]{2,1,0:T(8,128)S(1)}, u32[]{:S(2)}, u32[]{:S(2)}) collective-permute-start(f32[32,32,128]{2,1,0:T(8,128)S(1)} %last_step.10), channel_id=1, source_target_pairs={{0,5},{8,1},{2,7},{10,3},{4,8},{12,12},{6,10},{14,14},{22,19},{30,... | collective-permute-start | bytes 1572872 | tf_op jit(solution)/shard_map/ppermute | solution.py:501
  222.9 32.7 %collective-permute-start.9 = (f32[32,32,128]{2,1,0:T(8,128)S(1)}, f32[32,32,128]{2,1,0:T(8,128)S(1)}, u32[]{:S(2)}, u32[]{:S(2)}) collective-permute-start(f32[32,32,128]{2,1,0:T(8,128)S(1)} %last_step.9), channel_id=1, source_target_pairs={{0,3},{8,7},{2,5},{10,1},{4,14},{12,10},{6,8},{14,12},{22,17},{30,... | collective-permute-start | bytes 1572872 | tf_op jit(solution)/shard_map/ppermute | solution.py:501
  227.5 34.9 %collective-permute-start.8 = (f32[32,32,128]{2,1,0:T(8,128)S(1)}, f32[32,32,128]{2,1,0:T(8,128)S(1)}, u32[]{:S(2)}, u32[]{:S(2)}) collective-permute-start(f32[32,32,128]{2,1,0:T(8,128)S(1)} %last_step.8), channel_id=1, source_target_pairs={{0,1},{8,5},{2,3},{10,7},{4,12},{12,8},{6,14},{14,10},{22,23},{30,... | collective-permute-start | bytes 1572872 | tf_op jit(solution)/shard_map/ppermute | solution.py:501

commit v4 on v3

--- a/solution.py
+++ b/solution.py
@@ -92,8 +92,14 @@
     odd = along[:h, :h] - along[:h, h:]
     even_even = even[:q, :q] + even[:q, q:]
     even_odd = even[:q, :q] - even[:q, q:]
-    ah, al = np_split(across.T)
-    return ah, al, np.stack(np_split(odd)), np.stack(np_split(even_even) + np_split(even_odd))
+    size = 256
+    blocks = []
+    for table in (odd, even_even, even_odd):
+        count = table.shape[0] // size
+        for d in range(count - 1, -count, -1):
+            r, c = max(d, 0) * size, max(-d, 0) * size
+            blocks.append(table[r : r + size, c : c + size])
+    return np.stack(np_split(across.T)), np.stack(np_split(np.concatenate(blocks, axis=1)))
 
 
 def split(v):
@@ -109,98 +115,108 @@
     return dot(a_high, b_high) + (dot(a_high, b_low) + dot(a_low, b_high))
 
 
-def destripe_kernel(raw, ah, al, odd_in, even_in, out, rt, sm, dh, dl, s1h, s1l, d1h, d1l, odd, even, sems):
+def destripe_kernel(raw_in, across_in, along_in, out_to, raw, across, along, out, rt, sm, dh, dl, s1h, s1l, d1h, d1l, in_sems, out_sems):
     h, q = NY // 2, NY // 4
-    copies = [
-        pltpu.make_async_copy(odd_in, odd, sems.at[0]),
-        pltpu.make_async_copy(even_in, even, sems.at[1]),
+    across_copy = pltpu.make_async_copy(across_in, across, in_sems.at[0])
+    along_copy = pltpu.make_async_copy(along_in, along, in_sems.at[1])
+    raw_copies = [
+        pltpu.make_async_copy(raw_in.at[c, 0], raw.at[c], in_sems.at[2 + c]) for c in range(CH)
     ]
-
-    @pl.when(pl.program_id(0) == 0)
-    def _():
-        for copy in copies:
-            copy.start()
-
-    @pl.loop(0, NY // 256, unroll=4)
-    def _(i):
-        r = pl.multiple_of(i * 256, 256)
-        tile = raw[0, 0, :, pl.ds(r, 256)].T
-        rt[pl.ds(r, 256), :] = tile
-        th, tl = split(tile)
-        sm[pl.ds(r, 256), :] = dot3(th, tl, ah[...], al[...])
-
-    @pl.loop(0, q // 128)
-    def _(i):
-        r = pl.multiple_of(i * 128, 128)
-        parts = [sm[pl.ds(r + m * q, 128), :] for m in range(4)]
-        for m in range(2):
-            hi, lo = split(0.5 * (parts[m] - parts[m + 2]))
-            dh[pl.ds(r + m * q, 128), :] = hi
-            dl[pl.ds(r + m * q, 128), :] = lo
-        top = 0.5 * (parts[0] + parts[2])
-        bottom = 0.5 * (parts[1] + parts[3])
-        hi, lo = split(0.5 * (top + bottom))
-        s1h[pl.ds(r, 128), :] = hi
-        s1l[pl.ds(r, 128), :] = lo
-        hi, lo = split(0.5 * (top - bottom))
-        d1h[pl.ds(r, 128), :] = hi
-        d1l[pl.ds(r, 128), :] = lo
-
-    @pl.when(pl.program_id(0) == 0)
-    def _():
-        for copy in copies:
-            copy.wait()
-
-    def emit(row, smooth):
+    across_copy.start()
+    raw_copies[0].start()
+    raw_copies[1].start()
+    across_copy.wait()
+    for c in range(CH):
+        raw_copies[c].wait()
+        if c == 0:
+            along_copy.start()
+
+        @pl.loop(0, NY // 256, unroll=4)
+        def _(i):
+            r = pl.multiple_of(i * 256, 256)
+            tile = raw[c, :, pl.ds(r, 256)].T
+            rt[c, pl.ds(r, 256), :] = tile
+            th, tl = split(tile)
+            sm[c, pl.ds(r, 256), :] = dot3(th, tl, across[0], across[1])
+
+        @pl.loop(0, q // 128)
+        def _(i):
+            r = pl.multiple_of(i * 128, 128)
+            parts = [sm[c, pl.ds(r + m * q, 128), :] for m in range(4)]
+            for m in range(2):
+                hi, lo = split(0.5 * (parts[m] - parts[m + 2]))
+                dh[c, pl.ds(r + m * q, 128), :] = hi
+                dl[c, pl.ds(r + m * q, 128), :] = lo
+            top = 0.5 * (parts[0] + parts[2])
+            bottom = 0.5 * (parts[1] + parts[3])
+            hi, lo = split(0.5 * (top + bottom))
+            s1h[c, pl.ds(r, 128), :] = hi
+            s1l[c, pl.ds(r, 128), :] = lo
+            hi, lo = split(0.5 * (top - bottom))
+            d1h[c, pl.ds(r, 128), :] = hi
+            d1l[c, pl.ds(r, 128), :] = lo
+
+    along_copy.wait()
+    out_copies = []
+
+    def emit(c, row, smooth):
         for m in range(8):
             x, yl, z, core = place(row // LINES + m)
             at = pl.ds(row + m * LINES, LINES)
             part = smooth[m * LINES : (m + 1) * LINES, :]
-            clean = jnp.maximum(rt[at, :] - (sm[at, :] - part), 0.0)
+            clean = jnp.maximum(rt[c, at, :] - (sm[c, at, :] - part), 0.0)
             gx = (z * 2 + yl) * 2 + core
-            for side in range(2):
-                for half in range(2):
-                    to = (2 * side + half) * HL
-                    tile = clean[side * HL : (side + 1) * HL, half * 128 : (half + 1) * 128]
-                    out[gx, x, 0, to : to + HL, :] = tile
-
-    for i in range(2):
-        at = slice(i * 256, (i + 1) * 256)
-        ee = dot3(even[0, at, :], even[1, at, :], s1h[...], s1l[...])
-        eo = dot3(even[2, at, :], even[3, at, :], d1h[...], d1l[...])
-        for m in range(2):
-            row = m * q + i * 256
-            rows = slice(row, row + 256)
-            smooth_even = ee + eo if m == 0 else ee - eo
-            smooth_odd = dot3(odd[0, rows, :], odd[1, rows, :], dh[...], dl[...])
-            emit(row, smooth_even + smooth_odd)
-            emit(h + row, smooth_even - smooth_odd)
+            for half in range(2):
+                tile = clean[:, half * 128 : (half + 1) * 128]
+                out[c, gx, x, pl.ds(half, LINES, stride=2), :] = tile
+        first = (z * 2 + yl) * 2
+        copy = pltpu.make_async_copy(
+            out.at[c, pl.ds(first, 2)], out_to.at[pl.ds(first, 2), :, c], out_sems.at[len(out_copies)]
+        )
+        copy.start()
+        out_copies.append(copy)
+
+    def window(first, block, count, high, low):
+        at = slice(first + (count - 1 - block) * 256, first + (2 * count - 1 - block) * 256)
+        return dot3(along[0, :, at], along[1, :, at], high, low)
+
+    for c in range(CH):
+        for i in range(2):
+            ee = window(7 * 256, i, 2, s1h[c], s1l[c])
+            eo = window(10 * 256, i, 2, d1h[c], d1l[c])
+            for m in range(2):
+                row = m * q + i * 256
+                even = ee + eo if m == 0 else ee - eo
+                odd = window(0, 2 * m + i, 4, dh[c], dl[c])
+                emit(c, row, even + odd)
+                emit(c, h + row, even - odd)
+    for copy in out_copies:
+        copy.wait()
 
 
 def destripe(raw_stack):
-    tables = [jnp.asarray(t) for t in destripe_tables()]
-    whole, anywhere = (pl.BlockSpec(memory_space=m) for m in (pltpu.VMEM, pl.ANY))
+    across, along = (jnp.asarray(t) for t in destripe_tables())
+    anywhere = pl.BlockSpec(memory_space=pl.ANY)
     return pl.pallas_call(
         destripe_kernel,
-        grid=(CH,),
-        in_specs=[pl.BlockSpec((1, 1, NX, NY), lambda c: (c, 0, 0, 0)), whole, whole, anywhere, anywhere],
-        out_specs=pl.BlockSpec((16, 4, 1, 64, 128), lambda c: (0, 0, c, 0, 0)),
+        in_specs=[anywhere] * 3,
+        out_specs=anywhere,
         out_shape=jax.ShapeDtypeStruct((16, 4, CH, 64, 128), F32),
         scratch_shapes=[
-            pltpu.VMEM((NY, NX), F32),
-            pltpu.VMEM((NY, NX), F32),
-            pltpu.VMEM((NY // 2, NX), BF16),
-            pltpu.VMEM((NY // 2, NX), BF16),
+            pltpu.VMEM((CH, NX, NY), F32),
+            pltpu.VMEM(across.shape, BF16),
+            pltpu.VMEM(along.shape, BF16),
+            pltpu.VMEM((CH, 16, 4, 64, 128), F32),
+            pltpu.VMEM((CH, NY, NX), F32),
+            pltpu.VMEM((CH, NY, NX), F32),
+            pltpu.VMEM((CH, NY // 2, NX), BF16),
+            pltpu.VMEM((CH, NY // 2, NX), BF16),
         ]
-        + [pltpu.VMEM((NY // 4, NX), BF16)] * 4
-        + [
-            pltpu.VMEM((2, NY // 2, NY // 2), BF16),
-            pltpu.VMEM((4, NY // 4, NY // 4), BF16),
-            pltpu.SemaphoreType.DMA((2,)),
-        ],
+        + [pltpu.VMEM((CH, NY // 4, NX), BF16)] * 4
+        + [pltpu.SemaphoreType.DMA((4,)), pltpu.SemaphoreType.DMA((16,))],
         compiler_params=pltpu.CompilerParams(vmem_limit_bytes=60 * 1024 * 1024),
         name="destripe",
-    )(raw_stack, *tables)
+    )(raw_stack, across, along)
 
 
 def band(weights, size):
@@ -287,22 +303,20 @@
 
 
 def arrive_kernel(side, got, z_table, x_table, cleaned, outer, inner):
+    rows = got.reshape(NZ * LINES, 128)
     for i in range(HL // 2):
         for m in range(2):
             for half in range(2):
-                row = half * HL + 2 * i + m
-                tile = got[pl.ds(row, NZ, stride=LINES), :].T
+                row = 2 * (2 * i + m) + half
+                tile = rows[pl.ds(row, NZ, stride=LINES), :].T
                 cleaned[2 * i + m, half * 128 : (half + 1) * 128, :] = tile
         lines = [cleaned[2 * i], cleaned[2 * i + 1]]
         store_pair(side, i, filter_zx(lines, z_table[...], x_table[...]), outer, inner)
 
 
 def arrive(side, got, tables):
-    def kernel(got, *refs):
-        arrive_kernel(side, got.reshape(NZ * LINES, 128), *refs)
-
     return calls(
-        kernel,
+        functools.partial(arrive_kernel, side),
         f"arrive_{side}",
         ((HL, NX, NZ),) + HALF_SHAPES,
         grid=(1,),

time: 267 us -> 266 us (level)
  transfers between devices with their start and end apart: 17 -> 17, of which waited for: 16 -> 15; matrix products, arithmetic and copies ran while one was open for 0% -> 0% of each run, Pallas kernels for 32% -> 32%
where the time goes in v4:
time: 266 us
  waiting for transfers between devices  121 us (45%)
  Pallas kernels  108 us (41%)
  starting transfers between devices  33.3 us (13%)
    all_to_all x1, waiting for transfers between devices, local(): got = lax.all_to_all(blocks, AXES, split_axis=0, concat_axis=0, tiled=True)  47.5 us
    ppermute x8, waiting for transfers between devices, local(): parts.append(lax.ppermute(part, AXES, FINAL[j]))  39.6 us
    pallas_call x8, Pallas kernels, own_lines(): calls(functools.partial(own_kernel, way, side), f'own_lines_{side}', ((HL...  39 us
    ppermute x8, waiting for transfers between devices, exchange(): lax.ppermute(halves[side][0], AXES, DOWN if side == 0 else UP)  34.4 us
    pallas_call x6, Pallas kernels, step(): calls(functools.partial(step_kernel, ratio, side), f'ratio_step_{side}' i...  28 us
    ppermute x8, starting transfers between devices, local(): parts.append(lax.ppermute(part, AXES, FINAL[j]))  15 us
    pallas_call x1, Pallas kernels, destripe(): pl.pallas_call(destripe_kernel, in_specs=[anywhere] * 3, out_specs=anywhe...  12.4 us
    pallas_call x2, Pallas kernels, arrive(): calls(functools.partial(arrive_kernel, side), f'arrive_{side}', ((HL, NX,...  11.3 us
  transfers between devices with their start and end apart: 17, of which 15 were waited for; matrix products, arithmetic and copies ran while one was open for 0% of the time, Pallas kernels for 32%

profile of v4, /device:TPU:15, one launch (start us, length us, event | category | flops | bytes accessed | tf_op | source)
XLA Modules:
  0.0 265.7 jit_solution(14227571162868482106)
XLA Ops:
  0.0 12.4 %destripe.1 = f32[16,4,2,64,128]{4,3,2,1,0:T(8,128)} custom-call(f32[2,1,256,2048]{3,2,1,0:T(8,128)} %raw_in.1, bf16[2,256,256]{2,1,0:T(8,128)(2,1)} %constant.35.clone.across_in, bf16[2,256,3328]{2,1,0:T(8,128)(2,1)} %constant.36.clone.along_in), custom_call_target="tpu_custom_call" | custom-call | tf_op jit(solution)/shard_map/destripe/pallas_call | solution.py:200
  12.4 11.1 %all-to-all-start = ((f32[128,64,128]{2,1,0:T(8,128)}), f32[128,64,128]{2,1,0:T(8,128)}, u32[]{:S(2)}, u32[]{:S(2)}) async-start(f32[128,64,128]{2,1,0:T(8,128)} %bitcast.6), calls=%async_computation | async-start | bytes 8388608 | tf_op jit(solution)/shard_map/all_to_all | solution.py:482
  23.8 1.4 tables.1
  25.2 47.5 %all-to-all-done.got = f32[128,64,128]{2,1,0:T(8,128)} async-done(((f32[128,64,128]{2,1,0:T(8,128)}), f32[128,64,128]{2,1,0:T(8,128)}, u32[]{:S(2)}, u32[]{:S(2)}) %all-to-all-start) | async-done | bytes 4194336 | tf_op jit(solution)/shard_map/all_to_all | solution.py:482
  72.7 5.7 %arrive_0.1 = (f32[16,256,128]{2,1,0:T(8,128)S(1)}, f32[15,256,128]{2,1,0:T(8,128)}, f32[1,256,128]{2,1,0:T(8,128)S(1)}) custom-call(f32[128,64,128]{2,1,0:T(8,128)} %all-to-all-done.got, bf16[256,256]{1,0:T(8,128)(2,1)S(1)} %get-tuple-element.29.z_table, bf16[256,768]{1,0:T(8,128)(2,1)S(1)} %get-tuple-element.30.x_table), custom_call_target="tpu_custom_call" | custom-call | tf_op jit(solution)/shard_map/arrive_0/pallas_call | solution.py:318
  78.4 1.1 collective-permute-start.1
  79.5 5.7 %arrive_1.1 = (f32[16,256,128]{2,1,0:T(8,128)S(1)}, f32[15,256,128]{2,1,0:T(8,128)}, f32[1,256,128]{2,1,0:T(8,128)S(1)}) custom-call(f32[128,64,128]{2,1,0:T(8,128)} %all-to-all-done.got, bf16[256,256]{1,0:T(8,128)(2,1)S(1)} %get-tuple-element.29.z_table, bf16[256,768]{1,0:T(8,128)(2,1)S(1)} %get-tuple-element.30.x_table), custom_call_target="tpu_custom_call" | custom-call | tf_op jit(solution)/shard_map/arrive_1/pallas_call | solution.py:318
  85.2 1.3 copy-done
  86.5 1.0 collective-permute-start
  88.2 6.1 %own_lines_1.4.partial = f32[16,256,128]{2,1,0:T(8,128)S(1)} custom-call(f32[3,31]{1,0:T(4,128)S(1)} %bitcast_divide_fusion.taps, f32[15,256,128]{2,1,0:T(8,128)} %get-tuple-element.31.low, f32[1,256,128]{2,1,0:T(8,128)S(1)} %get-tuple-element.32.low_mid, f32[1,256,128]{2,1,0:T(8,128)S(1)} %get-tuple-element.33.high_mid, f32[15,256,128]{2,1,0:T(8,128)} %get-tuple-element.34.high), custom_call_target="tpu_custom_call" | custom-call | flops 4000000000 | bytes 1000000 | tf_op jit(solution)/shard_map/own_lines_1/pallas_call | solution.py:357
  94.2 6.2 %own_lines_0.4.partial = f32[16,256,128]{2,1,0:T(8,128)S(1)} custom-call(f32[3,31]{1,0:T(4,128)S(1)} %bitcast_divide_fusion.taps, f32[15,256,128]{2,1,0:T(8,128)} %get-tuple-element.31.low, f32[1,256,128]{2,1,0:T(8,128)S(1)} %get-tuple-element.32.low_mid, f32[1,256,128]{2,1,0:T(8,128)S(1)} %get-tuple-element.33.high_mid, f32[15,256,128]{2,1,0:T(8,128)} %get-tuple-element.34.high), custom_call_target="tpu_custom_call" | custom-call | flops 4000000000 | bytes 1000000 | tf_op jit(solution)/shard_map/own_lines_0/pallas_call | solution.py:357
  100.4 3.0 %collective-permute-done.1.halo = f32[15,256,128]{2,1,0:T(8,128)} collective-permute-done((f32[15,256,128]{2,1,0:T(8,128)}, f32[15,256,128]{2,1,0:T(8,128)}, u32[]{:S(2)}, u32[]{:S(2)}) %collective-permute-start.1) | collective-permute-done | bytes 1966112 | tf_op jit(solution)/shard_map/ppermute | solution.py:487
  103.4 5.5 %ratio_step_1.2 = (f32[15,256,128]{2,1,0:T(8,128)S(1)}, f32[1,256,128]{2,1,0:T(8,128)S(1)}) custom-call(f32[3,31]{1,0:T(4,128)S(1)} %bitcast_divide_fusion.taps, s32[20]{0:T(128)S(1)} %dynamic-slice_bitcast_fusion.meta, f32[16,256,128]{2,1,0:T(8,128)S(1)} %own_lines_1.4.partial, f32[15,256,128]{2,1,0:T(8,128)} %collective-permute-done.1.halo, ...), custom_call_target="tpu_custom_call" | custom-call | tf_op jit(solution)/shard_map/ratio_step_1/pallas_call | solution.py:406
  109.4 5.3 %ratio_step_0.2 = (f32[15,256,128]{2,1,0:T(8,128)S(1)}, f32[1,256,128]{2,1,0:T(8,128)S(1)}) custom-call(f32[3,31]{1,0:T(4,128)S(1)} %bitcast_divide_fusion.taps, s32[20]{0:T(128)S(1)} %dynamic-slice_bitcast_fusion.meta, f32[16,256,128]{2,1,0:T(8,128)S(1)} %own_lines_0.4.partial, f32[15,256,128]{2,1,0:T(8,128)} %collective-permute-done.halo, ...), custom_call_target="tpu_custom_call" | custom-call | tf_op jit(solution)/shard_map/ratio_step_0/pallas_call | solution.py:406
  114.7 1.6 collective-permute-start.3
  116.3 4.5 %own_lines_1.5.partial = f32[16,256,128]{2,1,0:T(8,128)S(1)} custom-call(f32[3,31]{1,0:T(4,128)S(1)} %bitcast_divide_fusion.taps, f32[15,256,128]{2,1,0:T(8,128)S(1)} %get-tuple-element.38.low, f32[1,256,128]{2,1,0:T(8,128)S(1)} %get-tuple-element.39.low_mid, f32[1,256,128]{2,1,0:T(8,128)S(1)} %get-tuple-element.41.high_mid, ...), custom_call_target="tpu_custom_call" | custom-call | flops 4000000000 | bytes 1000000 | tf_op jit(solution)/shard_map/own_lines_1/pallas_call | solution.py:357
  120.8 4.4 %own_lines_0.5.partial = f32[16,256,128]{2,1,0:T(8,128)S(1)} custom-call(f32[3,31]{1,0:T(4,128)S(1)} %bitcast_divide_fusion.taps, f32[15,256,128]{2,1,0:T(8,128)S(1)} %get-tuple-element.38.low, f32[1,256,128]{2,1,0:T(8,128)S(1)} %get-tuple-element.39.low_mid, f32[1,256,128]{2,1,0:T(8,128)S(1)} %get-tuple-element.41.high_mid, ...), custom_call_target="tpu_custom_call" | custom-call | flops 4000000000 | bytes 1000000 | tf_op jit(solution)/shard_map/own_lines_0/pallas_call | solution.py:357
  125.2 5.4 %collective-permute-done.2.halo = f32[15,256,128]{2,1,0:T(8,128)S(1)} collective-permute-done((f32[15,256,128]{2,1,0:T(8,128)S(1)}, f32[15,256,128]{2,1,0:T(8,128)S(1)}, u32[]{:S(2)}, u32[]{:S(2)}) %collective-permute-start.2) | collective-permute-done | bytes 1966112 | tf_op jit(solution)/shard_map/ppermute | solution.py:487
  130.6 4.1 %estimate_step_0.1 = (f32[16,256,128]{2,1,0:T(8,128)S(1)}, f32[15,256,128]{2,1,0:T(8,128)S(1)}, f32[1,256,128]{2,1,0:T(8,128)S(1)}) custom-call(f32[3,31]{1,0:T(4,128)S(1)} %bitcast_divide_fusion.taps, s32[20]{0:T(128)S(1)} %dynamic-slice_bitcast_fusion.meta, f32[16,256,128]{2,1,0:T(8,128)S(1)} %own_lines_0.5.partial, ...), custom_call_target="tpu_custom_call" | custom-call | tf_op jit(solution)/shard_map/estimate_step_0/pallas_call | solution.py:406
  134.7 1.8 collective-permute-start.5
  136.5 3.1 %collective-permute-done.3.halo = f32[15,256,128]{2,1,0:T(8,128)S(1)} collective-permute-done((f32[15,256,128]{2,1,0:T(8,128)S(1)}, f32[15,256,128]{2,1,0:T(8,128)S(1)}, u32[]{:S(2)}, u32[]{:S(2)}) %collective-permute-start.3) | collective-permute-done | bytes 1966112 | tf_op jit(solution)/shard_map/ppermute | solution.py:487
  139.6 4.2 %estimate_step_1.1 = (f32[16,256,128]{2,1,0:T(8,128)S(1)}, f32[15,256,128]{2,1,0:T(8,128)S(1)}, f32[1,256,128]{2,1,0:T(8,128)S(1)}) custom-call(f32[3,31]{1,0:T(4,128)S(1)} %bitcast_divide_fusion.taps, s32[20]{0:T(128)S(1)} %dynamic-slice_bitcast_fusion.meta, f32[16,256,128]{2,1,0:T(8,128)S(1)} %own_lines_1.5.partial, ...), custom_call_target="tpu_custom_call" | custom-call | tf_op jit(solution)/shard_map/estimate_step_1/pallas_call | solution.py:406
  143.9 4.5 %own_lines_1.6.partial = f32[16,256,128]{2,1,0:T(8,128)S(1)} custom-call(f32[3,31]{1,0:T(4,128)S(1)} %bitcast_divide_fusion.taps, f32[15,256,128]{2,1,0:T(8,128)S(1)} %get-tuple-element.43.low, f32[1,256,128]{2,1,0:T(8,128)S(1)} %get-tuple-element.44.low_mid, f32[1,256,128]{2,1,0:T(8,128)S(1)} %get-tuple-element.45.high_mid, ...), custom_call_target="tpu_custom_call" | custom-call | flops 4000000000 | bytes 1000000 | tf_op jit(solution)/shard_map/own_lines_1/pallas_call | solution.py:357
  148.3 4.4 %own_lines_0.6.partial = f32[16,256,128]{2,1,0:T(8,128)S(1)} custom-call(f32[3,31]{1,0:T(4,128)S(1)} %bitcast_divide_fusion.taps, f32[15,256,128]{2,1,0:T(8,128)S(1)} %get-tuple-element.43.low, f32[1,256,128]{2,1,0:T(8,128)S(1)} %get-tuple-element.44.low_mid, f32[1,256,128]{2,1,0:T(8,128)S(1)} %get-tuple-element.45.high_mid, ...), custom_call_target="tpu_custom_call" | custom-call | flops 4000000000 | bytes 1000000 | tf_op jit(solution)/shard_map/own_lines_0/pallas_call | solution.py:357
  152.8 8.1 %collective-permute-done.5.halo = f32[15,256,128]{2,1,0:T(8,128)S(1)} collective-permute-done((f32[15,256,128]{2,1,0:T(8,128)S(1)}, f32[15,256,128]{2,1,0:T(8,128)S(1)}, u32[]{:S(2)}, u32[]{:S(2)}) %collective-permute-start.5) | collective-permute-done | bytes 1966112 | tf_op jit(solution)/shard_map/ppermute | solution.py:487
  160.9 4.5 %ratio_step_1.3 = (f32[15,256,128]{2,1,0:T(8,128)S(1)}, f32[1,256,128]{2,1,0:T(8,128)S(1)}) custom-call(f32[3,31]{1,0:T(4,128)S(1)} %bitcast_divide_fusion.taps, s32[20]{0:T(128)S(1)} %dynamic-slice_bitcast_fusion.meta, f32[16,256,128]{2,1,0:T(8,128)S(1)} %own_lines_1.6.partial, f32[15,256,128]{2,1,0:T(8,128)S(1)} %collective-permute-done.5.halo, ...), custom_call_target="tpu_custom_call" | custom-call | tf_op jit(solution)/shard_map/ratio_step_1/pallas_call | solution.py:406
  165.5 4.3 %ratio_step_0.3 = (f32[15,256,128]{2,1,0:T(8,128)S(1)}, f32[1,256,128]{2,1,0:T(8,128)S(1)}) custom-call(f32[3,31]{1,0:T(4,128)S(1)} %bitcast_divide_fusion.taps, s32[20]{0:T(128)S(1)} %dynamic-slice_bitcast_fusion.meta, f32[16,256,128]{2,1,0:T(8,128)S(1)} %own_lines_0.6.partial, f32[15,256,128]{2,1,0:T(8,128)S(1)} %collective-permute-done.4.halo, ...), custom_call_target="tpu_custom_call" | custom-call | tf_op jit(solution)/shard_map/ratio_step_0/pallas_call | solution.py:406
  169.9 1.4 collective-permute-start.7
  171.3 4.5 %own_lines_1.7.refs_1_ = f32[16,256,128]{2,1,0:T(8,128)S(1)} custom-call(f32[3,31]{1,0:T(4,128)S(1)} %bitcast_divide_fusion.taps, f32[15,256,128]{2,1,0:T(8,128)S(1)} %get-tuple-element.47.low, f32[1,256,128]{2,1,0:T(8,128)S(1)} %get-tuple-element.48.low_mid, f32[1,256,128]{2,1,0:T(8,128)S(1)} %get-tuple-element.49.high_mid, ...), custom_call_target="tpu_custom_call" | custom-call | flops 4000000000 | bytes 1000000 | tf_op jit(solution)/shard_map/own_lines_1/pallas_call | solution.py:357
  175.8 4.4 %own_lines_0.7.refs_0_ = f32[16,256,128]{2,1,0:T(8,128)S(1)} custom-call(f32[3,31]{1,0:T(4,128)S(1)} %bitcast_divide_fusion.taps, f32[15,256,128]{2,1,0:T(8,128)S(1)} %get-tuple-element.47.low, f32[1,256,128]{2,1,0:T(8,128)S(1)} %get-tuple-element.48.low_mid, f32[1,256,128]{2,1,0:T(8,128)S(1)} %get-tuple-element.49.high_mid, ...), custom_call_target="tpu_custom_call" | custom-call | flops 4000000000 | bytes 1000000 | tf_op jit(solution)/shard_map/own_lines_0/pallas_call | solution.py:357
  180.3 6.8 %collective-permute-done.6.refs_2_ = f32[15,256,128]{2,1,0:T(8,128)S(1)} collective-permute-done((f32[15,256,128]{2,1,0:T(8,128)S(1)}, f32[15,256,128]{2,1,0:T(8,128)S(1)}, u32[]{:S(2)}, u32[]{:S(2)}) %collective-permute-start.6) | collective-permute-done | bytes 1966112 | tf_op jit(solution)/shard_map/ppermute | solution.py:487
  187.1 7.5 %collective-permute-done.7.refs_3_ = f32[15,256,128]{2,1,0:T(8,128)S(1)} collective-permute-done((f32[15,256,128]{2,1,0:T(8,128)S(1)}, f32[15,256,128]{2,1,0:T(8,128)S(1)}, u32[]{:S(2)}, u32[]{:S(2)}) %collective-permute-start.7) | collective-permute-done | bytes 1966112 | tf_op jit(solution)/shard_map/ppermute | solution.py:487
  195.7 0.9 last_step.14
  197.9 4.5 %collective-permute-start.13 = (f32[32,32,128]{2,1,0:T(8,128)S(1)}, f32[32,32,128]{2,1,0:T(8,128)S(1)}, u32[]{:S(2)}, u32[]{:S(2)}) collective-permute-start(f32[32,32,128]{2,1,0:T(8,128)S(1)} %last_step.13), channel_id=1, source_target_pairs={{0,2},{8,6},{2,4},{10,0},{4,15},{12,11},{6,9},{14,13},{22,16},{30,... | collective-permute-start | bytes 1572872 | tf_op jit(solution)/shard_map/ppermute | solution.py:515
  203.3 2.1 collective-permute-start.12
  205.4 0.9 last_step.11
  206.4 3.2 %collective-permute-start.11 = (f32[32,32,128]{2,1,0:T(8,128)S(1)}, f32[32,32,128]{2,1,0:T(8,128)S(1)}, u32[]{:S(2)}, u32[]{:S(2)}) collective-permute-start(f32[32,32,128]{2,1,0:T(8,128)S(1)} %last_step.11), channel_id=1, source_target_pairs={{0,7},{8,3},{2,1},{10,5},{4,10},{12,14},{6,12},{14,8},{22,21},{30,... | collective-permute-start | bytes 1572872 | tf_op jit(solution)/shard_map/ppermute | solution.py:515
  210.5 0.9 last_step.9
  211.5 0.9 last_step.8
  212.4 1.9 collective-permute-start.10
  214.4 7.3 %collective-permute-done.14.refs_2_ = f32[32,32,128]{2,1,0:T(8,128)S(1)} collective-permute-done((f32[32,32,128]{2,1,0:T(8,128)S(1)}, f32[32,32,128]{2,1,0:T(8,128)S(1)}, u32[]{:S(2)}, u32[]{:S(2)}) %collective-permute-start.14) | collective-permute-done | bytes 524320 | tf_op jit(solution)/shard_map/ppermute | solution.py:515
  221.7 4.6 %collective-permute-done.13.refs_1_ = f32[32,32,128]{2,1,0:T(8,128)S(1)} collective-permute-done((f32[32,32,128]{2,1,0:T(8,128)S(1)}, f32[32,32,128]{2,1,0:T(8,128)S(1)}, u32[]{:S(2)}, u32[]{:S(2)}) %collective-permute-start.13) | collective-permute-done | bytes 524320 | tf_op jit(solution)/shard_map/ppermute | solution.py:515
  226.3 2.9 %collective-permute-start.8 = (f32[32,32,128]{2,1,0:T(8,128)S(1)}, f32[32,32,128]{2,1,0:T(8,128)S(1)}, u32[]{:S(2)}, u32[]{:S(2)}) collective-permute-start(f32[32,32,128]{2,1,0:T(8,128)S(1)} %last_step.8), channel_id=1, source_target_pairs={{0,1},{8,5},{2,3},{10,7},{4,12},{12,8},{6,14},{14,10},{22,23},{30,... | collective-permute-start | bytes 1572872 | tf_op jit(solution)/shard_map/ppermute | solution.py:515
  230.0 4.3 %leave_0.1.refs_4_ = f32[8192,128]{1,0:T(8,128)} custom-call(s32[20]{0:T(128)S(1)} %dynamic-slice_bitcast_fusion.meta, f32[32,32,128]{2,1,0:T(8,128)S(1)} %collective-permute-done.12.refs_0_, f32[32,32,128]{2,1,0:T(8,128)S(1)} %collective-permute-done.13.refs_1_, f32[32,32,128]{2,1,0:T(8,128)S(1)} %collective-permute-done.14.refs_2_, ...), custom_call_target="tpu_custom_call" | custom-call | tf_op jit(solution)/shard_map/leave_0/pallas_call | solution.py:462
  234.7 9.5 %collective-permute-done.10.refs_2_ = f32[32,32,128]{2,1,0:T(8,128)S(1)} collective-permute-done((f32[32,32,128]{2,1,0:T(8,128)S(1)}, f32[32,32,128]{2,1,0:T(8,128)S(1)}, u32[]{:S(2)}, u32[]{:S(2)}) %collective-permute-start.10) | collective-permute-done | bytes 524320 | tf_op jit(solution)/shard_map/ppermute | solution.py:515
  244.2 10.2 %collective-permute-done.9.refs_1_ = f32[32,32,128]{2,1,0:T(8,128)S(1)} collective-permute-done((f32[32,32,128]{2,1,0:T(8,128)S(1)}, f32[32,32,128]{2,1,0:T(8,128)S(1)}, u32[]{:S(2)}, u32[]{:S(2)}) %collective-permute-start.9) | collective-permute-done | bytes 524320 | tf_op jit(solution)/shard_map/ppermute | solution.py:515
  254.4 6.8 %collective-permute-done.8.refs_0_ = f32[32,32,128]{2,1,0:T(8,128)S(1)} collective-permute-done((f32[32,32,128]{2,1,0:T(8,128)S(1)}, f32[32,32,128]{2,1,0:T(8,128)S(1)}, u32[]{:S(2)}, u32[]{:S(2)}) %collective-permute-start.8) | collective-permute-done | bytes 524320 | tf_op jit(solution)/shard_map/ppermute | solution.py:515
  261.2 4.3 %leave_1.1 = f32[8192,128]{1,0:T(8,128)} custom-call(s32[20]{0:T(128)S(1)} %dynamic-slice_bitcast_fusion.meta, f32[32,32,128]{2,1,0:T(8,128)S(1)} %collective-permute-done.8.refs_0_, f32[32,32,128]{2,1,0:T(8,128)S(1)} %collective-permute-done.9.refs_1_, f32[32,32,128]{2,1,0:T(8,128)S(1)} %collective-permute-done.10.refs_2_, ...), custom_call_target="tpu_custom_call", output_to_operand_aliasing={{}: (5, {})} | custom-call | tf_op jit(solution)/shard_map/leave_1/pallas_call | solution.py:462
  (23 shorter events, 6.9 us)
Async XLA Ops:
  12.4 11.2 %copy-start.2 = (f32[3,2,31]{2,1,0:T(2,128)S(1)}, f32[3,2,31]{2,1,0:T(2,128)}, u32[]{:S(2)}) copy-start(f32[3,2,31]{2,1,0:T(2,128)} %param.6) | copy-start | bytes 2236
  12.4 60.3 %all-to-all-start = ((f32[128,64,128]{2,1,0:T(8,128)}), f32[128,64,128]{2,1,0:T(8,128)}, u32[]{:S(2)}, u32[]{:S(2)}) async-start(f32[128,64,128]{2,1,0:T(8,128)} %bitcast.6), calls=%async_computation | async-start | bytes 8388608 | tf_op jit(solution)/shard_map/all_to_all | solution.py:482
  78.4 25.0 %collective-permute-start.1 = (f32[15,256,128]{2,1,0:T(8,128)}, f32[15,256,128]{2,1,0:T(8,128)}, u32[]{:S(2)}, u32[]{:S(2)}) collective-permute-start(f32[15,256,128]{2,1,0:T(8,128)} %get-tuple-element.31.low), channel_id=1, source_target_pairs={{8,0},{2,8},{10,2},{4,10},{12,4},{6,12},{14,6},{22,14},{30,22},{20... | collective-permute-start | bytes 5898248 | tf_op jit(solution)/shard_map/ppermute | solution.py:487
  85.2 1.3 copy-start
  86.5 22.9 %collective-permute-start = (f32[15,256,128]{2,1,0:T(8,128)}, f32[15,256,128]{2,1,0:T(8,128)}, u32[]{:S(2)}, u32[]{:S(2)}) collective-permute-start(f32[15,256,128]{2,1,0:T(8,128)} %get-tuple-element.34.high), channel_id=1, source_target_pairs={{0,8},{8,2},{2,10},{10,4},{4,12},{12,6},{6,14},{14,22},{22,30},{30... | collective-permute-start | bytes 5898248 | tf_op jit(solution)/shard_map/ppermute | solution.py:487
  94.2 9.2 %copy-start.1 = (f32[16,256,128]{2,1,0:T(8,128)S(1)}, f32[16,256,128]{2,1,0:T(8,128)}, u32[]{:S(2)}) copy-start(f32[16,256,128]{2,1,0:T(8,128)} %copy-done) | copy-start | bytes 6291460
  108.9 21.6 %collective-permute-start.2 = (f32[15,256,128]{2,1,0:T(8,128)S(1)}, f32[15,256,128]{2,1,0:T(8,128)S(1)}, u32[]{:S(2)}, u32[]{:S(2)}) collective-permute-start(f32[15,256,128]{2,1,0:T(8,128)S(1)} %get-tuple-element.42.high), channel_id=1, source_target_pairs={{0,8},{8,2},{2,10},{10,4},{4,12},{12,6},{6,14},{14,22},{22,30},{30... | collective-permute-start | bytes 5898248 | tf_op jit(solution)/shard_map/ppermute | solution.py:487
  114.7 24.9 %collective-permute-start.3 = (f32[15,256,128]{2,1,0:T(8,128)S(1)}, f32[15,256,128]{2,1,0:T(8,128)S(1)}, u32[]{:S(2)}, u32[]{:S(2)}) collective-permute-start(f32[15,256,128]{2,1,0:T(8,128)S(1)} %get-tuple-element.38.low), channel_id=1, source_target_pairs={{8,0},{2,8},{10,2},{4,10},{12,4},{6,12},{14,6},{22,14},{30,22},{20... | collective-permute-start | bytes 5898248 | tf_op jit(solution)/shard_map/ppermute | solution.py:487
  134.7 26.3 %collective-permute-start.5 = (f32[15,256,128]{2,1,0:T(8,128)S(1)}, f32[15,256,128]{2,1,0:T(8,128)S(1)}, u32[]{:S(2)}, u32[]{:S(2)}) collective-permute-start(f32[15,256,128]{2,1,0:T(8,128)S(1)} %get-tuple-element.43.low), channel_id=1, source_target_pairs={{8,0},{2,8},{10,2},{4,10},{12,4},{6,12},{14,6},{22,14},{30,22},{20... | collective-permute-start | bytes 5898248 | tf_op jit(solution)/shard_map/ppermute | solution.py:487
  143.8 21.8 %collective-permute-start.4 = (f32[15,256,128]{2,1,0:T(8,128)S(1)}, f32[15,256,128]{2,1,0:T(8,128)S(1)}, u32[]{:S(2)}, u32[]{:S(2)}) collective-permute-start(f32[15,256,128]{2,1,0:T(8,128)S(1)} %get-tuple-element.46.high), channel_id=1, source_target_pairs={{0,8},{8,2},{2,10},{10,4},{4,12},{12,6},{6,14},{14,22},{22,30},{30... | collective-permute-start | bytes 5898248 | tf_op jit(solution)/shard_map/ppermute | solution.py:487
  165.5 21.6 %collective-permute-start.6 = (f32[15,256,128]{2,1,0:T(8,128)S(1)}, f32[15,256,128]{2,1,0:T(8,128)S(1)}, u32[]{:S(2)}, u32[]{:S(2)}) collective-permute-start(f32[15,256,128]{2,1,0:T(8,128)S(1)} %get-tuple-element.50.high), channel_id=1, source_target_pairs={{0,8},{8,2},{2,10},{10,4},{4,12},{12,6},{6,14},{14,22},{22,30},{30... | collective-permute-start | bytes 5898248 | tf_op jit(solution)/shard_map/ppermute | solution.py:487
  169.9 24.7 %collective-permute-start.7 = (f32[15,256,128]{2,1,0:T(8,128)S(1)}, f32[15,256,128]{2,1,0:T(8,128)S(1)}, u32[]{:S(2)}, u32[]{:S(2)}) collective-permute-start(f32[15,256,128]{2,1,0:T(8,128)S(1)} %get-tuple-element.47.low), channel_id=1, source_target_pairs={{8,0},{2,8},{10,2},{4,10},{12,4},{6,12},{14,6},{22,14},{30,22},{20... | collective-permute-start | bytes 5898248 | tf_op jit(solution)/shard_map/ppermute | solution.py:487
  195.6 16.9 %collective-permute-start.15 = (f32[32,32,128]{2,1,0:T(8,128)S(1)}, f32[32,32,128]{2,1,0:T(8,128)S(1)}, u32[]{:S(2)}, u32[]{:S(2)}) collective-permute-start(f32[32,32,128]{2,1,0:T(8,128)S(1)} %last_step.15), channel_id=1, source_target_pairs={{0,6},{8,2},{2,0},{10,4},{4,11},{12,15},{6,13},{14,9},{22,20},{30,... | collective-permute-start | bytes 1572872 | tf_op jit(solution)/shard_map/ppermute | solution.py:515
  196.6 25.1 %collective-permute-start.14 = (f32[32,32,128]{2,1,0:T(8,128)S(1)}, f32[32,32,128]{2,1,0:T(8,128)S(1)}, u32[]{:S(2)}, u32[]{:S(2)}) collective-permute-start(f32[32,32,128]{2,1,0:T(8,128)S(1)} %last_step.14), channel_id=1, source_target_pairs={{0,4},{8,0},{2,6},{10,2},{4,9},{12,13},{6,11},{14,15},{22,18},{30,... | collective-permute-start | bytes 1572872 | tf_op jit(solution)/shard_map/ppermute | solution.py:515
  197.9 28.4 %collective-permute-start.13 = (f32[32,32,128]{2,1,0:T(8,128)S(1)}, f32[32,32,128]{2,1,0:T(8,128)S(1)}, u32[]{:S(2)}, u32[]{:S(2)}) collective-permute-start(f32[32,32,128]{2,1,0:T(8,128)S(1)} %last_step.13), channel_id=1, source_target_pairs={{0,2},{8,6},{2,4},{10,0},{4,15},{12,11},{6,9},{14,13},{22,16},{30,... | collective-permute-start | bytes 1572872 | tf_op jit(solution)/shard_map/ppermute | solution.py:515
  203.3 26.7 %collective-permute-start.12 = (f32[32,32,128]{2,1,0:T(8,128)S(1)}, f32[32,32,128]{2,1,0:T(8,128)S(1)}, u32[]{:S(2)}, u32[]{:S(2)}) collective-permute-start(f32[32,32,128]{2,1,0:T(8,128)S(1)} %last_step.12), channel_id=1, source_target_pairs={{0,0},{8,4},{2,2},{10,6},{4,13},{12,9},{6,15},{14,11},{22,22},{30,... | collective-permute-start | bytes 1572872 | tf_op jit(solution)/shard_map/ppermute | solution.py:515
  206.4 28.3 %collective-permute-start.11 = (f32[32,32,128]{2,1,0:T(8,128)S(1)}, f32[32,32,128]{2,1,0:T(8,128)S(1)}, u32[]{:S(2)}, u32[]{:S(2)}) collective-permute-start(f32[32,32,128]{2,1,0:T(8,128)S(1)} %last_step.11), channel_id=1, source_target_pairs={{0,7},{8,3},{2,1},{10,5},{4,10},{12,14},{6,12},{14,8},{22,21},{30,... | collective-permute-start | bytes 1572872 | tf_op jit(solution)/shard_map/ppermute | solution.py:515
  212.4 31.8 %collective-permute-start.10 = (f32[32,32,128]{2,1,0:T(8,128)S(1)}, f32[32,32,128]{2,1,0:T(8,128)S(1)}, u32[]{:S(2)}, u32[]{:S(2)}) collective-permute-start(f32[32,32,128]{2,1,0:T(8,128)S(1)} %last_step.10), channel_id=1, source_target_pairs={{0,5},{8,1},{2,7},{10,3},{4,8},{12,12},{6,10},{14,14},{22,19},{30,... | collective-permute-start | bytes 1572872 | tf_op jit(solution)/shard_map/ppermute | solution.py:515
  221.7 32.7 %collective-permute-start.9 = (f32[32,32,128]{2,1,0:T(8,128)S(1)}, f32[32,32,128]{2,1,0:T(8,128)S(1)}, u32[]{:S(2)}, u32[]{:S(2)}) collective-permute-start(f32[32,32,128]{2,1,0:T(8,128)S(1)} %last_step.9), channel_id=1, source_target_pairs={{0,3},{8,7},{2,5},{10,1},{4,14},{12,10},{6,8},{14,12},{22,17},{30,... | collective-permute-start | bytes 1572872 | tf_op jit(solution)/shard_map/ppermute | solution.py:515
  226.3 34.9 %collective-permute-start.8 = (f32[32,32,128]{2,1,0:T(8,128)S(1)}, f32[32,32,128]{2,1,0:T(8,128)S(1)}, u32[]{:S(2)}, u32[]{:S(2)}) collective-permute-start(f32[32,32,128]{2,1,0:T(8,128)S(1)} %last_step.8), channel_id=1, source_target_pairs={{0,1},{8,5},{2,3},{10,7},{4,12},{12,8},{6,14},{14,10},{22,23},{30,... | collective-permute-start | bytes 1572872 | tf_op jit(solution)/shard_map/ppermute | solution.py:515

commit v5 on v4

--- a/solution.py
+++ b/solution.py
@@ -46,7 +46,7 @@
 
 def final_target(channel, block, j):
     x, _, _, core = place(block)
-    xd = (x + 2 * core + (j & 3)) % 4
+    xd = (x + 2 * core + (1, 3, 0, 2)[j & 3]) % 4
     x8 = 2 * xd + (channel ^ (j >> 2) ^ ((block >> 2) & 1))
     return x8, (block >> 2) * 8 + x8
 

time: 266 us -> 260 us (0.977)
  the two profiles are of different devices: /device:TPU:15 before, /device:TPU:124 now
where the time goes in v5:
time: 260 us; the launch traced here: 259 us
  waiting for transfers between devices  118 us (45%)
  Pallas kernels  108 us (42%)
  starting transfers between devices  30.3 us (12%)
    all_to_all x1, waiting for transfers between devices, local(): got = lax.all_to_all(blocks, AXES, split_axis=0, concat_axis=0, tiled=True)  44.1 us
    pallas_call x8, Pallas kernels, own_lines(): calls(functools.partial(own_kernel, way, side), f'own_lines_{side}', ((HL...  39 us
    ppermute x8, waiting for transfers between devices, local(): parts.append(lax.ppermute(part, AXES, FINAL[j]))  38.6 us
    ppermute x8, waiting for transfers between devices, exchange(): lax.ppermute(halves[side][0], AXES, DOWN if side == 0 else UP)  35.5 us
    pallas_call x6, Pallas kernels, step(): calls(functools.partial(step_kernel, ratio, side), f'ratio_step_{side}' i...  28 us
    ppermute x8, starting transfers between devices, local(): parts.append(lax.ppermute(part, AXES, FINAL[j]))  15 us
    pallas_call x1, Pallas kernels, destripe(): pl.pallas_call(destripe_kernel, in_specs=[anywhere] * 3, out_specs=anywhe...  12.4 us
    pallas_call x2, Pallas kernels, arrive(): calls(functools.partial(arrive_kernel, side), f'arrive_{side}', ((HL, NX,...  11.3 us
  transfers between devices with their start and end apart: 17, of which 11 were waited for; matrix products, arithmetic and copies ran while one was open for 0% of the time, Pallas kernels for 33%

profile of v5, /device:TPU:124, one launch (start us, length us, event | category | flops | bytes accessed | tf_op | source)
XLA Modules:
  0.0 259.4 jit_solution(3013723701292064755)
XLA Ops:
  0.0 12.4 %destripe.1 = f32[16,4,2,64,128]{4,3,2,1,0:T(8,128)} custom-call(f32[2,1,256,2048]{3,2,1,0:T(8,128)} %raw_in.1, bf16[2,256,256]{2,1,0:T(8,128)(2,1)} %constant.35.clone.across_in, bf16[2,256,3328]{2,1,0:T(8,128)(2,1)} %constant.36.clone.along_in), custom_call_target="tpu_custom_call" | custom-call | tf_op jit(solution)/shard_map/destripe/pallas_call | solution.py:200
  12.4 10.2 %all-to-all-start = ((f32[128,64,128]{2,1,0:T(8,128)}), f32[128,64,128]{2,1,0:T(8,128)}, u32[]{:S(2)}, u32[]{:S(2)}) async-start(f32[128,64,128]{2,1,0:T(8,128)} %bitcast.6), calls=%async_computation | async-start | bytes 8388608 | tf_op jit(solution)/shard_map/all_to_all | solution.py:482
  22.8 1.4 tables.1
  24.2 44.1 %all-to-all-done.got = f32[128,64,128]{2,1,0:T(8,128)} async-done(((f32[128,64,128]{2,1,0:T(8,128)}), f32[128,64,128]{2,1,0:T(8,128)}, u32[]{:S(2)}, u32[]{:S(2)}) %all-to-all-start) | async-done | bytes 4194336 | tf_op jit(solution)/shard_map/all_to_all | solution.py:482
  68.3 5.7 %arrive_0.1 = (f32[16,256,128]{2,1,0:T(8,128)S(1)}, f32[15,256,128]{2,1,0:T(8,128)}, f32[1,256,128]{2,1,0:T(8,128)S(1)}) custom-call(f32[128,64,128]{2,1,0:T(8,128)} %all-to-all-done.got, bf16[256,256]{1,0:T(8,128)(2,1)S(1)} %get-tuple-element.29.z_table, bf16[256,768]{1,0:T(8,128)(2,1)S(1)} %get-tuple-element.30.x_table), custom_call_target="tpu_custom_call" | custom-call | tf_op jit(solution)/shard_map/arrive_0/pallas_call | solution.py:318
  74.0 1.4 collective-permute-start.1
  75.4 5.7 %arrive_1.1 = (f32[16,256,128]{2,1,0:T(8,128)S(1)}, f32[15,256,128]{2,1,0:T(8,128)}, f32[1,256,128]{2,1,0:T(8,128)S(1)}) custom-call(f32[128,64,128]{2,1,0:T(8,128)} %all-to-all-done.got, bf16[256,256]{1,0:T(8,128)(2,1)S(1)} %get-tuple-element.29.z_table, bf16[256,768]{1,0:T(8,128)(2,1)S(1)} %get-tuple-element.30.x_table), custom_call_target="tpu_custom_call" | custom-call | tf_op jit(solution)/shard_map/arrive_1/pallas_call | solution.py:318
  81.0 1.3 copy-done
  83.0 6.1 %own_lines_1.4.partial = f32[16,256,128]{2,1,0:T(8,128)S(1)} custom-call(f32[3,31]{1,0:T(4,128)S(1)} %bitcast_divide_fusion.taps, f32[15,256,128]{2,1,0:T(8,128)} %get-tuple-element.31.low, f32[1,256,128]{2,1,0:T(8,128)S(1)} %get-tuple-element.32.low_mid, f32[1,256,128]{2,1,0:T(8,128)S(1)} %get-tuple-element.33.high_mid, f32[15,256,128]{2,1,0:T(8,128)} %get-tuple-element.34.high), custom_call_target="tpu_custom_call" | custom-call | flops 4000000000 | bytes 1000000 | tf_op jit(solution)/shard_map/own_lines_1/pallas_call | solution.py:357
  89.1 6.2 %own_lines_0.4.partial = f32[16,256,128]{2,1,0:T(8,128)S(1)} custom-call(f32[3,31]{1,0:T(4,128)S(1)} %bitcast_divide_fusion.taps, f32[15,256,128]{2,1,0:T(8,128)} %get-tuple-element.31.low, f32[1,256,128]{2,1,0:T(8,128)S(1)} %get-tuple-element.32.low_mid, f32[1,256,128]{2,1,0:T(8,128)S(1)} %get-tuple-element.33.high_mid, f32[15,256,128]{2,1,0:T(8,128)} %get-tuple-element.34.high), custom_call_target="tpu_custom_call" | custom-call | flops 4000000000 | bytes 1000000 | tf_op jit(solution)/shard_map/own_lines_0/pallas_call | solution.py:357
  95.3 2.6 collective-permute-done.1.halo
  97.8 5.5 %ratio_step_1.2 = (f32[15,256,128]{2,1,0:T(8,128)S(1)}, f32[1,256,128]{2,1,0:T(8,128)S(1)}) custom-call(f32[3,31]{1,0:T(4,128)S(1)} %bitcast_divide_fusion.taps, s32[20]{0:T(128)S(1)} %dynamic-slice_bitcast_fusion.meta, f32[16,256,128]{2,1,0:T(8,128)S(1)} %own_lines_1.4.partial, f32[15,256,128]{2,1,0:T(8,128)} %collective-permute-done.1.halo, ...), custom_call_target="tpu_custom_call" | custom-call | tf_op jit(solution)/shard_map/ratio_step_1/pallas_call | solution.py:406
  103.4 1.2 collective-permute-start.2
  104.6 2.2 collective-permute-done.halo
  106.7 5.3 %ratio_step_0.2 = (f32[15,256,128]{2,1,0:T(8,128)S(1)}, f32[1,256,128]{2,1,0:T(8,128)S(1)}) custom-call(f32[3,31]{1,0:T(4,128)S(1)} %bitcast_divide_fusion.taps, s32[20]{0:T(128)S(1)} %dynamic-slice_bitcast_fusion.meta, f32[16,256,128]{2,1,0:T(8,128)S(1)} %own_lines_0.4.partial, f32[15,256,128]{2,1,0:T(8,128)} %collective-permute-done.halo, ...), custom_call_target="tpu_custom_call" | custom-call | tf_op jit(solution)/shard_map/ratio_step_0/pallas_call | solution.py:406
  112.1 4.5 %own_lines_1.5.partial = f32[16,256,128]{2,1,0:T(8,128)S(1)} custom-call(f32[3,31]{1,0:T(4,128)S(1)} %bitcast_divide_fusion.taps, f32[15,256,128]{2,1,0:T(8,128)S(1)} %get-tuple-element.38.low, f32[1,256,128]{2,1,0:T(8,128)S(1)} %get-tuple-element.39.low_mid, f32[1,256,128]{2,1,0:T(8,128)S(1)} %get-tuple-element.41.high_mid, ...), custom_call_target="tpu_custom_call" | custom-call | flops 4000000000 | bytes 1000000 | tf_op jit(solution)/shard_map/own_lines_1/pallas_call | solution.py:357
  116.6 4.4 %own_lines_0.5.partial = f32[16,256,128]{2,1,0:T(8,128)S(1)} custom-call(f32[3,31]{1,0:T(4,128)S(1)} %bitcast_divide_fusion.taps, f32[15,256,128]{2,1,0:T(8,128)S(1)} %get-tuple-element.38.low, f32[1,256,128]{2,1,0:T(8,128)S(1)} %get-tuple-element.39.low_mid, f32[1,256,128]{2,1,0:T(8,128)S(1)} %get-tuple-element.41.high_mid, ...), custom_call_target="tpu_custom_call" | custom-call | flops 4000000000 | bytes 1000000 | tf_op jit(solution)/shard_map/own_lines_0/pallas_call | solution.py:357
  121.1 6.9 %collective-permute-done.2.halo = f32[15,256,128]{2,1,0:T(8,128)S(1)} collective-permute-done((f32[15,256,128]{2,1,0:T(8,128)S(1)}, f32[15,256,128]{2,1,0:T(8,128)S(1)}, u32[]{:S(2)}, u32[]{:S(2)}) %collective-permute-start.2) | collective-permute-done | bytes 1966112 | tf_op jit(solution)/shard_map/ppermute | solution.py:487
  127.9 4.1 %estimate_step_0.1 = (f32[16,256,128]{2,1,0:T(8,128)S(1)}, f32[15,256,128]{2,1,0:T(8,128)S(1)}, f32[1,256,128]{2,1,0:T(8,128)S(1)}) custom-call(f32[3,31]{1,0:T(4,128)S(1)} %bitcast_divide_fusion.taps, s32[20]{0:T(128)S(1)} %dynamic-slice_bitcast_fusion.meta, f32[16,256,128]{2,1,0:T(8,128)S(1)} %own_lines_0.5.partial, ...), custom_call_target="tpu_custom_call" | custom-call | tf_op jit(solution)/shard_map/estimate_step_0/pallas_call | solution.py:406
  132.3 2.0 collective-permute-done.3.halo
  134.3 4.2 %estimate_step_1.1 = (f32[16,256,128]{2,1,0:T(8,128)S(1)}, f32[15,256,128]{2,1,0:T(8,128)S(1)}, f32[1,256,128]{2,1,0:T(8,128)S(1)}) custom-call(f32[3,31]{1,0:T(4,128)S(1)} %bitcast_divide_fusion.taps, s32[20]{0:T(128)S(1)} %dynamic-slice_bitcast_fusion.meta, f32[16,256,128]{2,1,0:T(8,128)S(1)} %own_lines_1.5.partial, ...), custom_call_target="tpu_custom_call" | custom-call | tf_op jit(solution)/shard_map/estimate_step_1/pallas_call | solution.py:406
  138.5 0.9 collective-permute-start.4
  139.4 4.5 %own_lines_1.6.partial = f32[16,256,128]{2,1,0:T(8,128)S(1)} custom-call(f32[3,31]{1,0:T(4,128)S(1)} %bitcast_divide_fusion.taps, f32[15,256,128]{2,1,0:T(8,128)S(1)} %get-tuple-element.43.low, f32[1,256,128]{2,1,0:T(8,128)S(1)} %get-tuple-element.44.low_mid, f32[1,256,128]{2,1,0:T(8,128)S(1)} %get-tuple-element.45.high_mid, ...), custom_call_target="tpu_custom_call" | custom-call | flops 4000000000 | bytes 1000000 | tf_op jit(solution)/shard_map/own_lines_1/pallas_call | solution.py:357
  143.9 4.4 %own_lines_0.6.partial = f32[16,256,128]{2,1,0:T(8,128)S(1)} custom-call(f32[3,31]{1,0:T(4,128)S(1)} %bitcast_divide_fusion.taps, f32[15,256,128]{2,1,0:T(8,128)S(1)} %get-tuple-element.43.low, f32[1,256,128]{2,1,0:T(8,128)S(1)} %get-tuple-element.44.low_mid, f32[1,256,128]{2,1,0:T(8,128)S(1)} %get-tuple-element.45.high_mid, ...), custom_call_target="tpu_custom_call" | custom-call | flops 4000000000 | bytes 1000000 | tf_op jit(solution)/shard_map/own_lines_0/pallas_call | solution.py:357
  148.3 7.0 %collective-permute-done.5.halo = f32[15,256,128]{2,1,0:T(8,128)S(1)} collective-permute-done((f32[15,256,128]{2,1,0:T(8,128)S(1)}, f32[15,256,128]{2,1,0:T(8,128)S(1)}, u32[]{:S(2)}, u32[]{:S(2)}) %collective-permute-start.5) | collective-permute-done | bytes 1966112 | tf_op jit(solution)/shard_map/ppermute | solution.py:487
  155.3 4.5 %ratio_step_1.3 = (f32[15,256,128]{2,1,0:T(8,128)S(1)}, f32[1,256,128]{2,1,0:T(8,128)S(1)}) custom-call(f32[3,31]{1,0:T(4,128)S(1)} %bitcast_divide_fusion.taps, s32[20]{0:T(128)S(1)} %dynamic-slice_bitcast_fusion.meta, f32[16,256,128]{2,1,0:T(8,128)S(1)} %own_lines_1.6.partial, f32[15,256,128]{2,1,0:T(8,128)S(1)} %collective-permute-done.5.halo, ...), custom_call_target="tpu_custom_call" | custom-call | tf_op jit(solution)/shard_map/ratio_step_1/pallas_call | solution.py:406
  159.9 1.2 collective-permute-start.6
  161.1 1.7 collective-permute-done.4.halo
  162.8 4.3 %ratio_step_0.3 = (f32[15,256,128]{2,1,0:T(8,128)S(1)}, f32[1,256,128]{2,1,0:T(8,128)S(1)}) custom-call(f32[3,31]{1,0:T(4,128)S(1)} %bitcast_divide_fusion.taps, s32[20]{0:T(128)S(1)} %dynamic-slice_bitcast_fusion.meta, f32[16,256,128]{2,1,0:T(8,128)S(1)} %own_lines_0.6.partial, f32[15,256,128]{2,1,0:T(8,128)S(1)} %collective-permute-done.4.halo, ...), custom_call_target="tpu_custom_call" | custom-call | tf_op jit(solution)/shard_map/ratio_step_0/pallas_call | solution.py:406
  167.2 4.5 %own_lines_1.7.refs_1_ = f32[16,256,128]{2,1,0:T(8,128)S(1)} custom-call(f32[3,31]{1,0:T(4,128)S(1)} %bitcast_divide_fusion.taps, f32[15,256,128]{2,1,0:T(8,128)S(1)} %get-tuple-element.47.low, f32[1,256,128]{2,1,0:T(8,128)S(1)} %get-tuple-element.48.low_mid, f32[1,256,128]{2,1,0:T(8,128)S(1)} %get-tuple-element.49.high_mid, ...), custom_call_target="tpu_custom_call" | custom-call | flops 4000000000 | bytes 1000000 | tf_op jit(solution)/shard_map/own_lines_1/pallas_call | solution.py:357
  171.7 4.4 %own_lines_0.7.refs_0_ = f32[16,256,128]{2,1,0:T(8,128)S(1)} custom-call(f32[3,31]{1,0:T(4,128)S(1)} %bitcast_divide_fusion.taps, f32[15,256,128]{2,1,0:T(8,128)S(1)} %get-tuple-element.47.low, f32[1,256,128]{2,1,0:T(8,128)S(1)} %get-tuple-element.48.low_mid, f32[1,256,128]{2,1,0:T(8,128)S(1)} %get-tuple-element.49.high_mid, ...), custom_call_target="tpu_custom_call" | custom-call | flops 4000000000 | bytes 1000000 | tf_op jit(solution)/shard_map/own_lines_0/pallas_call | solution.py:357
  176.1 8.3 %collective-permute-done.6.refs_2_ = f32[15,256,128]{2,1,0:T(8,128)S(1)} collective-permute-done((f32[15,256,128]{2,1,0:T(8,128)S(1)}, f32[15,256,128]{2,1,0:T(8,128)S(1)}, u32[]{:S(2)}, u32[]{:S(2)}) %collective-permute-start.6) | collective-permute-done | bytes 1966112 | tf_op jit(solution)/shard_map/ppermute | solution.py:487
  184.5 4.9 %collective-permute-done.7.refs_3_ = f32[15,256,128]{2,1,0:T(8,128)S(1)} collective-permute-done((f32[15,256,128]{2,1,0:T(8,128)S(1)}, f32[15,256,128]{2,1,0:T(8,128)S(1)}, u32[]{:S(2)}, u32[]{:S(2)}) %collective-permute-start.7) | collective-permute-done | bytes 1966112 | tf_op jit(solution)/shard_map/ppermute | solution.py:487
  189.3 0.9 last_step.15
  190.3 8.1 %collective-permute-start.15 = (f32[32,32,128]{2,1,0:T(8,128)S(1)}, f32[32,32,128]{2,1,0:T(8,128)S(1)}, u32[]{:S(2)}, u32[]{:S(2)}) collective-permute-start(f32[32,32,128]{2,1,0:T(8,128)S(1)} %last_step.15), channel_id=1, source_target_pairs={{0,4},{8,0},{2,6},{10,2},{4,9},{12,13},{6,11},{14,15},{22,18},{30,... | collective-permute-start | bytes 1572872 | tf_op jit(solution)/shard_map/ppermute | solution.py:515
  198.4 0.9 last_step.14
  199.4 1.9 collective-permute-start.14
  201.3 0.9 last_step.13
  202.3 0.9 last_step.12
  203.7 0.9 last_step.11
  204.7 4.3 %collective-permute-start.11 = (f32[32,32,128]{2,1,0:T(8,128)S(1)}, f32[32,32,128]{2,1,0:T(8,128)S(1)}, u32[]{:S(2)}, u32[]{:S(2)}) collective-permute-start(f32[32,32,128]{2,1,0:T(8,128)S(1)} %last_step.11), channel_id=1, source_target_pairs={{0,5},{8,1},{2,7},{10,3},{4,8},{12,12},{6,10},{14,14},{22,19},{30,... | collective-permute-start | bytes 1572872 | tf_op jit(solution)/shard_map/ppermute | solution.py:515
  209.0 0.9 last_step.10
  209.9 0.9 last_step.9
  210.9 0.9 last_step.8
  211.9 26.6 %collective-permute-done.14.refs_2_ = f32[32,32,128]{2,1,0:T(8,128)S(1)} collective-permute-done((f32[32,32,128]{2,1,0:T(8,128)S(1)}, f32[32,32,128]{2,1,0:T(8,128)S(1)}, u32[]{:S(2)}, u32[]{:S(2)}) %collective-permute-start.14) | collective-permute-done | bytes 524320 | tf_op jit(solution)/shard_map/ppermute | solution.py:515
  238.5 4.3 %leave_0.1.refs_4_ = f32[8192,128]{1,0:T(8,128)} custom-call(s32[20]{0:T(128)S(1)} %dynamic-slice_bitcast_fusion.meta, f32[32,32,128]{2,1,0:T(8,128)S(1)} %collective-permute-done.12.refs_0_, f32[32,32,128]{2,1,0:T(8,128)S(1)} %collective-permute-done.13.refs_1_, f32[32,32,128]{2,1,0:T(8,128)S(1)} %collective-permute-done.14.refs_2_, ...), custom_call_target="tpu_custom_call" | custom-call | tf_op jit(solution)/shard_map/leave_0/pallas_call | solution.py:462
  242.9 12.0 %collective-permute-done.9.refs_1_ = f32[32,32,128]{2,1,0:T(8,128)S(1)} collective-permute-done((f32[32,32,128]{2,1,0:T(8,128)S(1)}, f32[32,32,128]{2,1,0:T(8,128)S(1)}, u32[]{:S(2)}, u32[]{:S(2)}) %collective-permute-start.9) | collective-permute-done | bytes 524320 | tf_op jit(solution)/shard_map/ppermute | solution.py:515
  254.9 4.3 %leave_1.1 = f32[8192,128]{1,0:T(8,128)} custom-call(s32[20]{0:T(128)S(1)} %dynamic-slice_bitcast_fusion.meta, f32[32,32,128]{2,1,0:T(8,128)S(1)} %collective-permute-done.8.refs_0_, f32[32,32,128]{2,1,0:T(8,128)S(1)} %collective-permute-done.9.refs_1_, f32[32,32,128]{2,1,0:T(8,128)S(1)} %collective-permute-done.10.refs_2_, ...), custom_call_target="tpu_custom_call", output_to_operand_aliasing={{}: (5, {})} | custom-call | tf_op jit(solution)/shard_map/leave_1/pallas_call | solution.py:462
  (23 shorter events, 2.0 us)
Async XLA Ops:
  12.4 10.2 %copy-start.2 = (f32[3,2,31]{2,1,0:T(2,128)S(1)}, f32[3,2,31]{2,1,0:T(2,128)}, u32[]{:S(2)}) copy-start(f32[3,2,31]{2,1,0:T(2,128)} %param.6) | copy-start | bytes 2236
  12.4 55.9 %all-to-all-start = ((f32[128,64,128]{2,1,0:T(8,128)}), f32[128,64,128]{2,1,0:T(8,128)}, u32[]{:S(2)}, u32[]{:S(2)}) async-start(f32[128,64,128]{2,1,0:T(8,128)} %bitcast.6), calls=%async_computation | async-start | bytes 8388608 | tf_op jit(solution)/shard_map/all_to_all | solution.py:482
  74.0 23.8 %collective-permute-start.1 = (f32[15,256,128]{2,1,0:T(8,128)}, f32[15,256,128]{2,1,0:T(8,128)}, u32[]{:S(2)}, u32[]{:S(2)}) collective-permute-start(f32[15,256,128]{2,1,0:T(8,128)} %get-tuple-element.31.low), channel_id=1, source_target_pairs={{8,0},{2,8},{10,2},{4,10},{12,4},{6,12},{14,6},{22,14},{30,22},{20... | collective-permute-start | bytes 5898248 | tf_op jit(solution)/shard_map/ppermute | solution.py:487
  81.0 1.3 copy-start
  82.3 24.4 %collective-permute-start = (f32[15,256,128]{2,1,0:T(8,128)}, f32[15,256,128]{2,1,0:T(8,128)}, u32[]{:S(2)}, u32[]{:S(2)}) collective-permute-start(f32[15,256,128]{2,1,0:T(8,128)} %get-tuple-element.34.high), channel_id=1, source_target_pairs={{0,8},{8,2},{2,10},{10,4},{4,12},{12,6},{6,14},{14,22},{22,30},{30... | collective-permute-start | bytes 5898248 | tf_op jit(solution)/shard_map/ppermute | solution.py:487
  89.1 8.7 %copy-start.1 = (f32[16,256,128]{2,1,0:T(8,128)S(1)}, f32[16,256,128]{2,1,0:T(8,128)}, u32[]{:S(2)}) copy-start(f32[16,256,128]{2,1,0:T(8,128)} %copy-done) | copy-start | bytes 6291460
  103.4 24.6 %collective-permute-start.2 = (f32[15,256,128]{2,1,0:T(8,128)S(1)}, f32[15,256,128]{2,1,0:T(8,128)S(1)}, u32[]{:S(2)}, u32[]{:S(2)}) collective-permute-start(f32[15,256,128]{2,1,0:T(8,128)S(1)} %get-tuple-element.42.high), channel_id=1, source_target_pairs={{0,8},{8,2},{2,10},{10,4},{4,12},{12,6},{6,14},{14,22},{22,30},{30... | collective-permute-start | bytes 5898248 | tf_op jit(solution)/shard_map/ppermute | solution.py:487
  112.1 22.2 %collective-permute-start.3 = (f32[15,256,128]{2,1,0:T(8,128)S(1)}, f32[15,256,128]{2,1,0:T(8,128)S(1)}, u32[]{:S(2)}, u32[]{:S(2)}) collective-permute-start(f32[15,256,128]{2,1,0:T(8,128)S(1)} %get-tuple-element.38.low), channel_id=1, source_target_pairs={{8,0},{2,8},{10,2},{4,10},{12,4},{6,12},{14,6},{22,14},{30,22},{20... | collective-permute-start | bytes 5898248 | tf_op jit(solution)/shard_map/ppermute | solution.py:487
  132.0 23.3 %collective-permute-start.5 = (f32[15,256,128]{2,1,0:T(8,128)S(1)}, f32[15,256,128]{2,1,0:T(8,128)S(1)}, u32[]{:S(2)}, u32[]{:S(2)}) collective-permute-start(f32[15,256,128]{2,1,0:T(8,128)S(1)} %get-tuple-element.43.low), channel_id=1, source_target_pairs={{8,0},{2,8},{10,2},{4,10},{12,4},{6,12},{14,6},{22,14},{30,22},{20... | collective-permute-start | bytes 5898248 | tf_op jit(solution)/shard_map/ppermute | solution.py:487
  138.5 24.3 %collective-permute-start.4 = (f32[15,256,128]{2,1,0:T(8,128)S(1)}, f32[15,256,128]{2,1,0:T(8,128)S(1)}, u32[]{:S(2)}, u32[]{:S(2)}) collective-permute-start(f32[15,256,128]{2,1,0:T(8,128)S(1)} %get-tuple-element.46.high), channel_id=1, source_target_pairs={{0,8},{8,2},{2,10},{10,4},{4,12},{12,6},{6,14},{14,22},{22,30},{30... | collective-permute-start | bytes 5898248 | tf_op jit(solution)/shard_map/ppermute | solution.py:487
  159.9 24.6 %collective-permute-start.6 = (f32[15,256,128]{2,1,0:T(8,128)S(1)}, f32[15,256,128]{2,1,0:T(8,128)S(1)}, u32[]{:S(2)}, u32[]{:S(2)}) collective-permute-start(f32[15,256,128]{2,1,0:T(8,128)S(1)} %get-tuple-element.50.high), channel_id=1, source_target_pairs={{0,8},{8,2},{2,10},{10,4},{4,12},{12,6},{6,14},{14,22},{22,30},{30... | collective-permute-start | bytes 5898248 | tf_op jit(solution)/shard_map/ppermute | solution.py:487
  167.1 22.2 %collective-permute-start.7 = (f32[15,256,128]{2,1,0:T(8,128)S(1)}, f32[15,256,128]{2,1,0:T(8,128)S(1)}, u32[]{:S(2)}, u32[]{:S(2)}) collective-permute-start(f32[15,256,128]{2,1,0:T(8,128)S(1)} %get-tuple-element.47.low), channel_id=1, source_target_pairs={{8,0},{2,8},{10,2},{4,10},{12,4},{6,12},{14,6},{22,14},{30,22},{20... | collective-permute-start | bytes 5898248 | tf_op jit(solution)/shard_map/ppermute | solution.py:487
  190.3 21.6 %collective-permute-start.15 = (f32[32,32,128]{2,1,0:T(8,128)S(1)}, f32[32,32,128]{2,1,0:T(8,128)S(1)}, u32[]{:S(2)}, u32[]{:S(2)}) collective-permute-start(f32[32,32,128]{2,1,0:T(8,128)S(1)} %last_step.15), channel_id=1, source_target_pairs={{0,4},{8,0},{2,6},{10,2},{4,9},{12,13},{6,11},{14,15},{22,18},{30,... | collective-permute-start | bytes 1572872 | tf_op jit(solution)/shard_map/ppermute | solution.py:515
  199.4 39.2 %collective-permute-start.14 = (f32[32,32,128]{2,1,0:T(8,128)S(1)}, f32[32,32,128]{2,1,0:T(8,128)S(1)}, u32[]{:S(2)}, u32[]{:S(2)}) collective-permute-start(f32[32,32,128]{2,1,0:T(8,128)S(1)} %last_step.14), channel_id=1, source_target_pairs={{0,0},{8,4},{2,2},{10,6},{4,13},{12,9},{6,15},{14,11},{22,22},{30,... | collective-permute-start | bytes 1572872 | tf_op jit(solution)/shard_map/ppermute | solution.py:515
  202.2 36.3 %collective-permute-start.13 = (f32[32,32,128]{2,1,0:T(8,128)S(1)}, f32[32,32,128]{2,1,0:T(8,128)S(1)}, u32[]{:S(2)}, u32[]{:S(2)}) collective-permute-start(f32[32,32,128]{2,1,0:T(8,128)S(1)} %last_step.13), channel_id=1, source_target_pairs={{0,6},{8,2},{2,0},{10,4},{4,11},{12,15},{6,13},{14,9},{22,20},{30,... | collective-permute-start | bytes 1572872 | tf_op jit(solution)/shard_map/ppermute | solution.py:515
  203.3 35.3 %collective-permute-start.12 = (f32[32,32,128]{2,1,0:T(8,128)S(1)}, f32[32,32,128]{2,1,0:T(8,128)S(1)}, u32[]{:S(2)}, u32[]{:S(2)}) collective-permute-start(f32[32,32,128]{2,1,0:T(8,128)S(1)} %last_step.12), channel_id=1, source_target_pairs={{0,2},{8,6},{2,4},{10,0},{4,15},{12,11},{6,9},{14,13},{22,16},{30,... | collective-permute-start | bytes 1572872 | tf_op jit(solution)/shard_map/ppermute | solution.py:515
  204.7 38.2 %collective-permute-start.11 = (f32[32,32,128]{2,1,0:T(8,128)S(1)}, f32[32,32,128]{2,1,0:T(8,128)S(1)}, u32[]{:S(2)}, u32[]{:S(2)}) collective-permute-start(f32[32,32,128]{2,1,0:T(8,128)S(1)} %last_step.11), channel_id=1, source_target_pairs={{0,5},{8,1},{2,7},{10,3},{4,8},{12,12},{6,10},{14,14},{22,19},{30,... | collective-permute-start | bytes 1572872 | tf_op jit(solution)/shard_map/ppermute | solution.py:515
  211.9 31.0 %collective-permute-start.10 = (f32[32,32,128]{2,1,0:T(8,128)S(1)}, f32[32,32,128]{2,1,0:T(8,128)S(1)}, u32[]{:S(2)}, u32[]{:S(2)}) collective-permute-start(f32[32,32,128]{2,1,0:T(8,128)S(1)} %last_step.10), channel_id=1, source_target_pairs={{0,1},{8,5},{2,3},{10,7},{4,12},{12,8},{6,14},{14,10},{22,23},{30,... | collective-permute-start | bytes 1572872 | tf_op jit(solution)/shard_map/ppermute | solution.py:515
  238.5 16.4 %collective-permute-start.9 = (f32[32,32,128]{2,1,0:T(8,128)S(1)}, f32[32,32,128]{2,1,0:T(8,128)S(1)}, u32[]{:S(2)}, u32[]{:S(2)}) collective-permute-start(f32[32,32,128]{2,1,0:T(8,128)S(1)} %last_step.9), channel_id=1, source_target_pairs={{0,7},{8,3},{2,1},{10,5},{4,10},{12,14},{6,12},{14,8},{22,21},{30,... | collective-permute-start | bytes 1572872 | tf_op jit(solution)/shard_map/ppermute | solution.py:515
  238.5 16.4 %collective-permute-start.8 = (f32[32,32,128]{2,1,0:T(8,128)S(1)}, f32[32,32,128]{2,1,0:T(8,128)S(1)}, u32[]{:S(2)}, u32[]{:S(2)}) collective-permute-start(f32[32,32,128]{2,1,0:T(8,128)S(1)} %last_step.8), channel_id=1, source_target_pairs={{0,3},{8,7},{2,5},{10,1},{4,14},{12,10},{6,8},{14,12},{22,17},{30,... | collective-permute-start | bytes 1572872 | tf_op jit(solution)/shard_map/ppermute | solution.py:515
